TPU v7x, 32 devices: a whole 2x2x4 slice. The times are simulated.
32 devices in a mesh: wide: 16 (over z, y, x), narrow: 2 (over core).
Axes of the slice: x: 2, y: 2, z: 4, core: 2. Of those that a mesh axis runs over, the one named last changes fastest.
Arguments:
- particle_position: float32 [3, 256, 128], P(None, ('wide', 'narrow')), may hold values from -6 to 6
- particle_velocity: float32 [3, 256, 128], P(None, ('wide', 'narrow')), may hold values from -6 to 6
- radius: float32 [256, 128], P(('wide', 'narrow')), may hold values from 0.4 to 1
- block_live_count: int32 [256], P(('wide', 'narrow')), may hold values from 64 to 128
- cell_index: int32 [256, 128], P(('wide', 'narrow')), may hold values from 0 to 8191
- block_offset: int32 [256], P(('wide', 'narrow')), may hold values from -2 to 2, as said below
- neighbours: int32 [256, 6], P(('wide', 'narrow')), may hold values from 0 to 7, as said below
- gas_velocity: float32 [3, 128, 16, 128], P(None, 'wide', 'narrow'), may hold values from -6 to 6
- pressure_source: float32 [128, 16, 128], P('wide', 'narrow'), may hold values from -6 to 6
- void_before: float32 [128, 16, 128], P('wide', 'narrow'), may hold values from 0.6 to 1
Outputs:
- pressure: float32 [128, 16, 128], P('wide', 'narrow')
- gas_next: float32 [3, 128, 16, 128], P(None, 'wide', 'narrow')
- updated_particle_velocity: float32 [3, 256, 128], P(None, ('wide', 'narrow'))
Inputs may be any that keep to these rules, and one draw needn't show every extreme that they name: For a block held at index w along wide, w + block_offset lies in 0 to 15. At most 3 blocks of one device share one offset, and on every device some offset has exactly 3. `neighbours`: each block lists 6 different blocks of its own device, never itself.
All inputs are finite; a program needn't handle non-finite values.
Results may differ from a plain program's by a relative error of at most 0.0003.
Values sent between devices are 32-bit elements; how exact they have to be, the bound alone decides.
No kernel may reach another device: no remote copies, remote signals or barrier semaphores. Data moves between devices by JAX's collectives and lax.ppermute only.
A program may use at most 128 MiB of HBM per device.

v0:
```python
import math

import jax
import jax.numpy as jnp
from jax import lax
from jax.sharding import PartitionSpec as P

SPREAD = 2
LEVELS = 4
SWEEPS = 2
COARSE_SWEEPS = 4
CAP = 3


relax_weight = 0.8
solid_most = 0.6
void_power = 2.65
drag_base = 0.5
drag_slope = 0.5
stiffness = 16.0
softening = 0.1
particle_density = 2.0
gas_density = 1.0
step_duration = 0.25
gravity = -1.0


def padded_2(cells, sides, width):
    for axis, dim in sides:
        count = lax.axis_size(axis)
        ends = count - 1
        head = lax.slice_in_dim(cells, 0, width, axis=dim)
        tail = lax.slice_in_dim(cells, cells.shape[dim] - width, cells.shape[dim], axis=dim)
        cells = jnp.concatenate(
            [
                lax.ppermute(tail, axis, [(i, (i + 1) % count) for i in range(ends)]),
                cells,
                lax.ppermute(head, axis, [((i + 1) % count, i) for i in range(ends)]),
            ],
            axis=dim,
        )
    return cells


def from_behind(block, axis, distance):
    devices = range(lax.axis_size(axis))
    route = [(i - distance, i) for i in devices if i - distance in devices]
    return lax.ppermute(block, axis, route)


def restrict(grid_field):
    depth_cells, lane_cells, width_cells = grid_field.shape
    return grid_field.reshape(depth_cells // 2, 2, lane_cells // 2, 2, width_cells // 2, 2).mean(
        axis=(1, 3, 5)
    )


def prolong(grid_field):
    return jnp.repeat(jnp.repeat(jnp.repeat(grid_field, 2, axis=0), 2, axis=1), 2, axis=2)


def coefs_from_padded(padded, weight):
    middle = padded[1:-1, 1:-1, 1:-1]
    couplings = (
        0.5 * weight * (middle + padded[:-2, 1:-1, 1:-1]),
        0.5 * weight * (middle + padded[2:, 1:-1, 1:-1]),
        0.5 * weight * (middle + padded[1:-1, :-2, 1:-1]),
        0.5 * weight * (middle + padded[1:-1, 2:, 1:-1]),
        0.5 * weight * (middle + padded[1:-1, 1:-1, :-2]),
        0.5 * weight * (middle + padded[1:-1, 1:-1, 2:]),
    )
    diagonal = (
        couplings[0] + couplings[1] + couplings[2] + couplings[3] + couplings[4] + couplings[5]
    )
    return (couplings, diagonal)


def apply_padded(padded, couplings, diagonal):
    middle = padded[1:-1, 1:-1, 1:-1]
    beside = couplings[0] * padded[:-2, 1:-1, 1:-1] + couplings[1] * padded[2:, 1:-1, 1:-1]
    beside = beside + couplings[2] * padded[1:-1, :-2, 1:-1] + couplings[3] * padded[1:-1, 2:, 1:-1]
    beside = beside + couplings[4] * padded[1:-1, 1:-1, :-2] + couplings[5] * padded[1:-1, 1:-1, 2:]
    return diagonal * middle - beside


def unchanged(grid_field):
    return grid_field


def pad_cells(grid_field):
    padded = padded_2(grid_field, (("wide", 0), ("narrow", 1)), 1)
    return jnp.pad(padded, ((0, 0), (0, 0), (1, 1)))


def pad_slab(grid_field):
    padded = padded_2(grid_field, (("wide", 0),), 1)
    return jnp.pad(padded, ((0, 0), (1, 1), (1, 1)))


def cycle(right_side, levels, level_index):
    couplings, diagonal, padder, enter_level, leave_level = levels[level_index]
    right_side = enter_level(right_side)
    coarsest = level_index == len(levels) - 1
    sweep_total = COARSE_SWEEPS if coarsest else SWEEPS
    iterate = relax_weight * right_side / diagonal
    for sweep_index in range(sweep_total - 1):
        iterate = (
            iterate
            + relax_weight
            * (right_side - apply_padded(padder(iterate), couplings, diagonal))
            / diagonal
        )
    if not coarsest:
        residual = right_side - apply_padded(padder(iterate), couplings, diagonal)
        iterate = iterate + prolong(cycle(restrict(residual), levels, level_index + 1))
        for sweep_index in range(SWEEPS):
            iterate = (
                iterate
                + relax_weight
                * (right_side - apply_padded(padder(iterate), couplings, diagonal))
                / diagonal
            )
    return leave_level(iterate)


def pressure_gradient(padded):
    return jnp.stack(
        [
            0.5 * (padded[2:, 1:-1, 1:-1] - padded[:-2, 1:-1, 1:-1]),
            0.5 * (padded[1:-1, 2:, 1:-1] - padded[1:-1, :-2, 1:-1]),
            0.5 * (padded[1:-1, 1:-1, 2:] - padded[1:-1, 1:-1, :-2]),
        ]
    )


def pairwise_force(local_positions, local_radii, local_live_mask, there_pos, there_rad, there_live):
    apart_z = local_positions[0][:, :, None] - there_pos[0][:, None, :]
    apart_y = local_positions[1][:, :, None] - there_pos[1][:, None, :]
    apart_x = local_positions[2][:, :, None] - there_pos[2][:, None, :]
    distance = jnp.sqrt(
        apart_z * apart_z + apart_y * apart_y + apart_x * apart_x + softening * softening
    )
    intersection = jnp.maximum(local_radii[:, :, None] + there_rad[:, None, :] - distance, 0.0)
    weight = intersection * there_live[:, None, :] / distance
    return local_live_mask[None] * jnp.stack(
        [
            jnp.sum(apart_z * weight, axis=2),
            jnp.sum(apart_y * weight, axis=2),
            jnp.sum(apart_x * weight, axis=2),
        ]
    )


def block_contact_forces(slot_positions, slot_radii, live_flags, adjacent_blocks):
    block_count = slot_radii.shape[0]
    batch_extent = math.gcd(block_count, 8)
    factor = stiffness / (slot_radii.shape[1] * (adjacent_blocks.shape[1] + 1))

    def one_batch(batch_index):
        total_force_sum = pairwise_force(
            slot_positions, slot_radii, live_flags, slot_positions, slot_radii, live_flags
        )
        for column in range(adjacent_blocks.shape[1]):
            selected_blocks = adjacent_blocks[:, column]
            total_force_sum = total_force_sum + pairwise_force(
                slot_positions,
                slot_radii,
                live_flags,
                slot_positions[:, selected_blocks],
                slot_radii[selected_blocks],
                live_flags[selected_blocks],
            )
        return total_force_sum * factor

    stacked = lax.map(one_batch, jnp.arange(block_count // batch_extent, dtype=jnp.int32))
    return stacked.transpose(1, 0, 2, 3).reshape(3, block_count, -1)


def local(
    particle_position,
    particle_velocity,
    radius,
    block_live_count,
    cell_index,
    block_offset,
    neighbours,
    gas_velocity,
    pressure_source,
    void_before,
):
    block_count = radius.shape[0]
    slot_count = radius.shape[1]
    depth_cells, lane_cells, width_cells = pressure_source.shape
    total_cells = depth_cells * lane_cells * width_cells
    slot_index_list = jnp.arange(slot_count, dtype=jnp.int32)
    live_flags = (slot_index_list[None, :] < block_live_count[:, None]).astype(jnp.float32)
    particle_volume = radius * radius * radius
    volume_live_mask = particle_volume * live_flags
    payload = jnp.concatenate(
        [volume_live_mask[None], particle_velocity, cell_index.astype(jnp.float32)[None]], axis=0
    )
    payload = payload.transpose(1, 0, 2).reshape(block_count, 5 * slot_count)
    block_ids = jnp.arange(block_count, dtype=jnp.int32)
    earlier = block_ids[:, None] > block_ids[None, :]
    alike = block_offset[:, None] == block_offset[None, :]
    rank_within = jnp.sum(jnp.logical_and(earlier, alike), axis=1)
    slot_key = (block_offset + SPREAD) * CAP + rank_within
    selector = (
        jnp.arange((2 * SPREAD + 1) * CAP, dtype=jnp.int32)[:, None] == slot_key[None, :]
    ).astype(jnp.float32)
    outgoing = jnp.dot(selector, payload, precision=lax.Precision.HIGHEST)
    arrived = []
    for group_index in range(2 * SPREAD + 1):
        step_by = group_index - SPREAD
        group_rows = outgoing[group_index * CAP : (group_index + 1) * CAP]
        if step_by == 0:
            arrived.append(group_rows)
        else:
            arrived.append(from_behind(group_rows, "wide", step_by))
    incoming = jnp.concatenate(arrived, axis=0)
    row_count = incoming.shape[0]
    rows_in = incoming.reshape(row_count, 5, slot_count)
    vol_in = rows_in[:, 0].reshape(-1)
    vel_in = rows_in[:, 1:4].transpose(1, 0, 2).reshape(3, -1)
    where_in = rows_in[:, 4].reshape(-1).astype(jnp.int32)
    solid_sum = jnp.zeros((total_cells,), jnp.float32).at[where_in].add(vol_in)
    voidage = 1.0 - solid_most * solid_sum / (1.0 + solid_sum)
    slip_vel = gas_velocity.reshape(3, -1)[:, where_in] - vel_in
    slip_speed = jnp.sqrt(jnp.sum(slip_vel * slip_vel, axis=0))
    drag_force = (
        vol_in * (drag_base + drag_slope * slip_speed) * voidage[where_in] ** (-void_power)
    )[None] * slip_vel
    reaction = jnp.zeros((3, total_cells), jnp.float32).at[:, where_in].add(-drag_force)
    voidage_grid = voidage.reshape(depth_cells, lane_cells, width_cells)
    right_side = pressure_source + (void_before - voidage_grid) / step_duration
    fine_levels = [voidage_grid]
    for level_index in range(1, LEVELS):
        fine_levels.append(restrict(fine_levels[-1]))
    levels = []
    far_void = lax.all_gather(fine_levels[2], "narrow", axis=1, tiled=True)
    far_levels = [far_void]
    level_index = 3
    far_levels.append(restrict(far_levels[-1]))
    far_lanes = fine_levels[2].shape[1]
    far_start = lax.axis_index("narrow") * far_lanes

    def enter_far(grid_field):
        return lax.all_gather(grid_field, "narrow", axis=1, tiled=True)

    def leave_far(grid_field):
        return lax.dynamic_slice_in_dim(grid_field, far_start, far_lanes, 1)

    for level_index in range(LEVELS):
        if level_index < 2:
            couplings, diagonal = coefs_from_padded(
                pad_cells(fine_levels[level_index]), 0.25**level_index
            )
            levels.append((couplings, diagonal, pad_cells, unchanged, unchanged))
        else:
            couplings, diagonal = coefs_from_padded(
                pad_slab(far_levels[level_index - 2]), 0.25**level_index
            )
            enter_level = enter_far if level_index == 2 else unchanged
            leave_level = leave_far if level_index == 2 else unchanged
            levels.append((couplings, diagonal, pad_slab, enter_level, leave_level))
    pressure = cycle(right_side, levels, 0)
    pressure_padded = padded_2(pressure, (("wide", 0), ("narrow", 1)), 1)
    gradient = pressure_gradient(jnp.pad(pressure_padded, ((0, 0), (0, 0), (1, 1))))
    gas_next = gas_velocity + step_duration * (
        reaction.reshape(3, depth_cells, lane_cells, width_cells)
        / (gas_density * voidage_grid)[None]
        - gradient / gas_density
    )
    fluid_force = drag_force - vol_in[None] * gradient.reshape(3, -1)[:, where_in]
    returning = (
        fluid_force.reshape(3, row_count, slot_count)
        .transpose(1, 0, 2)
        .reshape(row_count, 3 * slot_count)
    )
    back_list = []
    for group_index in range(2 * SPREAD + 1):
        step_by = group_index - SPREAD
        group_rows = returning[group_index * CAP : (group_index + 1) * CAP]
        if step_by == 0:
            back_list.append(group_rows)
        else:
            back_list.append(from_behind(group_rows, "wide", -step_by))
    returned = jnp.concatenate(back_list, axis=0)
    on_blocks = jnp.dot(selector.T, returned, precision=lax.Precision.HIGHEST)
    fluid_on = on_blocks.reshape(block_count, 3, slot_count).transpose(1, 0, 2)
    contact_force = block_contact_forces(particle_position, radius, live_flags, neighbours)
    downward = jnp.array([gravity, 0.0, 0.0], jnp.float32)[:, None, None]
    particle_acceleration = (contact_force + fluid_on) / (particle_density * particle_volume)[
        None
    ] + downward
    updated_particle_velocity = live_flags[None] * (
        particle_velocity + step_duration * particle_acceleration
    )
    return (pressure, gas_next, updated_particle_velocity)


def solution(mesh):
    placed = (
        P(None, ("wide", "narrow"), None),
        P(None, ("wide", "narrow"), None),
        P(("wide", "narrow"), None),
        P(("wide", "narrow")),
        P(("wide", "narrow"), None),
        P(("wide", "narrow")),
        P(("wide", "narrow"), None),
        P(None, "wide", "narrow", None),
        P("wide", "narrow", None),
        P("wide", "narrow", None),
    )
    return jax.shard_map(
        local,
        mesh=mesh,
        in_specs=placed,
        out_specs=(
            P("wide", "narrow", None),
            P(None, "wide", "narrow", None),
            P(None, ("wide", "narrow"), None),
        ),
        check_vma=False,
    )
```

profile of v0, /device:TPU:0, one launch (start us, length us, event | category | flops | bytes accessed | tf_op | source)
XLA Modules:
  0.0 342.1 jit_solution(17968563249861148832)
XLA Ops:
  7.1 5.5 %collective-permute-start.2 = (f32[3,640]{1,0:T(4,128)S(1)}, f32[3,640]{1,0:T(4,128)S(1)}, u32[]{:S(2)}, u32[]{:S(2)}) collective-permute-start(f32[3,640]{1,0:T(4,128)S(1)} %get-tuple-element.102), channel_id=1, source_target_pairs={{0,2},{2,4},{4,6},{6,8},{8,10},{10,12},{12,14},{14,16},{16,18},{18... | collective-permute-start | bytes 23048 | tf_op jit(solution)/shard_map/ppermute | solution.py:48
  12.6 4.6 %collective-permute-start.3 = (f32[3,640]{1,0:T(4,128)S(1)}, f32[3,640]{1,0:T(4,128)S(1)}, u32[]{:S(2)}, u32[]{:S(2)}) collective-permute-start(f32[3,640]{1,0:T(4,128)S(1)} %get-tuple-element.101), channel_id=1, source_target_pairs={{0,4},{2,6},{4,8},{6,10},{8,12},{10,14},{12,16},{14,18},{16,20},{1... | collective-permute-start | bytes 23048 | tf_op jit(solution)/shard_map/ppermute | solution.py:48
  22.0 13.7 %scatter_custom_fusion = f32[8192]{0:T(1024)S(1)} fusion(s32[1920]{0:T(1024)S(1)} %fusion.215, f32[1920]{0:T(1024)S(1)} %bitcast.250, f32[]{:T(128)} %constant.24.clone.1), kind=kCustom, calls=%fused_computation.333 | custom fusion | flops 1920 | bytes 32772 | tf_op jit(solution)/shard_map/scatter-add | solution.py:226
  35.7 4.8 %collective-permute-start.4 = (f32[1,8,128]{2,1,0:T(8,128)S(1)}, f32[1,8,128]{2,1,0:T(8,128)S(1)}, u32[]{:S(2)}, u32[]{:S(2)}) collective-permute-start(f32[1,8,128]{2,1,0:T(8,128)S(1)} %get-tuple-element.117), channel_id=1, source_target_pairs={{0,2},{2,4},{4,6},{6,8},{8,10},{10,12},{12,14},{14,16},{16,18},{18... | collective-permute-start | bytes 12296 | tf_op jit(solution)/shard_map/ppermute | solution.py:36
  43.1 2.9 collective-permute-done.5
  51.3 3.2 collective-permute-start.8
  55.8 4.2 %collective-permute-done.9 = f32[1,8,128]{2,1,0:T(8,128)S(1)} collective-permute-done((f32[1,8,128]{2,1,0:T(8,128)S(1)}, f32[1,8,128]{2,1,0:T(8,128)S(1)}, u32[]{:S(2)}, u32[]{:S(2)}) %collective-permute-start.9) | collective-permute-done | bytes 4128 | tf_op jit(solution)/shard_map/ppermute | solution.py:38
  62.9 3.9 %collective-permute-start.16 = (f32[1,4,64]{2,1,0:T(4,128)S(1)}, f32[1,4,64]{2,1,0:T(4,128)S(1)}, u32[]{:S(2)}, u32[]{:S(2)}) collective-permute-start(f32[1,4,64]{2,1,0:T(4,128)S(1)} %get-tuple-element.167), channel_id=1, source_target_pairs={{0,2},{2,4},{4,6},{6,8},{8,10},{10,12},{12,14},{14,16},{16,18},{18... | collective-permute-start | bytes 3080 | tf_op jit(solution)/shard_map/ppermute | solution.py:36
  68.5 4.5 %collective-permute-start.12 = (f32[1,8,128]{2,1,0:T(8,128)S(1)}, f32[1,8,128]{2,1,0:T(8,128)S(1)}, u32[]{:S(2)}, u32[]{:S(2)}) collective-permute-start(f32[1,8,128]{2,1,0:T(8,128)S(1)} %get-tuple-element.112), channel_id=1, source_target_pairs={{0,2},{2,4},{4,6},{6,8},{8,10},{10,12},{12,14},{14,16},{16,18},{18... | collective-permute-start | bytes 12296 | tf_op jit(solution)/shard_map/ppermute | solution.py:36
  86.7 5.5 %collective-permute-start.20 = (f32[1,4,64]{2,1,0:T(4,128)S(1)}, f32[1,4,64]{2,1,0:T(4,128)S(1)}, u32[]{:S(2)}, u32[]{:S(2)}) collective-permute-start(f32[1,4,64]{2,1,0:T(4,128)S(1)} %get-tuple-element.164), channel_id=1, source_target_pairs={{0,2},{2,4},{4,6},{6,8},{8,10},{10,12},{12,14},{14,16},{16,18},{18... | collective-permute-start | bytes 3080 | tf_op jit(solution)/shard_map/ppermute | solution.py:36
  103.7 4.8 %collective-permute-start.24 = (f32[1,4,64]{2,1,0:T(4,128)S(1)}, f32[1,4,64]{2,1,0:T(4,128)S(1)}, u32[]{:S(2)}, u32[]{:S(2)}) collective-permute-start(f32[1,4,64]{2,1,0:T(4,128)S(1)} %get-tuple-element.162), channel_id=1, source_target_pairs={{0,2},{2,4},{4,6},{6,8},{8,10},{10,12},{12,14},{14,16},{16,18},{18... | collective-permute-start | bytes 3080 | tf_op jit(solution)/shard_map/ppermute | solution.py:36
  109.8 5.1 %collective-permute-start.28 = (f32[1,4,32]{2,0,1:T(1,128)S(1)}, f32[1,4,32]{2,0,1:T(1,128)S(1)}, u32[]{:S(2)}, u32[]{:S(2)}) collective-permute-start(f32[1,4,32]{2,0,1:T(1,128)S(1)} %get-tuple-element.179), channel_id=1, source_target_pairs={{0,2},{2,4},{4,6},{6,8},{8,10},{10,12},{12,14},{14,16},{16,18},{18... | collective-permute-start | bytes 1544 | tf_op jit(solution)/shard_map/ppermute | solution.py:36
  124.2 5.0 %collective-permute-start.30 = (f32[1,4,32]{2,0,1:T(1,128)S(1)}, f32[1,4,32]{2,0,1:T(1,128)S(1)}, u32[]{:S(2)}, u32[]{:S(2)}) collective-permute-start(f32[1,4,32]{2,0,1:T(1,128)S(1)} %get-tuple-element.177), channel_id=1, source_target_pairs={{0,2},{2,4},{4,6},{6,8},{8,10},{10,12},{12,14},{14,16},{16,18},{18... | collective-permute-start | bytes 1544 | tf_op jit(solution)/shard_map/ppermute | solution.py:36
  130.5 5.8 %collective-permute-start.34 = (f32[1,2,16]{2,1,0:T(2,128)S(1)}, f32[1,2,16]{2,1,0:T(2,128)S(1)}, u32[]{:S(2)}, u32[]{:S(2)}) collective-permute-start(f32[1,2,16]{2,1,0:T(2,128)S(1)} %multiply_bitcast_fusion), channel_id=1, source_target_pairs={{0,2},{2,4},{4,6},{6,8},{8,10},{10,12},{12,14},{14,16},{16,18},{18... | collective-permute-start | bytes 392 | tf_op jit(solution)/shard_map/ppermute | solution.py:36
  137.8 6.3 %collective-permute-start.32 = (f32[1,4,32]{2,0,1:T(1,128)S(1)}, f32[1,4,32]{2,0,1:T(1,128)S(1)}, u32[]{:S(2)}, u32[]{:S(2)}) collective-permute-start(f32[1,4,32]{2,0,1:T(1,128)S(1)} %get-tuple-element.175), channel_id=1, source_target_pairs={{0,2},{2,4},{4,6},{6,8},{8,10},{10,12},{12,14},{14,16},{16,18},{18... | collective-permute-start | bytes 1544 | tf_op jit(solution)/shard_map/ppermute | solution.py:36
  145.6 5.0 %collective-permute-done.33 = f32[1,4,32]{2,0,1:T(1,128)S(1)} collective-permute-done((f32[1,4,32]{2,0,1:T(1,128)S(1)}, f32[1,4,32]{2,0,1:T(1,128)S(1)}, u32[]{:S(2)}, u32[]{:S(2)}) %collective-permute-start.33) | collective-permute-done | bytes 544 | tf_op jit(solution)/shard_map/ppermute | solution.py:38
  151.0 5.5 %collective-permute-start.36 = (f32[1,2,16]{2,1,0:T(2,128)S(1)}, f32[1,2,16]{2,1,0:T(2,128)S(1)}, u32[]{:S(2)}, u32[]{:S(2)}) collective-permute-start(f32[1,2,16]{2,1,0:T(2,128)S(1)} %get-tuple-element.63), channel_id=1, source_target_pairs={{0,2},{2,4},{4,6},{6,8},{8,10},{10,12},{12,14},{14,16},{16,18},{18... | collective-permute-start | bytes 392 | tf_op jit(solution)/shard_map/ppermute | solution.py:36
  157.9 3.0 fusion.36
  160.9 2.9 collective-permute-done.37
  164.0 5.7 %collective-permute-start.38 = (f32[1,2,16]{2,1,0:T(2,128)S(1)}, f32[1,2,16]{2,1,0:T(2,128)S(1)}, u32[]{:S(2)}, u32[]{:S(2)}) collective-permute-start(f32[1,2,16]{2,1,0:T(2,128)S(1)} %divide_add_fusion.3), channel_id=1, source_target_pairs={{0,2},{2,4},{4,6},{6,8},{8,10},{10,12},{12,14},{14,16},{16,18},{18... | collective-permute-start | bytes 392 | tf_op jit(solution)/shard_map/ppermute | solution.py:36
  171.6 3.6 %collective-permute-done.39 = f32[1,2,16]{2,1,0:T(2,128)S(1)} collective-permute-done((f32[1,2,16]{2,1,0:T(2,128)S(1)}, f32[1,2,16]{2,1,0:T(2,128)S(1)}, u32[]{:S(2)}, u32[]{:S(2)}) %collective-permute-start.39) | collective-permute-done | bytes 160 | tf_op jit(solution)/shard_map/ppermute | solution.py:38
  175.4 4.8 %collective-permute-start.40 = (f32[1,2,16]{2,1,0:T(2,128)S(1)}, f32[1,2,16]{2,1,0:T(2,128)S(1)}, u32[]{:S(2)}, u32[]{:S(2)}) collective-permute-start(f32[1,2,16]{2,1,0:T(2,128)S(1)} %divide_add_fusion.2), channel_id=1, source_target_pairs={{0,2},{2,4},{4,6},{6,8},{8,10},{10,12},{12,14},{14,16},{16,18},{18... | collective-permute-start | bytes 392 | tf_op jit(solution)/shard_map/ppermute | solution.py:36
  181.5 4.1 %collective-permute-done.41 = f32[1,2,16]{2,1,0:T(2,128)S(1)} collective-permute-done((f32[1,2,16]{2,1,0:T(2,128)S(1)}, f32[1,2,16]{2,1,0:T(2,128)S(1)}, u32[]{:S(2)}, u32[]{:S(2)}) %collective-permute-start.41) | collective-permute-done | bytes 160 | tf_op jit(solution)/shard_map/ppermute | solution.py:38
  186.0 4.1 %collective-permute-start.42 = (f32[1,4,32]{2,0,1:T(1,128)S(1)}, f32[1,4,32]{2,0,1:T(1,128)S(1)}, u32[]{:S(2)}, u32[]{:S(2)}) collective-permute-start(f32[1,4,32]{2,0,1:T(1,128)S(1)} %get-tuple-element.172), channel_id=1, source_target_pairs={{0,2},{2,4},{4,6},{6,8},{8,10},{10,12},{12,14},{14,16},{16,18},{18... | collective-permute-start | bytes 1544 | tf_op jit(solution)/shard_map/ppermute | solution.py:36
  191.5 4.2 %collective-permute-done.43 = f32[1,4,32]{2,0,1:T(1,128)S(1)} collective-permute-done((f32[1,4,32]{2,0,1:T(1,128)S(1)}, f32[1,4,32]{2,0,1:T(1,128)S(1)}, u32[]{:S(2)}, u32[]{:S(2)}) %collective-permute-start.43) | collective-permute-done | bytes 544 | tf_op jit(solution)/shard_map/ppermute | solution.py:38
  195.8 4.8 %collective-permute-start.44 = (f32[1,4,32]{2,0,1:T(1,128)S(1)}, f32[1,4,32]{2,0,1:T(1,128)S(1)}, u32[]{:S(2)}, u32[]{:S(2)}) collective-permute-start(f32[1,4,32]{2,0,1:T(1,128)S(1)} %get-tuple-element.170), channel_id=1, source_target_pairs={{0,2},{2,4},{4,6},{6,8},{8,10},{10,12},{12,14},{14,16},{16,18},{18... | collective-permute-start | bytes 1544 | tf_op jit(solution)/shard_map/ppermute | solution.py:36
  202.5 3.6 %collective-permute-done.45 = f32[1,4,32]{2,0,1:T(1,128)S(1)} collective-permute-done((f32[1,4,32]{2,0,1:T(1,128)S(1)}, f32[1,4,32]{2,0,1:T(1,128)S(1)}, u32[]{:S(2)}, u32[]{:S(2)}) %collective-permute-start.45) | collective-permute-done | bytes 544 | tf_op jit(solution)/shard_map/ppermute | solution.py:38
  206.6 3.9 %collective-permute-start.46 = (f32[1,4,64]{2,1,0:T(4,128)S(1)}, f32[1,4,64]{2,1,0:T(4,128)S(1)}, u32[]{:S(2)}, u32[]{:S(2)}) collective-permute-start(f32[1,4,64]{2,1,0:T(4,128)S(1)} %get-tuple-element.160), channel_id=1, source_target_pairs={{0,2},{2,4},{4,6},{6,8},{8,10},{10,12},{12,14},{14,16},{16,18},{18... | collective-permute-start | bytes 3080 | tf_op jit(solution)/shard_map/ppermute | solution.py:36
  212.4 3.6 %collective-permute-done.47 = f32[1,4,64]{2,1,0:T(4,128)S(1)} collective-permute-done((f32[1,4,64]{2,1,0:T(4,128)S(1)}, f32[1,4,64]{2,1,0:T(4,128)S(1)}, u32[]{:S(2)}, u32[]{:S(2)}) %collective-permute-start.47) | collective-permute-done | bytes 1056 | tf_op jit(solution)/shard_map/ppermute | solution.py:38
  222.2 3.7 %collective-permute-start.50 = (f32[1,4,64]{2,1,0:T(4,128)S(1)}, f32[1,4,64]{2,1,0:T(4,128)S(1)}, u32[]{:S(2)}, u32[]{:S(2)}) collective-permute-start(f32[1,4,64]{2,1,0:T(4,128)S(1)} %get-tuple-element.158), channel_id=1, source_target_pairs={{0,2},{2,4},{4,6},{6,8},{8,10},{10,12},{12,14},{14,16},{16,18},{18... | collective-permute-start | bytes 3080 | tf_op jit(solution)/shard_map/ppermute | solution.py:36
  227.2 3.0 fusion.57
  235.6 2.6 copy.158
  238.9 4.3 %collective-permute-start.54 = (f32[1,8,128]{2,1,0:T(8,128)S(1)}, f32[1,8,128]{2,1,0:T(8,128)S(1)}, u32[]{:S(2)}, u32[]{:S(2)}) collective-permute-start(f32[1,8,128]{2,1,0:T(8,128)S(1)} %get-tuple-element.110), channel_id=1, source_target_pairs={{0,2},{2,4},{4,6},{6,8},{8,10},{10,12},{12,14},{14,16},{16,18},{18... | collective-permute-start | bytes 12296 | tf_op jit(solution)/shard_map/ppermute | solution.py:36
  244.5 4.4 %collective-permute-done.55 = f32[1,8,128]{2,1,0:T(8,128)S(1)} collective-permute-done((f32[1,8,128]{2,1,0:T(8,128)S(1)}, f32[1,8,128]{2,1,0:T(8,128)S(1)}, u32[]{:S(2)}, u32[]{:S(2)}) %collective-permute-start.55) | collective-permute-done | bytes 4128 | tf_op jit(solution)/shard_map/ppermute | solution.py:38
  252.2 5.7 %gather_fusion = f32[1920,3]{1,0:T(8,128)S(1)} fusion(f32[3,8192]{0,1:T(8,128)} %bitcast.229, s32[2048]{0:T(1024)S(1)} %pad_clamp_fusion), kind=kCustom, calls=%fused_computation | custom fusion | bytes 53760 | tf_op jit(solution)/shard_map/gather | solution.py:228
  258.5 4.4 %collective-permute-start.58 = (f32[1,8,128]{2,1,0:T(8,128)S(1)}, f32[1,8,128]{2,1,0:T(8,128)S(1)}, u32[]{:S(2)}, u32[]{:S(2)}) collective-permute-start(f32[1,8,128]{2,1,0:T(8,128)S(1)} %get-tuple-element.108), channel_id=1, source_target_pairs={{0,2},{2,4},{4,6},{6,8},{8,10},{10,12},{12,14},{14,16},{16,18},{18... | collective-permute-start | bytes 12296 | tf_op jit(solution)/shard_map/ppermute | solution.py:36
  264.2 10.4 %gather_fusion.1 = f32[1920]{0:T(1024)S(1)} fusion(f32[8192]{0:T(1024)S(1)} %get-tuple-element.118, s32[2048]{0:T(1024)S(1)} %pad_clamp_fusion), kind=kCustom, calls=%fused_computation.1 | custom fusion | bytes 23040 | tf_op jit(solution)/shard_map/gather | solution.py:231
  274.7 2.7 collective-permute-start.60
  282.1 4.9 %collective-permute-start.63 = (f32[1,8,128]{2,1,0:T(8,128)S(1)}, f32[1,8,128]{2,1,0:T(8,128)S(1)}, u32[]{:S(2)}, u32[]{:S(2)}) collective-permute-start(f32[1,8,128]{2,1,0:T(8,128)S(1)} %get-tuple-element.106), channel_id=1, source_target_pairs={{0,2},{2,4},{4,6},{6,8},{8,10},{10,12},{12,14},{14,16},{16,18},{18... | collective-permute-start | bytes 12296 | tf_op jit(solution)/shard_map/ppermute | solution.py:36
  289.6 3.0 collective-permute-start.65
  292.7 15.5 %scatter_custom_fusion.1 = f32[3,8192]{0,1:T(8,128)} fusion(s32[1920]{0:T(1024)S(1)} %fusion.215, f32[]{:T(128)} %constant.24.clone.1, f32[3,1920]{0,1:T(8,128)S(1)} %fusion.10), kind=kCustom, calls=%fused_computation.23 | custom fusion | flops 5760 | bytes 1081348 | tf_op jit(solution)/shard_map/scatter-add | solution.py:233
  308.2 2.8 copy.161
  311.6 2.6 copy.162
  314.2 5.7 %gather_fusion.20 = f32[1920,3]{1,0:T(8,128)S(1)} fusion(f32[3,8192]{0,1:T(8,128)} %copy.162, s32[2048]{0:T(1024)S(1)} %pad_clamp_fusion), kind=kCustom, calls=%fused_computation.20 | custom fusion | bytes 53760 | tf_op jit(solution)/shard_map/gather | solution.py:274
  320.3 5.3 %collective-permute-start.66 = (f32[3,384]{1,0:T(4,128)S(1)}, f32[3,384]{1,0:T(4,128)S(1)}, u32[]{:S(2)}, u32[]{:S(2)}) collective-permute-start(f32[3,384]{1,0:T(4,128)S(1)} %bitcast.254), channel_id=1, source_target_pairs={{0,4},{2,6},{4,8},{6,10},{8,12},{10,14},{12,16},{14,18},{16,20},{1... | collective-permute-start | bytes 13832 | tf_op jit(solution)/shard_map/ppermute | solution.py:48
  325.5 3.8 %collective-permute-start.67 = (f32[3,384]{1,0:T(4,128)S(1)}, f32[3,384]{1,0:T(4,128)S(1)}, u32[]{:S(2)}, u32[]{:S(2)}) collective-permute-start(f32[3,384]{1,0:T(4,128)S(1)} %bitcast.255), channel_id=1, source_target_pairs={{0,2},{2,4},{4,6},{6,8},{8,10},{10,12},{12,14},{14,16},{16,18},{18... | collective-permute-start | bytes 13832 | tf_op jit(solution)/shard_map/ppermute | solution.py:48
  332.6 5.1 %collective-permute-done.68 = f32[3,384]{1,0:T(4,128)S(1)} collective-permute-done((f32[3,384]{1,0:T(4,128)S(1)}, f32[3,384]{1,0:T(4,128)S(1)}, u32[]{:S(2)}, u32[]{:S(2)}) %collective-permute-start.68) | collective-permute-done | bytes 4640 | tf_op jit(solution)/shard_map/ppermute | solution.py:48
  337.7 3.4 collective-permute-done.69
  (292 shorter events, 107.7 us)
Async XLA Ops:
  4.5 17.1 %collective-permute-start = (f32[3,640]{1,0:T(4,128)S(1)}, f32[3,640]{1,0:T(4,128)S(1)}, u32[]{:S(2)}, u32[]{:S(2)}) collective-permute-start(f32[3,640]{1,0:T(4,128)S(1)} %get-tuple-element.105), channel_id=1, source_target_pairs={{4,0},{6,2},{8,4},{10,6},{12,8},{14,10},{16,12},{18,14},{20,16},{2... | collective-permute-start | bytes 23048 | tf_op jit(solution)/shard_map/ppermute | solution.py:48
  5.8 15.9 %collective-permute-start.1 = (f32[3,640]{1,0:T(4,128)S(1)}, f32[3,640]{1,0:T(4,128)S(1)}, u32[]{:S(2)}, u32[]{:S(2)}) collective-permute-start(f32[3,640]{1,0:T(4,128)S(1)} %get-tuple-element.104), channel_id=1, source_target_pairs={{2,0},{4,2},{6,4},{8,6},{10,8},{12,10},{14,12},{16,14},{18,16},{20... | collective-permute-start | bytes 23048 | tf_op jit(solution)/shard_map/ppermute | solution.py:48
  7.1 14.6 %collective-permute-start.2 = (f32[3,640]{1,0:T(4,128)S(1)}, f32[3,640]{1,0:T(4,128)S(1)}, u32[]{:S(2)}, u32[]{:S(2)}) collective-permute-start(f32[3,640]{1,0:T(4,128)S(1)} %get-tuple-element.102), channel_id=1, source_target_pairs={{0,2},{2,4},{4,6},{6,8},{8,10},{10,12},{12,14},{14,16},{16,18},{18... | collective-permute-start | bytes 23048 | tf_op jit(solution)/shard_map/ppermute | solution.py:48
  12.6 9.1 %collective-permute-start.3 = (f32[3,640]{1,0:T(4,128)S(1)}, f32[3,640]{1,0:T(4,128)S(1)}, u32[]{:S(2)}, u32[]{:S(2)}) collective-permute-start(f32[3,640]{1,0:T(4,128)S(1)} %get-tuple-element.101), channel_id=1, source_target_pairs={{0,4},{2,6},{4,8},{6,10},{8,12},{10,14},{12,16},{14,18},{16,20},{1... | collective-permute-start | bytes 23048 | tf_op jit(solution)/shard_map/ppermute | solution.py:48
  35.7 7.4 %collective-permute-start.4 = (f32[1,8,128]{2,1,0:T(8,128)S(1)}, f32[1,8,128]{2,1,0:T(8,128)S(1)}, u32[]{:S(2)}, u32[]{:S(2)}) collective-permute-start(f32[1,8,128]{2,1,0:T(8,128)S(1)} %get-tuple-element.117), channel_id=1, source_target_pairs={{0,2},{2,4},{4,6},{6,8},{8,10},{10,12},{12,14},{14,16},{16,18},{18... | collective-permute-start | bytes 12296 | tf_op jit(solution)/shard_map/ppermute | solution.py:36
  60.0 8.1 %collective-permute-start.10 = (f32[10,1,128]{2,1,0:T(1,128)S(1)}, f32[10,1,128]{2,1,0:T(1,128)S(1)}, u32[]{:S(2)}, u32[]{:S(2)}) collective-permute-start(f32[10,1,128]{2,1,0:T(1,128)S(1)} %get-tuple-element.97), channel_id=1, source_target_pairs={{0,1},{2,3},{4,5},{6,7},{8,9},{10,11},{12,13},{14,15},{16,17},{18,... | collective-permute-start | bytes 15368 | tf_op jit(solution)/shard_map/ppermute | solution.py:36
  61.6 6.6 %collective-permute-start.11 = (f32[10,1,128]{2,1,0:T(1,128)S(1)}, f32[10,1,128]{2,1,0:T(1,128)S(1)}, u32[]{:S(2)}, u32[]{:S(2)}) collective-permute-start(f32[10,1,128]{2,1,0:T(1,128)S(1)} %get-tuple-element.98), channel_id=1, source_target_pairs={{1,0},{3,2},{5,4},{7,6},{9,8},{11,10},{13,12},{15,14},{17,16},{19,... | collective-permute-start | bytes 15368 | tf_op jit(solution)/shard_map/ppermute | solution.py:38
  62.9 11.4 %collective-permute-start.16 = (f32[1,4,64]{2,1,0:T(4,128)S(1)}, f32[1,4,64]{2,1,0:T(4,128)S(1)}, u32[]{:S(2)}, u32[]{:S(2)}) collective-permute-start(f32[1,4,64]{2,1,0:T(4,128)S(1)} %get-tuple-element.167), channel_id=1, source_target_pairs={{0,2},{2,4},{4,6},{6,8},{8,10},{10,12},{12,14},{14,16},{16,18},{18... | collective-permute-start | bytes 3080 | tf_op jit(solution)/shard_map/ppermute | solution.py:36
  66.9 7.5 %collective-permute-start.17 = (f32[1,4,64]{2,1,0:T(4,128)S(1)}, f32[1,4,64]{2,1,0:T(4,128)S(1)}, u32[]{:S(2)}, u32[]{:S(2)}) collective-permute-start(f32[1,4,64]{2,1,0:T(4,128)S(1)} %get-tuple-element.166), channel_id=1, source_target_pairs={{2,0},{4,2},{6,4},{8,6},{10,8},{12,10},{14,12},{16,14},{18,16},{20... | collective-permute-start | bytes 3080 | tf_op jit(solution)/shard_map/ppermute | solution.py:38
  68.5 9.4 %collective-permute-start.12 = (f32[1,8,128]{2,1,0:T(8,128)S(1)}, f32[1,8,128]{2,1,0:T(8,128)S(1)}, u32[]{:S(2)}, u32[]{:S(2)}) collective-permute-start(f32[1,8,128]{2,1,0:T(8,128)S(1)} %get-tuple-element.112), channel_id=1, source_target_pairs={{0,2},{2,4},{4,6},{6,8},{8,10},{10,12},{12,14},{14,16},{16,18},{18... | collective-permute-start | bytes 12296 | tf_op jit(solution)/shard_map/ppermute | solution.py:36
  73.0 6.2 %collective-permute-start.13 = (f32[1,8,128]{2,1,0:T(8,128)S(1)}, f32[1,8,128]{2,1,0:T(8,128)S(1)}, u32[]{:S(2)}, u32[]{:S(2)}) collective-permute-start(f32[1,8,128]{2,1,0:T(8,128)S(1)} %get-tuple-element.113), channel_id=1, source_target_pairs={{2,0},{4,2},{6,4},{8,6},{10,8},{12,10},{14,12},{16,14},{18,16},{20... | collective-permute-start | bytes 12296 | tf_op jit(solution)/shard_map/ppermute | solution.py:38
  74.3 7.9 %collective-permute-start.18 = (f32[6,1,64]{2,1,0:T(1,128)S(1)}, f32[6,1,64]{2,1,0:T(1,128)S(1)}, u32[]{:S(2)}, u32[]{:S(2)}) collective-permute-start(f32[6,1,64]{2,1,0:T(1,128)S(1)} %get-tuple-element.157), channel_id=1, source_target_pairs={{0,1},{2,3},{4,5},{6,7},{8,9},{10,11},{12,13},{14,15},{16,17},{18,... | collective-permute-start | bytes 4616 | tf_op jit(solution)/shard_map/ppermute | solution.py:36
  76.5 5.7 %collective-permute-start.19 = (f32[6,1,64]{2,1,0:T(1,128)S(1)}, f32[6,1,64]{2,1,0:T(1,128)S(1)}, u32[]{:S(2)}, u32[]{:S(2)}) collective-permute-start(f32[6,1,64]{2,1,0:T(1,128)S(1)} %get-tuple-element.156), channel_id=1, source_target_pairs={{1,0},{3,2},{5,4},{7,6},{9,8},{11,10},{13,12},{15,14},{17,16},{19,... | collective-permute-start | bytes 4616 | tf_op jit(solution)/shard_map/ppermute | solution.py:38
  86.7 10.6 %collective-permute-start.20 = (f32[1,4,64]{2,1,0:T(4,128)S(1)}, f32[1,4,64]{2,1,0:T(4,128)S(1)}, u32[]{:S(2)}, u32[]{:S(2)}) collective-permute-start(f32[1,4,64]{2,1,0:T(4,128)S(1)} %get-tuple-element.164), channel_id=1, source_target_pairs={{0,2},{2,4},{4,6},{6,8},{8,10},{10,12},{12,14},{14,16},{16,18},{18... | collective-permute-start | bytes 3080 | tf_op jit(solution)/shard_map/ppermute | solution.py:36
  92.2 6.1 %collective-permute-start.21 = (f32[1,4,64]{2,1,0:T(4,128)S(1)}, f32[1,4,64]{2,1,0:T(4,128)S(1)}, u32[]{:S(2)}, u32[]{:S(2)}) collective-permute-start(f32[1,4,64]{2,1,0:T(4,128)S(1)} %get-tuple-element.165), channel_id=1, source_target_pairs={{2,0},{4,2},{6,4},{8,6},{10,8},{12,10},{14,12},{16,14},{18,16},{20... | collective-permute-start | bytes 3080 | tf_op jit(solution)/shard_map/ppermute | solution.py:38
  103.7 12.5 %collective-permute-start.24 = (f32[1,4,64]{2,1,0:T(4,128)S(1)}, f32[1,4,64]{2,1,0:T(4,128)S(1)}, u32[]{:S(2)}, u32[]{:S(2)}) collective-permute-start(f32[1,4,64]{2,1,0:T(4,128)S(1)} %get-tuple-element.162), channel_id=1, source_target_pairs={{0,2},{2,4},{4,6},{6,8},{8,10},{10,12},{12,14},{14,16},{16,18},{18... | collective-permute-start | bytes 3080 | tf_op jit(solution)/shard_map/ppermute | solution.py:36
  108.5 7.7 %collective-permute-start.25 = (f32[1,4,64]{2,1,0:T(4,128)S(1)}, f32[1,4,64]{2,1,0:T(4,128)S(1)}, u32[]{:S(2)}, u32[]{:S(2)}) collective-permute-start(f32[1,4,64]{2,1,0:T(4,128)S(1)} %get-tuple-element.163), channel_id=1, source_target_pairs={{2,0},{4,2},{6,4},{8,6},{10,8},{12,10},{14,12},{16,14},{18,16},{20... | collective-permute-start | bytes 3080 | tf_op jit(solution)/shard_map/ppermute | solution.py:38
  109.8 9.4 %collective-permute-start.28 = (f32[1,4,32]{2,0,1:T(1,128)S(1)}, f32[1,4,32]{2,0,1:T(1,128)S(1)}, u32[]{:S(2)}, u32[]{:S(2)}) collective-permute-start(f32[1,4,32]{2,0,1:T(1,128)S(1)} %get-tuple-element.179), channel_id=1, source_target_pairs={{0,2},{2,4},{4,6},{6,8},{8,10},{10,12},{12,14},{14,16},{16,18},{18... | collective-permute-start | bytes 1544 | tf_op jit(solution)/shard_map/ppermute | solution.py:36
  114.9 6.6 %collective-permute-start.29 = (f32[1,4,32]{2,0,1:T(1,128)S(1)}, f32[1,4,32]{2,0,1:T(1,128)S(1)}, u32[]{:S(2)}, u32[]{:S(2)}) collective-permute-start(f32[1,4,32]{2,0,1:T(1,128)S(1)} %get-tuple-element.180), channel_id=1, source_target_pairs={{2,0},{4,2},{6,4},{8,6},{10,8},{12,10},{14,12},{16,14},{18,16},{20... | collective-permute-start | bytes 1544 | tf_op jit(solution)/shard_map/ppermute | solution.py:38
  124.2 13.4 %collective-permute-start.30 = (f32[1,4,32]{2,0,1:T(1,128)S(1)}, f32[1,4,32]{2,0,1:T(1,128)S(1)}, u32[]{:S(2)}, u32[]{:S(2)}) collective-permute-start(f32[1,4,32]{2,0,1:T(1,128)S(1)} %get-tuple-element.177), channel_id=1, source_target_pairs={{0,2},{2,4},{4,6},{6,8},{8,10},{10,12},{12,14},{14,16},{16,18},{18... | collective-permute-start | bytes 1544 | tf_op jit(solution)/shard_map/ppermute | solution.py:36
  129.2 8.4 %collective-permute-start.31 = (f32[1,4,32]{2,0,1:T(1,128)S(1)}, f32[1,4,32]{2,0,1:T(1,128)S(1)}, u32[]{:S(2)}, u32[]{:S(2)}) collective-permute-start(f32[1,4,32]{2,0,1:T(1,128)S(1)} %get-tuple-element.178), channel_id=1, source_target_pairs={{2,0},{4,2},{6,4},{8,6},{10,8},{12,10},{14,12},{16,14},{18,16},{20... | collective-permute-start | bytes 1544 | tf_op jit(solution)/shard_map/ppermute | solution.py:38
  130.5 15.0 %collective-permute-start.34 = (f32[1,2,16]{2,1,0:T(2,128)S(1)}, f32[1,2,16]{2,1,0:T(2,128)S(1)}, u32[]{:S(2)}, u32[]{:S(2)}) collective-permute-start(f32[1,2,16]{2,1,0:T(2,128)S(1)} %multiply_bitcast_fusion), channel_id=1, source_target_pairs={{0,2},{2,4},{4,6},{6,8},{8,10},{10,12},{12,14},{14,16},{16,18},{18... | collective-permute-start | bytes 392 | tf_op jit(solution)/shard_map/ppermute | solution.py:36
  136.3 9.2 %collective-permute-start.35 = (f32[1,2,16]{2,1,0:T(2,128)S(1)}, f32[1,2,16]{2,1,0:T(2,128)S(1)}, u32[]{:S(2)}, u32[]{:S(2)}) collective-permute-start(f32[1,2,16]{2,1,0:T(2,128)S(1)} %multiply_bitcast_fusion), channel_id=1, source_target_pairs={{2,0},{4,2},{6,4},{8,6},{10,8},{12,10},{14,12},{16,14},{18,16},{20... | collective-permute-start | bytes 392 | tf_op jit(solution)/shard_map/ppermute | solution.py:38
  137.8 7.8 %collective-permute-start.32 = (f32[1,4,32]{2,0,1:T(1,128)S(1)}, f32[1,4,32]{2,0,1:T(1,128)S(1)}, u32[]{:S(2)}, u32[]{:S(2)}) collective-permute-start(f32[1,4,32]{2,0,1:T(1,128)S(1)} %get-tuple-element.175), channel_id=1, source_target_pairs={{0,2},{2,4},{4,6},{6,8},{8,10},{10,12},{12,14},{14,16},{16,18},{18... | collective-permute-start | bytes 1544 | tf_op jit(solution)/shard_map/ppermute | solution.py:36
  144.2 6.4 %collective-permute-start.33 = (f32[1,4,32]{2,0,1:T(1,128)S(1)}, f32[1,4,32]{2,0,1:T(1,128)S(1)}, u32[]{:S(2)}, u32[]{:S(2)}) collective-permute-start(f32[1,4,32]{2,0,1:T(1,128)S(1)} %get-tuple-element.176), channel_id=1, source_target_pairs={{2,0},{4,2},{6,4},{8,6},{10,8},{12,10},{14,12},{16,14},{18,16},{20... | collective-permute-start | bytes 1544 | tf_op jit(solution)/shard_map/ppermute | solution.py:38
  151.0 9.9 %collective-permute-start.36 = (f32[1,2,16]{2,1,0:T(2,128)S(1)}, f32[1,2,16]{2,1,0:T(2,128)S(1)}, u32[]{:S(2)}, u32[]{:S(2)}) collective-permute-start(f32[1,2,16]{2,1,0:T(2,128)S(1)} %get-tuple-element.63), channel_id=1, source_target_pairs={{0,2},{2,4},{4,6},{6,8},{8,10},{10,12},{12,14},{14,16},{16,18},{18... | collective-permute-start | bytes 392 | tf_op jit(solution)/shard_map/ppermute | solution.py:36
  156.6 7.3 %collective-permute-start.37 = (f32[1,2,16]{2,1,0:T(2,128)S(1)}, f32[1,2,16]{2,1,0:T(2,128)S(1)}, u32[]{:S(2)}, u32[]{:S(2)}) collective-permute-start(f32[1,2,16]{2,1,0:T(2,128)S(1)} %get-tuple-element.63), channel_id=1, source_target_pairs={{2,0},{4,2},{6,4},{8,6},{10,8},{12,10},{14,12},{16,14},{18,16},{20... | collective-permute-start | bytes 392 | tf_op jit(solution)/shard_map/ppermute | solution.py:38
  164.0 7.6 %collective-permute-start.38 = (f32[1,2,16]{2,1,0:T(2,128)S(1)}, f32[1,2,16]{2,1,0:T(2,128)S(1)}, u32[]{:S(2)}, u32[]{:S(2)}) collective-permute-start(f32[1,2,16]{2,1,0:T(2,128)S(1)} %divide_add_fusion.3), channel_id=1, source_target_pairs={{0,2},{2,4},{4,6},{6,8},{8,10},{10,12},{12,14},{14,16},{16,18},{18... | collective-permute-start | bytes 392 | tf_op jit(solution)/shard_map/ppermute | solution.py:36
  175.4 6.1 %collective-permute-start.40 = (f32[1,2,16]{2,1,0:T(2,128)S(1)}, f32[1,2,16]{2,1,0:T(2,128)S(1)}, u32[]{:S(2)}, u32[]{:S(2)}) collective-permute-start(f32[1,2,16]{2,1,0:T(2,128)S(1)} %divide_add_fusion.2), channel_id=1, source_target_pairs={{0,2},{2,4},{4,6},{6,8},{8,10},{10,12},{12,14},{14,16},{16,18},{18... | collective-permute-start | bytes 392 | tf_op jit(solution)/shard_map/ppermute | solution.py:36
  195.8 6.7 %collective-permute-start.44 = (f32[1,4,32]{2,0,1:T(1,128)S(1)}, f32[1,4,32]{2,0,1:T(1,128)S(1)}, u32[]{:S(2)}, u32[]{:S(2)}) collective-permute-start(f32[1,4,32]{2,0,1:T(1,128)S(1)} %get-tuple-element.170), channel_id=1, source_target_pairs={{0,2},{2,4},{4,6},{6,8},{8,10},{10,12},{12,14},{14,16},{16,18},{18... | collective-permute-start | bytes 1544 | tf_op jit(solution)/shard_map/ppermute | solution.py:36
  206.6 5.8 %collective-permute-start.46 = (f32[1,4,64]{2,1,0:T(4,128)S(1)}, f32[1,4,64]{2,1,0:T(4,128)S(1)}, u32[]{:S(2)}, u32[]{:S(2)}) collective-permute-start(f32[1,4,64]{2,1,0:T(4,128)S(1)} %get-tuple-element.160), channel_id=1, source_target_pairs={{0,2},{2,4},{4,6},{6,8},{8,10},{10,12},{12,14},{14,16},{16,18},{18... | collective-permute-start | bytes 3080 | tf_op jit(solution)/shard_map/ppermute | solution.py:36
  216.0 6.0 %collective-permute-start.48 = (f32[6,1,64]{2,1,0:T(1,128)S(1)}, f32[6,1,64]{2,1,0:T(1,128)S(1)}, u32[]{:S(2)}, u32[]{:S(2)}) collective-permute-start(f32[6,1,64]{2,1,0:T(1,128)S(1)} %get-tuple-element.148), channel_id=1, source_target_pairs={{0,1},{2,3},{4,5},{6,7},{8,9},{10,11},{12,13},{14,15},{16,17},{18,... | collective-permute-start | bytes 4616 | tf_op jit(solution)/shard_map/ppermute | solution.py:36
  222.2 8.0 %collective-permute-start.50 = (f32[1,4,64]{2,1,0:T(4,128)S(1)}, f32[1,4,64]{2,1,0:T(4,128)S(1)}, u32[]{:S(2)}, u32[]{:S(2)}) collective-permute-start(f32[1,4,64]{2,1,0:T(4,128)S(1)} %get-tuple-element.158), channel_id=1, source_target_pairs={{0,2},{2,4},{4,6},{6,8},{8,10},{10,12},{12,14},{14,16},{16,18},{18... | collective-permute-start | bytes 3080 | tf_op jit(solution)/shard_map/ppermute | solution.py:36
  231.4 6.9 %collective-permute-start.52 = (f32[6,1,64]{2,1,0:T(1,128)S(1)}, f32[6,1,64]{2,1,0:T(1,128)S(1)}, u32[]{:S(2)}, u32[]{:S(2)}) collective-permute-start(f32[6,1,64]{2,1,0:T(1,128)S(1)} %get-tuple-element.146), channel_id=1, source_target_pairs={{0,1},{2,3},{4,5},{6,7},{8,9},{10,11},{12,13},{14,15},{16,17},{18,... | collective-permute-start | bytes 4616 | tf_op jit(solution)/shard_map/ppermute | solution.py:36
  238.9 5.6 %collective-permute-start.54 = (f32[1,8,128]{2,1,0:T(8,128)S(1)}, f32[1,8,128]{2,1,0:T(8,128)S(1)}, u32[]{:S(2)}, u32[]{:S(2)}) collective-permute-start(f32[1,8,128]{2,1,0:T(8,128)S(1)} %get-tuple-element.110), channel_id=1, source_target_pairs={{0,2},{2,4},{4,6},{6,8},{8,10},{10,12},{12,14},{14,16},{16,18},{18... | collective-permute-start | bytes 12296 | tf_op jit(solution)/shard_map/ppermute | solution.py:36
  243.1 5.7 %collective-permute-start.55 = (f32[1,8,128]{2,1,0:T(8,128)S(1)}, f32[1,8,128]{2,1,0:T(8,128)S(1)}, u32[]{:S(2)}, u32[]{:S(2)}) collective-permute-start(f32[1,8,128]{2,1,0:T(8,128)S(1)} %get-tuple-element.111), channel_id=1, source_target_pairs={{2,0},{4,2},{6,4},{8,6},{10,8},{12,10},{14,12},{16,14},{18,16},{20... | collective-permute-start | bytes 12296 | tf_op jit(solution)/shard_map/ppermute | solution.py:38
  248.9 9.3 %collective-permute-start.56 = (f32[10,1,128]{2,1,0:T(1,128)S(1)}, f32[10,1,128]{2,1,0:T(1,128)S(1)}, u32[]{:S(2)}, u32[]{:S(2)}) collective-permute-start(f32[10,1,128]{2,1,0:T(1,128)S(1)} %get-tuple-element.93), channel_id=1, source_target_pairs={{0,1},{2,3},{4,5},{6,7},{8,9},{10,11},{12,13},{14,15},{16,17},{18,... | collective-permute-start | bytes 15368 | tf_op jit(solution)/shard_map/ppermute | solution.py:36
  250.9 7.3 %collective-permute-start.57 = (f32[10,1,128]{2,1,0:T(1,128)S(1)}, f32[10,1,128]{2,1,0:T(1,128)S(1)}, u32[]{:S(2)}, u32[]{:S(2)}) collective-permute-start(f32[10,1,128]{2,1,0:T(1,128)S(1)} %get-tuple-element.94), channel_id=1, source_target_pairs={{1,0},{3,2},{5,4},{7,6},{9,8},{11,10},{13,12},{15,14},{17,16},{19,... | collective-permute-start | bytes 15368 | tf_op jit(solution)/shard_map/ppermute | solution.py:38
  258.5 16.2 %collective-permute-start.58 = (f32[1,8,128]{2,1,0:T(8,128)S(1)}, f32[1,8,128]{2,1,0:T(8,128)S(1)}, u32[]{:S(2)}, u32[]{:S(2)}) collective-permute-start(f32[1,8,128]{2,1,0:T(8,128)S(1)} %get-tuple-element.108), channel_id=1, source_target_pairs={{0,2},{2,4},{4,6},{6,8},{8,10},{10,12},{12,14},{14,16},{16,18},{18... | collective-permute-start | bytes 12296 | tf_op jit(solution)/shard_map/ppermute | solution.py:36
  262.9 11.8 %collective-permute-start.59 = (f32[1,8,128]{2,1,0:T(8,128)S(1)}, f32[1,8,128]{2,1,0:T(8,128)S(1)}, u32[]{:S(2)}, u32[]{:S(2)}) collective-permute-start(f32[1,8,128]{2,1,0:T(8,128)S(1)} %get-tuple-element.109), channel_id=1, source_target_pairs={{2,0},{4,2},{6,4},{8,6},{10,8},{12,10},{14,12},{16,14},{18,16},{20... | collective-permute-start | bytes 12296 | tf_op jit(solution)/shard_map/ppermute | solution.py:38
  280.8 6.5 %collective-permute-start.62 = (f32[1,8,128]{2,1,0:T(8,128)S(1)}, f32[1,8,128]{2,1,0:T(8,128)S(1)}, u32[]{:S(2)}, u32[]{:S(2)}) collective-permute-start(f32[1,8,128]{2,1,0:T(8,128)S(1)} %get-tuple-element.107), channel_id=1, source_target_pairs={{2,0},{4,2},{6,4},{8,6},{10,8},{12,10},{14,12},{16,14},{18,16},{20... | collective-permute-start | bytes 12296 | tf_op jit(solution)/shard_map/ppermute | solution.py:38
  282.1 6.2 %collective-permute-start.63 = (f32[1,8,128]{2,1,0:T(8,128)S(1)}, f32[1,8,128]{2,1,0:T(8,128)S(1)}, u32[]{:S(2)}, u32[]{:S(2)}) collective-permute-start(f32[1,8,128]{2,1,0:T(8,128)S(1)} %get-tuple-element.106), channel_id=1, source_target_pairs={{0,2},{2,4},{4,6},{6,8},{8,10},{10,12},{12,14},{14,16},{16,18},{18... | collective-permute-start | bytes 12296 | tf_op jit(solution)/shard_map/ppermute | solution.py:36
  288.3 22.8 %collective-permute-start.64 = (f32[10,1,128]{2,1,0:T(1,128)S(1)}, f32[10,1,128]{2,1,0:T(1,128)S(1)}, u32[]{:S(2)}, u32[]{:S(2)}) collective-permute-start(f32[10,1,128]{2,1,0:T(1,128)S(1)} %get-tuple-element.90), channel_id=1, source_target_pairs={{1,0},{3,2},{5,4},{7,6},{9,8},{11,10},{13,12},{15,14},{17,16},{19,... | collective-permute-start | bytes 15368 | tf_op jit(solution)/shard_map/ppermute | solution.py:38
  289.6 21.5 %collective-permute-start.65 = (f32[10,1,128]{2,1,0:T(1,128)S(1)}, f32[10,1,128]{2,1,0:T(1,128)S(1)}, u32[]{:S(2)}, u32[]{:S(2)}) collective-permute-start(f32[10,1,128]{2,1,0:T(1,128)S(1)} %get-tuple-element.89), channel_id=1, source_target_pairs={{0,1},{2,3},{4,5},{6,7},{8,9},{10,11},{12,13},{14,15},{16,17},{18,... | collective-permute-start | bytes 15368 | tf_op jit(solution)/shard_map/ppermute | solution.py:36
  320.3 12.3 %collective-permute-start.66 = (f32[3,384]{1,0:T(4,128)S(1)}, f32[3,384]{1,0:T(4,128)S(1)}, u32[]{:S(2)}, u32[]{:S(2)}) collective-permute-start(f32[3,384]{1,0:T(4,128)S(1)} %bitcast.254), channel_id=1, source_target_pairs={{0,4},{2,6},{4,8},{6,10},{8,12},{10,14},{12,16},{14,18},{16,20},{1... | collective-permute-start | bytes 13832 | tf_op jit(solution)/shard_map/ppermute | solution.py:48
  325.5 7.1 %collective-permute-start.67 = (f32[3,384]{1,0:T(4,128)S(1)}, f32[3,384]{1,0:T(4,128)S(1)}, u32[]{:S(2)}, u32[]{:S(2)}) collective-permute-start(f32[3,384]{1,0:T(4,128)S(1)} %bitcast.255), channel_id=1, source_target_pairs={{0,2},{2,4},{4,6},{6,8},{8,10},{10,12},{12,14},{14,16},{16,18},{18... | collective-permute-start | bytes 13832 | tf_op jit(solution)/shard_map/ppermute | solution.py:48
  329.3 8.4 %collective-permute-start.68 = (f32[3,384]{1,0:T(4,128)S(1)}, f32[3,384]{1,0:T(4,128)S(1)}, u32[]{:S(2)}, u32[]{:S(2)}) collective-permute-start(f32[3,384]{1,0:T(4,128)S(1)} %bitcast.256), channel_id=1, source_target_pairs={{2,0},{4,2},{6,4},{8,6},{10,8},{12,10},{14,12},{16,14},{18,16},{20... | collective-permute-start | bytes 13832 | tf_op jit(solution)/shard_map/ppermute | solution.py:48
  330.6 10.4 %collective-permute-start.69 = (f32[3,384]{1,0:T(4,128)S(1)}, f32[3,384]{1,0:T(4,128)S(1)}, u32[]{:S(2)}, u32[]{:S(2)}) collective-permute-start(f32[3,384]{1,0:T(4,128)S(1)} %bitcast.257), channel_id=1, source_target_pairs={{4,0},{6,2},{8,4},{10,6},{12,8},{14,10},{16,12},{18,14},{20,16},{2... | collective-permute-start | bytes 13832 | tf_op jit(solution)/shard_map/ppermute | solution.py:48
  (31 other events, 637.0 us)
where the time goes:
time: 344 us; the launch traced here: 342 us
  starting transfers between devices  180 us (52%)
  waiting for transfers between devices  56.7 us (16%)
  local copies, waits for them, and re-layouts  49.9 us (15%)
  other arithmetic  47 us (14%)
  blocking collectives  4.38 us (1%)
    ppermute x31, starting transfers between devices, padded_2(): lax.ppermute(tail, axis, [(i, (i + 1) % count) for i in range(ends)])  116 us
    ppermute x31, waiting for transfers between devices, padded_2(): lax.ppermute(head, axis, [((i + 1) % count, i) for i in range(ends)])  47.2 us
    ppermute x31, starting transfers between devices, padded_2(): lax.ppermute(head, axis, [((i + 1) % count, i) for i in range(ends)])  40 us
    ppermute x8, starting transfers between devices, from_behind(): return lax.ppermute(block, axis, route)  24.2 us
    scatter-add x1, other arithmetic, local(): jnp.zeros((3, total_cells), jnp.float32).at[:, where_in].add(-drag_force)  15.5 us
    scatter-add x1, other arithmetic, local(): solid_sum = jnp.zeros((total_cells,), jnp.float32).at[where_in].add(vol_in)  13.7 us
    gather x1, local copies, waits for them, and re-layouts, local(): voidage[where_in] ** (-void_power)  10.4 us
    ppermute x8, waiting for transfers between devices, from_behind(): return lax.ppermute(block, axis, route)  8.48 us
  transfers between devices with their start and end apart: 70, of which 19 were waited for; matrix products, arithmetic and copies ran while one was open for 19% of the time, Pallas kernels for 0%

commit v1 on v0

v1 whole, which is shorter than its diff:
```python
import functools

import jax
import jax.numpy as jnp
from jax import lax
from jax.experimental import pallas as pl
from jax.experimental.pallas import tpu as pltpu
from jax.sharding import PartitionSpec as P

SPREAD = 2
SWEEPS = 2
COARSE_SWEEPS = 4
CAP = 3
GROUPS = 2 * SPREAD + 1
HALO = 5
REACH = 4

relax_weight = 0.8
solid_most = 0.6
void_power = 2.65
drag_base = 0.5
drag_slope = 0.5
stiffness = 16.0
softening = 0.1
particle_density = 2.0
gas_density = 1.0
step_duration = 0.25
gravity = -1.0

F32 = jnp.float32
BF16 = jnp.bfloat16
VMEM = pl.BlockSpec(memory_space=pltpu.VMEM)
SMEM = pl.BlockSpec(memory_space=pltpu.SMEM)
HIGHEST = lax.Precision.HIGHEST
VOL_ROW = 0
CELL_ROW = 3 * CAP
VEL_ROW = 6 * CAP
SOURCE_ROW = 32
VMEM_LIMIT = 60 * 1024 * 1024


def call(kernel, out_shape, in_specs, out_specs, scratch=(), flops=0):
    return pl.pallas_call(
        kernel,
        out_shape=out_shape,
        in_specs=in_specs,
        out_specs=out_specs,
        scratch_shapes=list(scratch),
        compiler_params=pltpu.CompilerParams(vmem_limit_bytes=VMEM_LIMIT),
        cost_estimate=pl.CostEstimate(flops=flops, bytes_accessed=1 << 18, transcendentals=0),
    )


def f32s(*shape):
    return jax.ShapeDtypeStruct(shape, F32)


def iota(shape, dim):
    return lax.broadcasted_iota(jnp.int32, shape, dim)


def back(value, step, axis):
    return pltpu.roll(value, step, axis)


def ahead(value, step, axis):
    return pltpu.roll(value, value.shape[axis] - step, axis)


def ranks(offset_ref, count):
    offsets = [offset_ref[i] for i in range(count)]
    found = []
    for i in range(count):
        rank = jnp.int32(0)
        for j in range(i):
            rank = rank + jnp.where(offsets[j] == offsets[i], 1, 0)
        found.append(rank)
    return offsets, found


def pack_kernel(wide, offset_ref, count_ref, radius_ref, vel_ref, cell_ref, source_ref, before_ref, send_ref, s_ref):
    w = lax.axis_index("wide")
    blocks, slots = radius_ref.shape
    depth, lanes, _ = source_ref.shape
    send_ref[...] = jnp.zeros(send_ref.shape, F32)
    offsets, rank = ranks(offset_ref, blocks)
    slot = iota((1, slots), 1)
    for b in range(blocks):
        radius = radius_ref[b : b + 1, :]
        vol = jnp.where(slot < count_ref[b], radius * radius * radius, 0.0)
        cell = cell_ref[b : b + 1, :].astype(F32)
        for e in (-1, 0, 1):
            target = w + offsets[b] - e

            @pl.when(jnp.logical_and(target >= 0, target < wide))
            def _():
                row = (e + 1) * CAP + rank[b]
                send_ref[target, pl.ds(VOL_ROW + row, 1), :] = vol
                send_ref[target, pl.ds(CELL_ROW + row, 1), :] = cell
                if e == 0:
                    for c in range(3):
                        send_ref[target, pl.ds(VEL_ROW + c * CAP + rank[b], 1), :] = vel_ref[c, b : b + 1, :]

    for z in range(depth):
        s_ref[z] = source_ref[z] + before_ref[z] * (1.0 / step_duration)

    @pl.when(w + 1 < wide)
    def _():
        for z in range(REACH):
            send_ref[w + 1, SOURCE_ROW + z * lanes : SOURCE_ROW + (z + 1) * lanes, :] = s_ref[depth - REACH + z]

    @pl.when(w > 0)
    def _():
        for z in range(REACH):
            send_ref[w - 1, SOURCE_ROW + z * lanes : SOURCE_ROW + (z + 1) * lanes, :] = s_ref[z]


def cell_rows(cell_row):
    cell = cell_row.astype(jnp.int32)
    return cell >> 7, cell & 127


def pieces_of(value):
    high = value.astype(BF16).astype(F32)
    return high, value - high


def contract(lhs, rhs):
    return lax.dot_general(lhs, rhs, (((1,), (1,)), ((), ())), preferred_element_type=F32)


def solid_of(vols, cells, first, rows):
    total = jnp.zeros((2 * rows, 128), F32)
    place = iota((rows, 128), 0) + first
    column = iota((128, 128), 0)
    for pair in range(0, len(vols), 2):
        left, right = [], []
        for k in range(pair, min(pair + 2, len(vols))):
            zy, x = cell_rows(cells[k])
            here = place == zy
            high, low = pieces_of(vols[k])
            left.append(
                jnp.concatenate([jnp.where(here, high, 0.0), jnp.where(here, low, 0.0)], axis=0).astype(BF16)
            )
            right.append(jnp.where(column == x, 1.0, 0.0).astype(BF16))
        total = total + contract(jnp.concatenate(left, axis=1), jnp.concatenate(right, axis=1))
    return total[:rows] + total[rows:]


def void_kernel(wide, recv_ref, s_ref, window_ref, rows_ref):
    w = lax.axis_index("wide")
    depth, lanes, _ = s_ref.shape
    cells = depth * lanes
    rows_ref[...] = jnp.zeros(rows_ref.shape, F32)
    for e in (-1, 0, 1):
        vols, codes = [], []
        for g in range(GROUPS):
            source = w + e - (g - SPREAD)
            inside = jnp.logical_and(source >= 0, source < wide)
            source = jnp.clip(source, 0, wide - 1)
            row = (e + 1) * CAP
            for r in range(CAP):
                k = g * CAP + r
                vol = jnp.where(inside, recv_ref[source, VOL_ROW + row + r : VOL_ROW + row + r + 1, :], 0.0)
                code = recv_ref[source, CELL_ROW + row + r : CELL_ROW + row + r + 1, :]
                vols.append(vol)
                codes.append(code)
                if e == 0:
                    rows_ref[0, k : k + 1, :] = vol
                    rows_ref[1, k : k + 1, :] = code
                    for c in range(3):
                        at = VEL_ROW + c * CAP + r
                        rows_ref[2 + c, k : k + 1, :] = recv_ref[source, at : at + 1, :]
        low = depth - HALO if e < 0 else 0
        layers = depth if e == 0 else HALO
        first = 0 if e >= 0 else (low * lanes) // 16 * 16
        count = cells if e == 0 else -(-(layers * lanes + (low * lanes - first)) // 16) * 16
        solid = solid_of(vols, codes, first, count)
        void = 1.0 - solid_most * solid / (1.0 + solid)
        exists = jnp.logical_and(w + e >= 0, w + e < wide)
        void = jnp.where(exists, void, 0.0)
        base = HALO + (e * HALO if e < 0 else e * depth)
        for z in range(layers):
            start = (low + z) * lanes - first
            window_ref[base + z] = void[start : start + lanes]
    voids = depth + 2 * HALO
    for z in range(depth):
        window_ref[voids + REACH + z] = s_ref[z]
    for e in (-1, 1):
        beside = w + e
        exists = jnp.logical_and(beside >= 0, beside < wide)
        beside = jnp.clip(beside, 0, wide - 1)
        for z in range(REACH):
            part = recv_ref[beside, SOURCE_ROW + z * lanes : SOURCE_ROW + (z + 1) * lanes, :]
            at = voids + (z if e < 0 else REACH + depth + z)
            window_ref[at] = jnp.where(exists, part, 0.0)


def gather_cells(refs, zy, x, rows):
    found = [jnp.zeros(zy.shape, F32) for _ in refs]
    for row in range(rows):
        here = zy == row
        for i, ref in enumerate(refs):
            source = jnp.broadcast_to(ref(row), zy.shape)
            found[i] = jnp.where(here, jnp.take_along_axis(source, x, axis=1), found[i])
    return found


def drag_kernel(window_ref, rows_ref, gas_ref, drag_ref, base_ref):
    _, depth, lanes, _ = gas_ref.shape
    cells = depth * lanes
    vol = rows_ref[0]
    zy, x = cell_rows(rows_ref[1])

    def table(c):
        return lambda row: gas_ref[c, row // lanes, row % lanes : row % lanes + 1, :]

    def voids(row):
        return window_ref[HALO + row // lanes, row % lanes : row % lanes + 1, :]

    gas_z, gas_y, gas_x, void = gather_cells([table(0), table(1), table(2), voids], zy, x, cells)
    slips = [gas_z - rows_ref[2], gas_y - rows_ref[3], gas_x - rows_ref[4]]
    speed = jnp.sqrt(slips[0] * slips[0] + slips[1] * slips[1] + slips[2] * slips[2])
    scale = vol * (drag_base + drag_slope * speed) * jnp.exp(-void_power * jnp.log(void))
    drags = [scale * slip for slip in slips]
    for c in range(3):
        drag_ref[c] = drags[c]
    split = []
    for c in range(3):
        split += list(pieces_of(drags[c]))
    total = jnp.zeros((6 * cells, 128), F32)
    place = iota((cells, 128), 0)
    column = iota((128, 128), 0)
    for pair in range(0, vol.shape[0], 2):
        left, right = [], []
        for k in range(pair, pair + 2):
            here = place == zy[k : k + 1]
            left.append(
                jnp.concatenate([jnp.where(here, part[k : k + 1], 0.0) for part in split], axis=0).astype(BF16)
            )
            right.append(jnp.where(column == x[k : k + 1], 1.0, 0.0).astype(BF16))
        total = total + contract(jnp.concatenate(left, axis=1), jnp.concatenate(right, axis=1))
    for z in range(depth):
        per_void = step_duration / (gas_density * window_ref[HALO + z])
        for c in range(3):
            start = 2 * c * cells + z * lanes
            given = total[start : start + lanes] + total[start + cells : start + cells + lanes]
            base_ref[c, z] = gas_ref[c, z] - per_void * given


def fill_window(pieces, spots, lanes, void_ref, source_ref):
    voids = void_ref.shape[0]
    for piece, spot in zip(pieces, spots):
        at = pl.ds(spot * lanes if isinstance(spot, int) else pl.multiple_of(spot * lanes, lanes), lanes)
        for z in range(voids):
            void_ref[z, at, :] = piece[z]
        for z in range(source_ref.shape[0]):
            source_ref[z, at, :] = piece[voids + z]


def side_masks(lanes, width):
    y, x = iota((lanes, width), 0), iota((lanes, width), 1)
    return (y >= 1, y < lanes - 1, x >= 1, x < width - 1)


def sides(value, masks, step_y, step_x):
    return (
        jnp.where(masks[0], back(value, step_y, 0), 0.0),
        jnp.where(masks[1], ahead(value, step_y, 0), 0.0),
        jnp.where(masks[2], back(value, step_x, 1), 0.0),
        jnp.where(masks[3], ahead(value, step_x, 1), 0.0),
    )


def fine_start(void_ref, source_ref, coef_ref, diag_ref, first_ref):
    layers, lanes, width = source_ref.shape
    masks = side_masks(lanes, width)
    for i in range(layers):
        p = void_ref[i + 1]
        around = (void_ref[i], void_ref[i + 2]) + sides(p, masks, 1, 1)
        sums = [p + q for q in around]
        diag = sums[0] + sums[1] + sums[2] + sums[3] + sums[4] + sums[5]
        inside = p > 0.0
        inverse = jnp.where(inside, relax_weight / jnp.where(inside, diag, 1.0), 0.0)
        for k in range(6):
            coef = sums[k] * inverse
            if k >= 2:
                coef = jnp.where(masks[k - 2], coef, 0.0)
            coef_ref[k, i] = coef
        if diag_ref is not None:
            diag_ref[i] = diag * (0.5 / relax_weight)
        first_ref[i] = (source_ref[i] - p * (1.0 / step_duration)) * inverse * 2.0


def pull(coef_ref, i, below, here, above, step_y=1, step_x=1):
    total = coef_ref[0, i] * below + coef_ref[1, i] * above
    total = total + coef_ref[2, i] * back(here, step_y, 0) + coef_ref[3, i] * ahead(here, step_y, 0)
    return total + coef_ref[4, i] * back(here, step_x, 1) + coef_ref[5, i] * ahead(here, step_x, 1)


def fine_sweep(coef_ref, first_ref, old_ref, new_ref, start, stop):
    for i in range(start, stop):
        here = old_ref[i]
        new_ref[i] = (
            (1.0 - relax_weight) * here
            + first_ref[i]
            + pull(coef_ref, i, old_ref[i - 1], here, old_ref[i + 1])
        )


def spread_matrix(rows, columns, shift):
    return jnp.where(iota((rows, columns), 1) // 2 + shift == iota((rows, columns), 0), 1.0, 0.0)


def mean_matrix(width, shift):
    return jnp.where(iota((width, width), 0) // 2 + shift == iota((width, width), 1), 0.125, 0.0)


def coarsen_kernel(wide, *refs):
    *pieces, send_ref, void_ref, source_ref, coef_ref, diag_ref, first_ref, next_ref, fold_ref = refs
    narrow = len(pieces)
    lanes = pieces[0].shape[1]
    n = lax.axis_index("narrow")
    spots = [n, 1 - n] if narrow == 2 else list(range(narrow))
    fill_window(pieces, spots, lanes, void_ref, source_ref)
    fine_start(void_ref, source_ref, coef_ref, diag_ref, first_ref)
    layers, width_y, width = source_ref.shape
    depth = layers - 2 * REACH
    fine_sweep(coef_ref, first_ref, first_ref, next_ref, REACH - 1, layers - REACH + 1)
    half = depth // 2
    rows = half * width_y
    for k in range(half):
        total = jnp.zeros((width_y, width), F32)
        for i in (REACH + 2 * k, REACH + 2 * k + 1):
            here = next_ref[i]
            total = total + diag_ref[i] * (
                first_ref[i]
                - relax_weight * here
                + pull(coef_ref, i, next_ref[i - 1], here, next_ref[i + 1])
            )
        fold_ref[0, k * width_y : (k + 1) * width_y, :] = total
        fold_ref[1, k * width_y : (k + 1) * width_y, :] = void_ref[HALO + 2 * k] + void_ref[HALO + 2 * k + 1]
    right = fold_ref[0, pl.ds(0, rows // 2, stride=2), :] + fold_ref[0, pl.ds(1, rows // 2, stride=2), :]
    porous = fold_ref[1, pl.ds(0, rows // 2, stride=2), :] + fold_ref[1, pl.ds(1, rows // 2, stride=2), :]
    coarse = jnp.dot(right, mean_matrix(width, 0), precision=HIGHEST, preferred_element_type=F32)
    coarse = coarse + jnp.dot(porous, mean_matrix(width, width // 2), precision=HIGHEST, preferred_element_type=F32)
    for t in range(wide):
        send_ref[t] = coarse


def loop(count, body, unroll=4):
    while count % unroll:
        unroll //= 2

    def step(i, _):
        for j in range(unroll):
            body(i * unroll + j)
        return 0

    lax.fori_loop(0, count // unroll, step, 0)


def close_halves(ref, first_half):
    last = ref.shape[0] - 2
    half = ref.shape[2] // 2
    ref[0] = jnp.where(first_half, 0.0, pltpu.roll(ref[last], half, 1))
    ref[last + 1] = jnp.where(first_half, pltpu.roll(ref[1], half, 1), 0.0)


class Level:
    def __init__(self, index, refs):
        self.index = index
        self.step = 2 ** (index - 1)
        self.porous, self.right, self.coef, self.diag, self.first, self.one, self.two = refs
        self.layers, lanes, width = self.right.shape
        half = width // 2
        y, x = iota((lanes, width), 0), iota((lanes, width), 1) % half
        self.first_half = iota((lanes, width), 1) < half
        self.masks = (y >= self.step, y < lanes - self.step, x >= self.step, x < half - self.step)

    def start(self):
        weight = 0.5 * 0.25**self.index
        close_halves(self.porous, self.first_half)

        def body(i):
            p = self.porous[i + 1]
            around = (self.porous[i], self.porous[i + 2]) + sides(p, self.masks, self.step, self.step)
            sums = [p + q for q in around]
            diag = sums[0] + sums[1] + sums[2] + sums[3] + sums[4] + sums[5]
            inverse = relax_weight / diag
            for k in range(6):
                coef = sums[k] * inverse
                if k >= 2:
                    coef = jnp.where(self.masks[k - 2], coef, 0.0)
                self.coef[k, i] = coef
            self.diag[i] = diag * (weight / relax_weight)

        loop(self.layers, body)

    def begin(self):
        weight = 0.5 * 0.25**self.index

        def body(i):
            value = self.right[i] / self.diag[i]
            self.first[i] = value
            self.one[i + 1] = value

        loop(self.layers, body)

    def sweep(self):
        close_halves(self.one, self.first_half)

        def body(i):
            here = self.one[i + 1]
            self.two[i + 1] = (
                (1.0 - relax_weight) * here
                + self.first[i]
                + pull(self.coef, i, self.one[i], here, self.one[i + 2], self.step, self.step)
            )

        loop(self.layers, body)
        self.one, self.two = self.two, self.one

    def residual(self, i):
        here = self.one[i + 1]
        return self.diag[i] * (
            self.first[i]
            - relax_weight * here
            + pull(self.coef, i, self.one[i], here, self.one[i + 2], self.step, self.step)
        )

    def mean(self, value):
        y, x = iota(value.shape, 0), iota(value.shape, 1)
        value = value + jnp.where(
            (y & self.step) == 0, ahead(value, self.step, 0), back(value, self.step, 0)
        )
        value = value + jnp.where(
            (x & self.step) == 0, ahead(value, self.step, 1), back(value, self.step, 1)
        )
        return value * 0.125


def coarse_cycle(levels, index):
    level = levels[index]
    level.begin()
    last = index == len(levels) - 1
    for _ in range((COARSE_SWEEPS if last else SWEEPS) - 1):
        level.sweep()
    if not last:
        under = levels[index + 1]
        close_halves(level.one, level.first_half)

        def body(i):
            under.right[i] = level.mean(level.residual(2 * i) + level.residual(2 * i + 1))

        loop(under.layers, body)
        coarse_cycle(levels, index + 1)

        def add(i):
            correction = under.one[i + 1]
            level.one[2 * i + 1] = level.one[2 * i + 1] + correction
            level.one[2 * i + 2] = level.one[2 * i + 2] + correction

        loop(under.layers, add)
        for _ in range(SWEEPS):
            level.sweep()


def solve_kernel(wide, recv_ref, rows_ref, drag_ref, base_ref, *refs):
    pieces, refs = refs[: len(refs) - 33], refs[len(refs) - 33 :]
    pressure_ref, gas_ref, send_ref = refs[:3]
    level_refs = [refs[3 + 7 * i : 10 + 7 * i] for i in range(3)]
    void_ref, source_ref, coef_ref, first_ref, one_ref, two_ref, coarse_ref, fold_ref, slope_ref = refs[24:33]
    narrow = len(pieces)
    lanes = pieces[0].shape[1]
    n = lax.axis_index("narrow")
    w = lax.axis_index("wide")
    spots = [n, 1 - n] if narrow == 2 else list(range(narrow))
    fill_window(pieces, spots, lanes, void_ref, source_ref)
    layers, width_y, width = source_ref.shape
    depth = layers - 2 * REACH
    half, coarse_y = depth // 2, width_y // 2
    levels = [Level(i + 1, level_refs[i]) for i in range(3)]
    top = levels[0]
    middle = width // 2

    def unpack(t):
        for z in range(half):
            low = recv_ref[t, pl.ds(z * coarse_y, coarse_y), :]
            high = recv_ref[t + wide // 2, pl.ds(z * coarse_y, coarse_y), :]
            top.right[t * half + z] = jnp.where(top.first_half, low, pltpu.roll(high, middle, 1))
            top.porous[t * half + z + 1] = jnp.where(top.first_half, pltpu.roll(low, middle, 1), high)

    loop(wide // 2, unpack)
    for upper, lower in ((levels[0], levels[1]), (levels[1], levels[2])):

        def narrow_down(i):
            lower.porous[i + 1] = upper.mean(upper.porous[2 * i + 1] + upper.porous[2 * i + 2])

        loop(lower.layers, narrow_down)
    for level in levels:
        level.start()
    coarse_cycle(levels, 0)

    fine_start(void_ref, source_ref, coef_ref, None, first_ref)
    fine_sweep(coef_ref, first_ref, first_ref, one_ref, 1, layers - 1)
    total = top.layers
    spans = layers // 2
    for k in range(spans):
        z = w * half - REACH // 2 + k
        inside = jnp.logical_and(z >= 0, z < 2 * total)
        z = jnp.clip(z, 0, 2 * total - 1)
        upper = z >= total
        value = top.one[jnp.where(upper, z - total, z) + 1]
        value = jnp.where(upper, pltpu.roll(value, middle, 1), value)
        coarse_ref[k * coarse_y : (k + 1) * coarse_y, :] = jnp.where(inside, value, 0.0)
    wider = jnp.dot(coarse_ref[...], spread_matrix(width, width, 0), precision=HIGHEST, preferred_element_type=F32)
    count = spans * coarse_y
    fold_ref[pl.ds(0, count, stride=2), :] = wider
    fold_ref[pl.ds(1, count, stride=2), :] = wider
    for i in range(1, layers - 1):
        k = i // 2
        correction = fold_ref[k * width_y : (k + 1) * width_y, :]
        one_ref[i] = one_ref[i] + jnp.where(void_ref[i + 1] > 0.0, correction, 0.0)
    fine_sweep(coef_ref, first_ref, one_ref, two_ref, 2, layers - 2)
    fine_sweep(coef_ref, first_ref, two_ref, one_ref, 3, layers - 3)

    masks = side_masks(width_y, width)
    own = pl.ds(pl.multiple_of(n * lanes, lanes), lanes)
    for z in range(depth):
        i = REACH + z
        here = one_ref[i]
        before_y, after_y, before_x, after_x = sides(here, masks, 1, 1)
        slope_ref[0, z] = 0.5 * (one_ref[i + 1] - one_ref[i - 1])
        slope_ref[1, z] = 0.5 * (after_y - before_y)
        slope_ref[2, z] = 0.5 * (after_x - before_x)
        pressure_ref[z] = one_ref[i, own, :]
        for c in range(3):
            gas_ref[c, z] = base_ref[c, z] - (step_duration / gas_density) * slope_ref[c, z, own, :]

    zy, x = cell_rows(rows_ref[1])

    def table(c):
        return lambda row: slope_ref[c, row // lanes, pl.ds(n * lanes + row % lanes, 1), :]

    slopes = gather_cells([table(0), table(1), table(2)], zy, x, depth * lanes)
    forces = [drag_ref[c] - rows_ref[0] * slopes[c] for c in range(3)]
    for g in range(GROUPS):
        target = w - (g - SPREAD)

        @pl.when(jnp.logical_and(target >= 0, target < wide))
        def _():
            for c in range(3):
                send_ref[target, c * CAP : (c + 1) * CAP, :] = forces[c][g * CAP : (g + 1) * CAP]


def contact_kernel(near_ref, count_ref, pos_ref, radius_ref, force_ref, across_ref):
    blocks, slots = radius_ref.shape
    neighbours = near_ref.shape[1]
    slot = iota((1, slots), 1)
    for b in range(blocks):
        radius = jnp.where(slot < count_ref[b], radius_ref[b : b + 1, :], -100.0)
        for q in range(4):
            row = pos_ref[q, b : b + 1, :] if q < 3 else radius
            across_ref[q, b] = jnp.broadcast_to(row, (slots, slots)).T

    factor = stiffness / (slots * (neighbours + 1))
    for b in range(blocks):
        mine = [jnp.broadcast_to(pos_ref[c, b : b + 1, :], (8, slots)) for c in range(3)]
        mine_radius = jnp.broadcast_to(radius_ref[b : b + 1, :], (8, slots))

        def one(k, sums):
            j = jnp.where(k < neighbours, near_ref[b, jnp.minimum(k, neighbours - 1)], b)
            sums = list(sums)
            for row in range(0, slots, 8):
                apart = [mine[c] - across_ref[c, j, row : row + 8, :] for c in range(3)]
                square = apart[0] * apart[0] + apart[1] * apart[1] + (apart[2] * apart[2] + softening * softening)
                inverse = lax.rsqrt(square)
                overlap = jnp.maximum(mine_radius + across_ref[3, j, row : row + 8, :] - square * inverse, 0.0)
                weight = overlap * inverse
                for c in range(3):
                    sums[c] = sums[c] + apart[c] * weight
            return tuple(sums)

        sums = lax.fori_loop(0, neighbours + 1, one, tuple(jnp.zeros((8, slots), F32) for _ in range(3)))
        for c in range(3):
            force_ref[c, b : b + 1, :] = jnp.sum(sums[c], axis=0, keepdims=True) * factor


def move_kernel(wide, offset_ref, count_ref, recv_ref, contact_ref, radius_ref, vel_ref, out_ref):
    w = lax.axis_index("wide")
    blocks, slots = radius_ref.shape
    offsets, rank = ranks(offset_ref, blocks)
    slot = iota((1, slots), 1)
    for b in range(blocks):
        home = jnp.clip(w + offsets[b], 0, wide - 1)
        live = jnp.where(slot < count_ref[b], 1.0, 0.0)
        radius = radius_ref[b : b + 1, :]
        inverse = 1.0 / (particle_density * (radius * radius * radius))
        for c in range(3):
            fluid = recv_ref[home, pl.ds(c * CAP + rank[b], 1), :]
            push = (contact_ref[c, b : b + 1, :] + fluid) * inverse
            if c == 0:
                push = push + gravity
            out_ref[c, b : b + 1, :] = live * (vel_ref[c, b : b + 1, :] + step_duration * push)


def local(
    particle_position,
    particle_velocity,
    radius,
    block_live_count,
    cell_index,
    block_offset,
    neighbours,
    gas_velocity,
    pressure_source,
    void_before,
):
    wide, narrow = lax.axis_size("wide"), lax.axis_size("narrow")
    blocks, slots = radius.shape
    depth, lanes, width = pressure_source.shape
    width_y = lanes * narrow
    voids, layers = depth + 2 * HALO, depth + 2 * REACH
    half, coarse_y = depth // 2, width_y // 2
    slot_rows = -(-GROUPS * CAP // 8) * 8

    send, source = call(
        functools.partial(pack_kernel, wide),
        (f32s(wide, SOURCE_ROW + REACH * lanes, width), f32s(depth, lanes, width)),
        [SMEM, SMEM] + [VMEM] * 5,
        (VMEM, VMEM),
    )(block_offset, block_live_count, radius, particle_velocity, cell_index, pressure_source, void_before)
    recv = lax.all_to_all(send, "wide", 0, 0)

    contact = call(
        contact_kernel,
        f32s(3, blocks, slots),
        [SMEM, SMEM, VMEM, VMEM],
        VMEM,
        [pltpu.VMEM((4, blocks, slots, slots), F32)],
        flops=56 * 128 * 128 * 20,
    )(neighbours, block_live_count, particle_position, radius)

    window, rows = call(
        functools.partial(void_kernel, wide),
        (f32s(voids + layers, lanes, width), f32s(5, slot_rows, slots)),
        [VMEM] * 2,
        (VMEM, VMEM),
    )(recv, source)
    if narrow == 2:
        pieces = [window, lax.ppermute(window, "narrow", [(0, 1), (1, 0)])]
    else:
        every = lax.all_gather(window, "narrow")
        pieces = [every[i] for i in range(narrow)]

    fine = [
        pltpu.VMEM((voids, width_y, width), F32),
        pltpu.VMEM((layers, width_y, width), F32),
        pltpu.VMEM((6, layers, width_y, width), F32),
    ]
    plane = pltpu.VMEM((layers, width_y, width), F32)
    coarse = call(
        functools.partial(coarsen_kernel, wide),
        f32s(wide, half * coarse_y, width),
        [VMEM] * len(pieces),
        VMEM,
        fine + [plane, plane, plane, pltpu.VMEM((2, half * width_y, width), F32)],
    )(*pieces)
    gathered = lax.all_to_all(coarse, "wide", 0, 0)

    drag, base = call(
        drag_kernel,
        (f32s(3, slot_rows, slots), f32s(3, depth, lanes, width)),
        [VMEM] * 3,
        (VMEM, VMEM),
        flops=10_000_000,
    )(window, rows, gas_velocity)

    level_scratch = []
    for index in range(3):
        count = wide * half // 2 >> index
        body = pltpu.VMEM((count, coarse_y, width), F32)
        edged = pltpu.VMEM((count + 2, coarse_y, width), F32)
        level_scratch += [edged, body, pltpu.VMEM((6, count, coarse_y, width), F32), body, body, edged, edged]
    pressure, gas_next, returning = call(
        functools.partial(solve_kernel, wide),
        (f32s(depth, lanes, width), f32s(3, depth, lanes, width), f32s(wide, slot_rows, slots)),
        [VMEM] * (4 + len(pieces)),
        (VMEM, VMEM, VMEM),
        level_scratch
        + fine
        + [plane, plane, plane]
        + [
            pltpu.VMEM((layers // 2 * coarse_y, width), F32),
            pltpu.VMEM((layers // 2 * width_y, width), F32),
            pltpu.VMEM((3, depth, width_y, width), F32),
        ],
    )(gathered, rows, drag, base, *pieces)
    returned = lax.all_to_all(returning, "wide", 0, 0)

    updated = call(
        functools.partial(move_kernel, wide),
        f32s(3, blocks, slots),
        [SMEM, SMEM] + [VMEM] * 4,
        VMEM,
    )(block_offset, block_live_count, returned, contact, radius, particle_velocity)
    return (pressure, gas_next, updated)


def solution(mesh):
    placed = (
        P(None, ("wide", "narrow"), None),
        P(None, ("wide", "narrow"), None),
        P(("wide", "narrow"), None),
        P(("wide", "narrow")),
        P(("wide", "narrow"), None),
        P(("wide", "narrow")),
        P(("wide", "narrow"), None),
        P(None, "wide", "narrow", None),
        P("wide", "narrow", None),
        P("wide", "narrow", None),
    )
    return jax.shard_map(
        local,
        mesh=mesh,
        in_specs=placed,
        out_specs=(
            P("wide", "narrow", None),
            P(None, "wide", "narrow", None),
            P(None, ("wide", "narrow"), None),
        ),
        check_vma=False,
    )
```

time: 344 us -> 72.7 us (0.21)
  starting transfers between devices: 180 us -> 7.44 us
  local copies, waits for them, and re-layouts: 49.9 us -> 2.01 us
  other arithmetic: 47 us -> 0 us
  waiting for transfers between devices: 56.7 us -> 11.4 us
  Pallas kernels: 0 us -> 27 us
  blocking collectives: 4.38 us -> 23.5 us
    ppermute x70 -> x1, starting transfers between devices: 180 us -> 0.01 us  [local(): pieces = [window, lax.ppermute(window, 'narrow', [(0, 1), (1, 0)])]]
    ppermute x70 -> x1, waiting for transfers between devices: 56.7 us -> 1.57 us  [local(): pieces = [window, lax.ppermute(window, 'narrow', [(0, 1), (1, 0)])]]
    gather x23 -> x0, local copies, waits for them, and re-layouts: 34.5 us -> none  [the longest x1 10.4 us: local(): voidage[where_in] ** (-void_power)]
    scatter-add x2 -> x0, other arithmetic: 29.2 us -> none  [the longest x1 15.5 us: local(): jnp.zeros((3, total_cells), jnp.float32).at[:, where_in].add(-drag_force)]
    pallas_call x0 -> x7, Pallas kernels: none -> 27 us  [the longest x1 10.9 us: local(): call(functools.partial(solve_kernel, wide), (f32s(depth, lanes, width), f...]
    all_to_all x0 -> x1, blocking collectives: none -> 23.5 us  [local(): recv = lax.all_to_all(send, 'wide', 0, 0)]
    all_to_all x0 -> x2, waiting for transfers between devices: none -> 9.83 us  [the longest x1 7.37 us: local(): gathered = lax.all_to_all(coarse, 'wide', 0, 0)]
    reduce_sum x12 -> x0, other arithmetic: 9.21 us -> none  [the longest x3 7.31 us: pairwise_force(): jnp.sum(apart_z * weight, axis=2)]
  transfers between devices with their start and end apart: 70 -> 3, of which waited for: 19 -> 3; matrix products, arithmetic and copies ran while one was open for 19% -> 0% of each run, Pallas kernels for 0% -> 11%
where the time goes in v1:
time: 72.7 us; the launch traced here: 72.1 us
  Pallas kernels  27 us (37%)
  blocking collectives  23.5 us (32%)
  waiting for transfers between devices  11.4 us (16%)
  starting transfers between devices  7.44 us (10%)
  local copies, waits for them, and re-layouts  2.01 us (3%)
    all_to_all x1, blocking collectives, local(): recv = lax.all_to_all(send, 'wide', 0, 0)  23.5 us
    pallas_call x1, Pallas kernels, local(): call(functools.partial(solve_kernel, wide), (f32s(depth, lanes, width), f...  10.9 us
    all_to_all x1, waiting for transfers between devices, local(): gathered = lax.all_to_all(coarse, 'wide', 0, 0)  7.37 us
    pallas_call x1, Pallas kernels, local(): call(contact_kernel, f32s(3, blocks, slots), [SMEM, SMEM, VMEM, VMEM], VM...  5.34 us
    all_to_all x1, starting transfers between devices, local(): gathered = lax.all_to_all(coarse, 'wide', 0, 0)  3.9 us
    all_to_all x1, starting transfers between devices, local(): returned = lax.all_to_all(returning, 'wide', 0, 0)  3.54 us
    pallas_call x1, Pallas kernels, local(): call(drag_kernel, (f32s(3, slot_rows, slots), f32s(3, depth, lanes, width...  2.81 us
    all_to_all x1, waiting for transfers between devices, local(): returned = lax.all_to_all(returning, 'wide', 0, 0)  2.46 us
  transfers between devices with their start and end apart: 3, of which 3 were waited for; matrix products, arithmetic and copies ran while one was open for 0% of the time, Pallas kernels for 11%

profile of v1, /device:TPU:0, one launch (start us, length us, event | category | flops | bytes accessed | tf_op | source)
XLA Modules:
  0.0 72.1 jit_solution(5880668225056756416)
XLA Ops:
  0.6 1.8 %shard_map.121 = (f32[16,64,128]{2,1,0:T(8,128)}, f32[8,8,128]{2,1,0:T(8,128)}) custom-call(s32[8]{0:T(128)} %offset_ref.3, s32[8]{0:T(128)} %count_ref.5, f32[8,128]{1,0:T(8,128)} %radius_ref.5, f32[3,8,128]{2,1,0:T(8,128)} %vel_ref.3, s32[8,128]{1,0:T(8,128)} %cell_ref.1, f32[8,8,128]{2,1,0:T(8,128)} %source_ref.1, f32[8,8,128]{2,1,0:T(8,128)} %before_ref.1), custom_call_target="tpu_custom_call" | custom-call | bytes 262144 | tf_op jit(solution)/shard_map/pallas_call | solution.py:628
  2.4 23.5 %all_to_all.15.recv_ref = f32[16,64,128]{2,1,0:T(8,128)} all-to-all(f32[16,64,128]{2,1,0:T(8,128)} %get-tuple-element.12), channel_id=1, replica_groups=mesh['wide'=16,'narrow'=2] {'wide'}, dimensions={0} | all-to-all | bytes 1048576 | tf_op jit(solution)/shard_map/all_to_all | solution.py:634
  26.0 2.4 %shard_map.122 = (f32[34,8,128]{2,1,0:T(8,128)}, f32[5,16,128]{2,1,0:T(8,128)}) custom-call(f32[16,64,128]{2,1,0:T(8,128)} %all_to_all.15.recv_ref, f32[8,8,128]{2,1,0:T(8,128)} %get-tuple-element.13.s_ref), custom_call_target="tpu_custom_call" | custom-call | bytes 262144 | tf_op jit(solution)/shard_map/pallas_call | solution.py:645
  28.3 0.0 collective-permute-start
  28.3 1.6 %collective-permute-done.refs_1_ = f32[34,8,128]{2,1,0:T(8,128)S(1)} collective-permute-done((f32[34,8,128]{2,1,0:T(8,128)}, f32[34,8,128]{2,1,0:T(8,128)S(1)}, u32[]{:S(2)}, u32[]{:S(2)}) %collective-permute-start) | collective-permute-done | bytes 139296 | tf_op jit(solution)/shard_map/ppermute | solution.py:652
  29.9 0.0 copy-start.1
  29.9 0.7 copy-done.1
  30.6 2.3 %shard_map.123 = f32[16,32,128]{2,1,0:T(8,128)} custom-call(f32[34,8,128]{2,1,0:T(8,128)} %get-tuple-element.14.refs_0_.window_ref, f32[34,8,128]{2,1,0:T(8,128)} %copy-done.1), custom_call_target="tpu_custom_call" | custom-call | bytes 262144 | tf_op jit(solution)/shard_map/pallas_call | solution.py:663
  32.8 3.9 %all-to-all-start.1 = ((f32[16,32,128]{2,1,0:T(8,128)}), f32[16,32,128]{2,1,0:T(8,128)S(1)}, u32[]{:S(2)}, u32[]{:S(2)}) async-start(f32[16,32,128]{2,1,0:T(8,128)} %shard_map.123), calls=%async_computation.1 | async-start | bytes 524288 | tf_op jit(solution)/shard_map/all_to_all | solution.py:670
  36.8 2.8 %shard_map.124 = (f32[3,16,128]{2,1,0:T(8,128)}, f32[3,8,8,128]{3,2,1,0:T(8,128)}) custom-call(f32[34,8,128]{2,1,0:T(8,128)} %get-tuple-element.14.refs_0_.window_ref, f32[5,16,128]{2,1,0:T(8,128)} %get-tuple-element.15.rows_ref, f32[3,8,8,128]{3,2,1,0:T(8,128)} %gas_ref.1), custom_call_target="tpu_custom_call" | custom-call | flops 10000000 | bytes 262144 | tf_op jit(solution)/shard_map/pallas_call | solution.py:672
  39.6 7.4 %all-to-all-done.1.recv_ref = f32[16,32,128]{2,1,0:T(8,128)S(1)} async-done(((f32[16,32,128]{2,1,0:T(8,128)}), f32[16,32,128]{2,1,0:T(8,128)S(1)}, u32[]{:S(2)}, u32[]{:S(2)}) %all-to-all-start.1) | async-done | bytes 262176 | tf_op jit(solution)/shard_map/all_to_all | solution.py:670
  46.9 0.0 copy-start
  46.9 0.7 copy-done
  47.6 10.9 %shard_map.125 = (f32[8,8,128]{2,1,0:T(8,128)}, f32[3,8,8,128]{3,2,1,0:T(8,128)}, f32[16,16,128]{2,1,0:T(8,128)}) custom-call(f32[16,32,128]{2,1,0:T(8,128)} %copy-done, f32[5,16,128]{2,1,0:T(8,128)} %get-tuple-element.15.rows_ref, f32[3,16,128]{2,1,0:T(8,128)} %get-tuple-element.16.drag_ref, f32[3,8,8,128]{3,2,1,0:T(8,128)} %get-tuple-element.17.base_ref, ...), custom_call_target="tpu_custom_call" | custom-call | bytes 262144 | tf_op jit(solution)/shard_map/pallas_call | solution.py:686
  58.5 3.5 %all-to-all-start.2 = ((f32[16,16,128]{2,1,0:T(8,128)}), f32[16,16,128]{2,1,0:T(8,128)S(1)}, u32[]{:S(2)}, u32[]{:S(2)}) async-start(f32[16,16,128]{2,1,0:T(8,128)} %get-tuple-element.20), calls=%async_computation.2 | async-start | bytes 262144 | tf_op jit(solution)/shard_map/all_to_all | solution.py:700
  62.0 5.3 %shard_map.126.contact_ref = f32[3,8,128]{2,1,0:T(8,128)} custom-call(s32[8,6]{1,0:T(8,128)} %near_ref.1, s32[8]{0:T(128)} %count_ref.5, f32[3,8,128]{2,1,0:T(8,128)} %pos_ref.1, f32[8,128]{1,0:T(8,128)} %radius_ref.5), custom_call_target="tpu_custom_call" | custom-call | flops 18350080 | bytes 262144 | tf_op jit(solution)/shard_map/pallas_call | solution.py:636
  67.4 2.5 %all-to-all-done.2.recv_ref = f32[16,16,128]{2,1,0:T(8,128)S(1)} async-done(((f32[16,16,128]{2,1,0:T(8,128)}), f32[16,16,128]{2,1,0:T(8,128)S(1)}, u32[]{:S(2)}, u32[]{:S(2)}) %all-to-all-start.2) | async-done | bytes 131104 | tf_op jit(solution)/shard_map/all_to_all | solution.py:700
  69.8 0.0 copy-start.2
  69.8 0.6 copy-done.2
  70.5 1.6 %shard_map.127 = f32[3,8,128]{2,1,0:T(8,128)} custom-call(s32[8]{0:T(128)} %offset_ref.3, s32[8]{0:T(128)} %count_ref.5, f32[16,16,128]{2,1,0:T(8,128)} %copy-done.2, f32[3,8,128]{2,1,0:T(8,128)} %shard_map.126.contact_ref, f32[8,128]{1,0:T(8,128)} %radius_ref.5, f32[3,8,128]{2,1,0:T(8,128)} %vel_ref.3), custom_call_target="tpu_custom_call" | custom-call | bytes 262144 | tf_op jit(solution)/shard_map/pallas_call | solution.py:702
Async XLA Ops:
  28.3 1.6 %collective-permute-start = (f32[34,8,128]{2,1,0:T(8,128)}, f32[34,8,128]{2,1,0:T(8,128)S(1)}, u32[]{:S(2)}, u32[]{:S(2)}) collective-permute-start(f32[34,8,128]{2,1,0:T(8,128)} %get-tuple-element.14.refs_0_.window_ref), channel_id=1, source_target_pairs={{0,1},{1,0},{2,3},{3,2},{4,5},{5,4},{6,7},{7,6},{8,9},{9,8},{10,11... | collective-permute-start | bytes 417800 | tf_op jit(solution)/shard_map/ppermute | solution.py:652
  29.9 0.7 copy-start.1
  32.8 14.1 %all-to-all-start.1 = ((f32[16,32,128]{2,1,0:T(8,128)}), f32[16,32,128]{2,1,0:T(8,128)S(1)}, u32[]{:S(2)}, u32[]{:S(2)}) async-start(f32[16,32,128]{2,1,0:T(8,128)} %shard_map.123), calls=%async_computation.1 | async-start | bytes 524288 | tf_op jit(solution)/shard_map/all_to_all | solution.py:670
  46.9 0.7 copy-start
  58.5 11.3 %all-to-all-start.2 = ((f32[16,16,128]{2,1,0:T(8,128)}), f32[16,16,128]{2,1,0:T(8,128)S(1)}, u32[]{:S(2)}, u32[]{:S(2)}) async-start(f32[16,16,128]{2,1,0:T(8,128)} %get-tuple-element.20), calls=%async_computation.2 | async-start | bytes 262144 | tf_op jit(solution)/shard_map/all_to_all | solution.py:700
  69.8 0.6 copy-start.2

commit v2 on v1

--- a/solution.py
+++ b/solution.py
@@ -1,4 +1,5 @@
 import functools
+import math
 
 import jax
 import jax.numpy as jnp
@@ -35,20 +36,27 @@
 VOL_ROW = 0
 CELL_ROW = 3 * CAP
 VEL_ROW = 6 * CAP
-SOURCE_ROW = 32
-VMEM_LIMIT = 60 * 1024 * 1024
-
-
-def call(kernel, out_shape, in_specs, out_specs, scratch=(), flops=0):
-    return pl.pallas_call(
-        kernel,
-        out_shape=out_shape,
-        in_specs=in_specs,
-        out_specs=out_specs,
-        scratch_shapes=list(scratch),
-        compiler_params=pltpu.CompilerParams(vmem_limit_bytes=VMEM_LIMIT),
-        cost_estimate=pl.CostEstimate(flops=flops, bytes_accessed=1 << 18, transcendentals=0),
-    )
+SEND_ROWS = -(-9 * CAP // 8) * 8
+UNROLL = 32
+VMEM_SPARE = 4 * 1024 * 1024
+VMEM_MOST = 60 * 1024 * 1024
+
+
+def call(kernel, out_shape, in_specs, out_specs, scratch=(), flops=0, spare=VMEM_SPARE):
+    def run(*args):
+        held = [*args, *jax.tree.leaves(out_shape), *scratch]
+        need = sum(4 * math.prod(array.shape) for array in held)
+        return pl.pallas_call(
+            kernel,
+            out_shape=out_shape,
+            in_specs=in_specs,
+            out_specs=out_specs,
+            scratch_shapes=list(scratch),
+            compiler_params=pltpu.CompilerParams(vmem_limit_bytes=min(2 * need + spare, VMEM_MOST)),
+            cost_estimate=pl.CostEstimate(flops=flops, bytes_accessed=1 << 18, transcendentals=0),
+        )(*args)
+
+    return run
 
 
 def f32s(*shape):
@@ -78,7 +86,7 @@
     return offsets, found
 
 
-def pack_kernel(wide, offset_ref, count_ref, radius_ref, vel_ref, cell_ref, source_ref, before_ref, send_ref, s_ref):
+def pack_kernel(wide, offset_ref, count_ref, radius_ref, vel_ref, cell_ref, source_ref, before_ref, send_ref, s_ref, edge_ref, other_edge_ref):
     w = lax.axis_index("wide")
     blocks, slots = radius_ref.shape
     depth, lanes, _ = source_ref.shape
@@ -104,15 +112,10 @@
     for z in range(depth):
         s_ref[z] = source_ref[z] + before_ref[z] * (1.0 / step_duration)
 
-    @pl.when(w + 1 < wide)
-    def _():
+    for turn, ref in enumerate((edge_ref, other_edge_ref)):
+        upward = w % 2 == turn
         for z in range(REACH):
-            send_ref[w + 1, SOURCE_ROW + z * lanes : SOURCE_ROW + (z + 1) * lanes, :] = s_ref[depth - REACH + z]
-
-    @pl.when(w > 0)
-    def _():
-        for z in range(REACH):
-            send_ref[w - 1, SOURCE_ROW + z * lanes : SOURCE_ROW + (z + 1) * lanes, :] = s_ref[z]
+            ref[z] = jnp.where(upward, s_ref[depth - REACH + z], s_ref[z])
 
 
 def cell_rows(cell_row):
@@ -147,7 +150,7 @@
     return total[:rows] + total[rows:]
 
 
-def void_kernel(wide, recv_ref, s_ref, window_ref, rows_ref):
+def void_kernel(wide, recv_ref, edge_ref, other_edge_ref, s_ref, window_ref, rows_ref):
     w = lax.axis_index("wide")
     depth, lanes, _ = s_ref.shape
     cells = depth * lanes
@@ -189,9 +192,9 @@
     for e in (-1, 1):
         beside = w + e
         exists = jnp.logical_and(beside >= 0, beside < wide)
-        beside = jnp.clip(beside, 0, wide - 1)
+        turn = w % 2 == (0 if e > 0 else 1)
         for z in range(REACH):
-            part = recv_ref[beside, SOURCE_ROW + z * lanes : SOURCE_ROW + (z + 1) * lanes, :]
+            part = jnp.where(turn, edge_ref[z], other_edge_ref[z])
             at = voids + (z if e < 0 else REACH + depth + z)
             window_ref[at] = jnp.where(exists, part, 0.0)
 
@@ -348,7 +351,12 @@
         send_ref[t] = coarse
 
 
-def loop(count, body, unroll=4):
+def loop(count, body, size=1):
+    unroll = max(1, UNROLL // size)
+    if count <= unroll:
+        for i in range(count):
+            body(i)
+        return
     while count % unroll:
         unroll //= 2
 
@@ -371,9 +379,10 @@
     def __init__(self, index, refs):
         self.index = index
         self.step = 2 ** (index - 1)
-        self.porous, self.right, self.coef, self.diag, self.first, self.one, self.two = refs
+        self.porous, self.right, self.coef, self.diag, self.scale, self.first, self.one, self.two = refs
         self.layers, lanes, width = self.right.shape
         half = width // 2
+        self.size = -(-lanes // 8)
         y, x = iota((lanes, width), 0), iota((lanes, width), 1) % half
         self.first_half = iota((lanes, width), 1) < half
         self.masks = (y >= self.step, y < lanes - self.step, x >= self.step, x < half - self.step)
@@ -394,18 +403,17 @@
                     coef = jnp.where(self.masks[k - 2], coef, 0.0)
                 self.coef[k, i] = coef
             self.diag[i] = diag * (weight / relax_weight)
-
-        loop(self.layers, body)
+            self.scale[i] = inverse * (1.0 / weight)
+
+        loop(self.layers, body, self.size)
 
     def begin(self):
-        weight = 0.5 * 0.25**self.index
-
         def body(i):
-            value = self.right[i] / self.diag[i]
+            value = self.right[i] * self.scale[i]
             self.first[i] = value
             self.one[i + 1] = value
 
-        loop(self.layers, body)
+        loop(self.layers, body, self.size)
 
     def sweep(self):
         close_halves(self.one, self.first_half)
@@ -418,7 +426,7 @@
                 + pull(self.coef, i, self.one[i], here, self.one[i + 2], self.step, self.step)
             )
 
-        loop(self.layers, body)
+        loop(self.layers, body, self.size)
         self.one, self.two = self.two, self.one
 
     def residual(self, i):
@@ -453,7 +461,7 @@
         def body(i):
             under.right[i] = level.mean(level.residual(2 * i) + level.residual(2 * i + 1))
 
-        loop(under.layers, body)
+        loop(under.layers, body, level.size)
         coarse_cycle(levels, index + 1)
 
         def add(i):
@@ -461,16 +469,16 @@
             level.one[2 * i + 1] = level.one[2 * i + 1] + correction
             level.one[2 * i + 2] = level.one[2 * i + 2] + correction
 
-        loop(under.layers, add)
+        loop(under.layers, add, level.size)
         for _ in range(SWEEPS):
             level.sweep()
 
 
 def solve_kernel(wide, recv_ref, rows_ref, drag_ref, base_ref, *refs):
-    pieces, refs = refs[: len(refs) - 33], refs[len(refs) - 33 :]
+    pieces, refs = refs[: len(refs) - 36], refs[len(refs) - 36 :]
     pressure_ref, gas_ref, send_ref = refs[:3]
-    level_refs = [refs[3 + 7 * i : 10 + 7 * i] for i in range(3)]
-    void_ref, source_ref, coef_ref, first_ref, one_ref, two_ref, coarse_ref, fold_ref, slope_ref = refs[24:33]
+    level_refs = [refs[3 + 8 * i : 11 + 8 * i] for i in range(3)]
+    void_ref, source_ref, coef_ref, first_ref, one_ref, two_ref, coarse_ref, fold_ref, slope_ref = refs[27:36]
     narrow = len(pieces)
     lanes = pieces[0].shape[1]
     n = lax.axis_index("narrow")
@@ -491,13 +499,13 @@
             top.right[t * half + z] = jnp.where(top.first_half, low, pltpu.roll(high, middle, 1))
             top.porous[t * half + z + 1] = jnp.where(top.first_half, pltpu.roll(low, middle, 1), high)
 
-    loop(wide // 2, unpack)
+    loop(wide // 2, unpack, half * top.size)
     for upper, lower in ((levels[0], levels[1]), (levels[1], levels[2])):
 
         def narrow_down(i):
             lower.porous[i + 1] = upper.mean(upper.porous[2 * i + 1] + upper.porous[2 * i + 2])
 
-        loop(lower.layers, narrow_down)
+        loop(lower.layers, narrow_down, upper.size)
     for level in levels:
         level.start()
     coarse_cycle(levels, 0)
@@ -605,6 +613,11 @@
             out_ref[c, b : b + 1, :] = live * (vel_ref[c, b : b + 1, :] + step_duration * push)
 
 
+def pairs_of(count, turn):
+    lower = range(turn, count - 1, 2)
+    return [(i, i + 1) for i in lower] + [(i + 1, i) for i in lower]
+
+
 def local(
     particle_position,
     particle_velocity,
@@ -625,13 +638,15 @@
     half, coarse_y = depth // 2, width_y // 2
     slot_rows = -(-GROUPS * CAP // 8) * 8
 
-    send, source = call(
+    send, source, edge, other_edge = call(
         functools.partial(pack_kernel, wide),
-        (f32s(wide, SOURCE_ROW + REACH * lanes, width), f32s(depth, lanes, width)),
+        (f32s(wide, SEND_ROWS, width), f32s(depth, lanes, width), f32s(REACH, lanes, width), f32s(REACH, lanes, width)),
         [SMEM, SMEM] + [VMEM] * 5,
-        (VMEM, VMEM),
+        (VMEM,) * 4,
+        spare=VMEM_MOST,
     )(block_offset, block_live_count, radius, particle_velocity, cell_index, pressure_source, void_before)
     recv = lax.all_to_all(send, "wide", 0, 0)
+    edges = [lax.ppermute(part, "wide", pairs_of(wide, turn)) for turn, part in enumerate((edge, other_edge))]
 
     contact = call(
         contact_kernel,
@@ -645,9 +660,9 @@
     window, rows = call(
         functools.partial(void_kernel, wide),
         (f32s(voids + layers, lanes, width), f32s(5, slot_rows, slots)),
-        [VMEM] * 2,
+        [VMEM] * 4,
         (VMEM, VMEM),
-    )(recv, source)
+    )(recv, *edges, source)
     if narrow == 2:
         pieces = [window, lax.ppermute(window, "narrow", [(0, 1), (1, 0)])]
     else:
@@ -682,7 +697,8 @@
         count = wide * half // 2 >> index
         body = pltpu.VMEM((count, coarse_y, width), F32)
         edged = pltpu.VMEM((count + 2, coarse_y, width), F32)
-        level_scratch += [edged, body, pltpu.VMEM((6, count, coarse_y, width), F32), body, body, edged, edged]
+        level_scratch += [edged, body, pltpu.VMEM((6, count, coarse_y, width), F32), body, body, body, edged, edged]
+    gathered, contact = lax.optimization_barrier((gathered, contact))
     pressure, gas_next, returning = call(
         functools.partial(solve_kernel, wide),
         (f32s(depth, lanes, width), f32s(3, depth, lanes, width), f32s(wide, slot_rows, slots)),

time: 72.7 us -> 56.5 us (0.78)
  blocking collectives: 23.5 us -> 11.3 us
  Pallas kernels: 27 us -> 15.5 us
  starting transfers between devices: 7.44 us -> 15.5 us
  local copies, waits for them, and re-layouts: 2.01 us -> 0.04 us
  waiting for transfers between devices: 11.4 us -> 12.9 us
    all_to_all x1, blocking collectives: 23.5 us -> 11.3 us  [local(): returned = lax.all_to_all(returning, 'wide', 0, 0)]
    pallas_call x7, Pallas kernels: 27 us -> 15.5 us  [run(): pl.pallas_call(kernel, out_shape=out_shape, in_specs=in_specs, out_specs=...]
    all_to_all x1, starting transfers between devices: 3.54 us -> 8.45 us  [local(): recv = lax.all_to_all(send, 'wide', 0, 0)]
    all_to_all x1, waiting for transfers between devices: 7.37 us -> 4.33 us  [local(): gathered = lax.all_to_all(coarse, 'wide', 0, 0)]
    all_to_all x1, waiting for transfers between devices: 2.46 us -> 5.48 us  [local(): recv = lax.all_to_all(send, 'wide', 0, 0)]
    ppermute x0 -> x2, starting transfers between devices: none -> 2.64 us  [local(): lax.ppermute(part, 'wide', pairs_of(wide, turn))]
    unnamed x6 -> x20, local copies, waits for them, and re-layouts: 2.01 us -> 0.04 us
    ppermute x0 -> x2, waiting for transfers between devices: none -> 1.73 us  [local(): lax.ppermute(part, 'wide', pairs_of(wide, turn))]
  transfers between devices with their start and end apart: 3 -> 5, of which waited for: 3 -> 4; matrix products, arithmetic and copies ran while one was open for 0% -> 0% of each run, Pallas kernels for 11% -> 10%
where the time goes in v2:
time: 56.5 us; the launch traced here: 56 us
  Pallas kernels  15.5 us (27%)
  starting transfers between devices  15.5 us (27%)
  waiting for transfers between devices  12.9 us (23%)
  blocking collectives  11.3 us (20%)
  between operations  0.76 us (1%)
    pallas_call x7, Pallas kernels, run(): pl.pallas_call(kernel, out_shape=out_shape, in_specs=in_specs, out_specs=...  15.5 us
    all_to_all x1, blocking collectives, local(): returned = lax.all_to_all(returning, 'wide', 0, 0)  11.3 us
    all_to_all x1, starting transfers between devices, local(): recv = lax.all_to_all(send, 'wide', 0, 0)  8.45 us
    all_to_all x1, waiting for transfers between devices, local(): recv = lax.all_to_all(send, 'wide', 0, 0)  5.48 us
    all_to_all x1, starting transfers between devices, local(): gathered = lax.all_to_all(coarse, 'wide', 0, 0)  4.35 us
    all_to_all x1, waiting for transfers between devices, local(): gathered = lax.all_to_all(coarse, 'wide', 0, 0)  4.33 us
    ppermute x2, starting transfers between devices, local(): lax.ppermute(part, 'wide', pairs_of(wide, turn))  2.64 us
    ppermute x2, waiting for transfers between devices, local(): lax.ppermute(part, 'wide', pairs_of(wide, turn))  1.73 us
  transfers between devices with their start and end apart: 5, of which 4 were waited for; matrix products, arithmetic and copies ran while one was open for 0% of the time, Pallas kernels for 10%

profile of v2, /device:TPU:0, one launch (start us, length us, event | category | flops | bytes accessed | tf_op | source)
XLA Modules:
  0.0 56.0 jit_solution(6547626721833057183)
XLA Ops:
  0.6 1.7 %shard_map.121 = (f32[16,32,128]{2,1,0:T(8,128)}, f32[8,8,128]{2,1,0:T(8,128)}, f32[4,8,128]{2,1,0:T(8,128)}, f32[4,8,128]{2,1,0:T(8,128)}) custom-call(s32[8]{0:T(128)} %offset_ref.3, s32[8]{0:T(128)} %count_ref.5, f32[8,128]{1,0:T(8,128)} %radius_ref.5, f32[3,8,128]{2,1,0:T(8,128)} %vel_ref.3, s32[8,128]{1,0:T(8,128)} %cell_ref.1, ...), custom_call_target="tpu_custom_call" | custom-call | bytes 262144 | tf_op jit(solution)/shard_map/pallas_call | solution.py:49
  2.3 0.0 copy-start.9
  2.3 0.0 copy-start.8
  2.4 0.0 copy-start.2
  2.4 8.5 %all-to-all-start = ((f32[16,32,128]{2,1,0:T(8,128)}), f32[16,32,128]{2,1,0:T(8,128)S(1)}, u32[]{:S(2)}, u32[]{:S(2)}) async-start(f32[16,32,128]{2,1,0:T(8,128)} %get-tuple-element.16), calls=%async_computation | async-start | bytes 524288 | tf_op jit(solution)/shard_map/all_to_all | solution.py:648
  10.8 0.0 copy-done.9
  10.8 2.0 %collective-permute-start = (f32[4,8,128]{2,1,0:T(8,128)S(1)}, f32[4,8,128]{2,1,0:T(8,128)S(1)}, u32[]{:S(2)}, u32[]{:S(2)}) collective-permute-start(f32[4,8,128]{2,1,0:T(8,128)S(1)} %copy-done.9), channel_id=1, source_target_pairs={{0,2},{4,6},{8,10},{12,14},{16,18},{20,22},{24,26},{28,30},{2,0},{... | collective-permute-start | bytes 49160 | tf_op jit(solution)/shard_map/ppermute | solution.py:649
  12.8 0.0 copy-done.8
  12.8 0.7 %collective-permute-start.1 = (f32[4,8,128]{2,1,0:T(8,128)S(1)}, f32[4,8,128]{2,1,0:T(8,128)S(1)}, u32[]{:S(2)}, u32[]{:S(2)}) collective-permute-start(f32[4,8,128]{2,1,0:T(8,128)S(1)} %copy-done.8), channel_id=1, source_target_pairs={{2,4},{6,8},{10,12},{14,16},{18,20},{22,24},{26,28},{4,2},{8,6},{1... | collective-permute-start | bytes 49160 | tf_op jit(solution)/shard_map/ppermute | solution.py:649
  13.5 1.7 %collective-permute-done.edge_ref = f32[4,8,128]{2,1,0:T(8,128)S(1)} collective-permute-done((f32[4,8,128]{2,1,0:T(8,128)S(1)}, f32[4,8,128]{2,1,0:T(8,128)S(1)}, u32[]{:S(2)}, u32[]{:S(2)}) %collective-permute-start) | collective-permute-done | bytes 16416 | tf_op jit(solution)/shard_map/ppermute | solution.py:649
  15.2 0.0 collective-permute-done.1.other_edge_ref
  15.2 5.5 %all-to-all-done.recv_ref = f32[16,32,128]{2,1,0:T(8,128)S(1)} async-done(((f32[16,32,128]{2,1,0:T(8,128)}), f32[16,32,128]{2,1,0:T(8,128)S(1)}, u32[]{:S(2)}, u32[]{:S(2)}) %all-to-all-start) | async-done | bytes 262176 | tf_op jit(solution)/shard_map/all_to_all | solution.py:648
  20.7 0.0 copy-done.2
  20.7 0.7 %shard_map.122 = (f32[34,8,128]{2,1,0:T(8,128)S(1)}, f32[5,16,128]{2,1,0:T(8,128)S(1)}) custom-call(f32[16,32,128]{2,1,0:T(8,128)S(1)} %all-to-all-done.recv_ref, f32[4,8,128]{2,1,0:T(8,128)S(1)} %collective-permute-done.edge_ref, f32[4,8,128]{2,1,0:T(8,128)S(1)} %collective-permute-done.1.other_edge_ref, f32[8,8,128]{2,1,0:T(8,128)S(1)} %copy-done.2), custom_call_target="tpu_custom_call" | custom-call | bytes 262144 | tf_op jit(solution)/shard_map/pallas_call | solution.py:49
  21.4 0.1 collective-permute-start.2
  21.4 1.3 %collective-permute-done.2.refs_1_ = f32[34,8,128]{2,1,0:T(8,128)S(1)} collective-permute-done((f32[34,8,128]{2,1,0:T(8,128)S(1)}, f32[34,8,128]{2,1,0:T(8,128)S(1)}, u32[]{:S(2)}, u32[]{:S(2)}) %collective-permute-start.2) | collective-permute-done | bytes 139296 | tf_op jit(solution)/shard_map/ppermute | solution.py:667
  22.8 1.3 %shard_map.123 = f32[16,32,128]{2,1,0:T(8,128)} custom-call(f32[34,8,128]{2,1,0:T(8,128)S(1)} %get-tuple-element.20.refs_0_.window_ref, f32[34,8,128]{2,1,0:T(8,128)S(1)} %collective-permute-done.2.refs_1_), custom_call_target="tpu_custom_call" | custom-call | bytes 262144 | tf_op jit(solution)/shard_map/pallas_call | solution.py:49
  24.1 0.0 copy-start.3
  24.1 0.0 copy-start.5
  24.1 0.0 copy-start.6
  24.1 0.0 copy-start.7
  24.1 0.0 copy-start
  24.1 4.3 %all-to-all-start.1 = ((f32[16,32,128]{2,1,0:T(8,128)}), f32[16,32,128]{2,1,0:T(8,128)S(1)}, u32[]{:S(2)}, u32[]{:S(2)}) async-start(f32[16,32,128]{2,1,0:T(8,128)} %shard_map.123), calls=%async_computation.1 | async-start | bytes 524288 | tf_op jit(solution)/shard_map/all_to_all | solution.py:685
  28.5 0.0 copy-done.3
  28.5 0.0 copy-done.5
  28.5 0.0 copy-done.6
  28.5 0.0 copy-done.7
  28.5 4.6 %shard_map.124.contact_ref = f32[3,8,128]{2,1,0:T(8,128)S(1)} custom-call(s32[8,6]{1,0:T(8,128)S(1)} %copy-done.7, s32[8]{0:T(128)S(1)} %copy-done.5, f32[3,8,128]{2,1,0:T(8,128)S(1)} %copy-done.6, f32[8,128]{1,0:T(8,128)S(1)} %copy-done.3), custom_call_target="tpu_custom_call" | custom-call | flops 18350080 | bytes 262144 | tf_op jit(solution)/shard_map/pallas_call | solution.py:49
  33.1 0.0 copy-done
  33.1 1.2 %shard_map.125 = (f32[3,16,128]{2,1,0:T(8,128)S(1)}, f32[3,8,8,128]{3,2,1,0:T(8,128)S(1)}) custom-call(f32[34,8,128]{2,1,0:T(8,128)S(1)} %get-tuple-element.20.refs_0_.window_ref, f32[5,16,128]{2,1,0:T(8,128)S(1)} %get-tuple-element.22.rows_ref, f32[3,8,8,128]{3,2,1,0:T(8,128)S(1)} %copy-done), custom_call_target="tpu_custom_call" | custom-call | flops 10000000 | bytes 262144 | tf_op jit(solution)/shard_map/pallas_call | solution.py:49
  34.3 4.3 %all-to-all-done.1.recv_ref = f32[16,32,128]{2,1,0:T(8,128)S(1)} async-done(((f32[16,32,128]{2,1,0:T(8,128)}), f32[16,32,128]{2,1,0:T(8,128)S(1)}, u32[]{:S(2)}, u32[]{:S(2)}) %all-to-all-start.1) | async-done | bytes 262176 | tf_op jit(solution)/shard_map/all_to_all | solution.py:685
  38.6 4.8 %shard_map.126 = (f32[8,8,128]{2,1,0:T(8,128)}, f32[3,8,8,128]{3,2,1,0:T(8,128)}, f32[16,16,128]{2,1,0:T(8,128)S(1)}) custom-call(f32[16,32,128]{2,1,0:T(8,128)S(1)} %all-to-all-done.1.recv_ref, f32[5,16,128]{2,1,0:T(8,128)S(1)} %get-tuple-element.22.rows_ref, f32[3,16,128]{2,1,0:T(8,128)S(1)} %get-tuple-element.23.drag_ref, ...), custom_call_target="tpu_custom_call" | custom-call | bytes 262144 | tf_op jit(solution)/shard_map/pallas_call | solution.py:49
  43.5 0.0 copy-start.1
  43.5 0.0 copy-start.4
  43.5 11.3 %all_to_all.15.recv_ref = f32[16,16,128]{2,1,0:T(8,128)S(1)} all-to-all(f32[16,16,128]{2,1,0:T(8,128)S(1)} %get-tuple-element.27), channel_id=1, replica_groups=mesh['wide'=16,'narrow'=2] {'wide'}, dimensions={0} | all-to-all | bytes 262144 | tf_op jit(solution)/shard_map/all_to_all | solution.py:716
  54.7 0.0 copy-done.1
  54.7 0.0 copy-done.4
  54.8 1.2 %shard_map.127 = f32[3,8,128]{2,1,0:T(8,128)} custom-call(s32[8]{0:T(128)S(1)} %copy-done.4, s32[8]{0:T(128)S(1)} %copy-done.5, f32[16,16,128]{2,1,0:T(8,128)S(1)} %all_to_all.15.recv_ref, f32[3,8,128]{2,1,0:T(8,128)S(1)} %shard_map.124.contact_ref, f32[8,128]{1,0:T(8,128)S(1)} %copy-done.3, f32[3,8,128]{2,1,0:T(8,128)S(1)} %copy-done.1), custom_call_target="tpu_custom_call" | custom-call | bytes 262144 | tf_op jit(solution)/shard_map/pallas_call | solution.py:49
Async XLA Ops:
  2.3 8.5 %copy-start.9 = (f32[4,8,128]{2,1,0:T(8,128)S(1)}, f32[4,8,128]{2,1,0:T(8,128)}, u32[]{:S(2)}) copy-start(f32[4,8,128]{2,1,0:T(8,128)} %get-tuple-element.17) | copy-start | bytes 49156
  2.3 10.5 %copy-start.8 = (f32[4,8,128]{2,1,0:T(8,128)S(1)}, f32[4,8,128]{2,1,0:T(8,128)}, u32[]{:S(2)}) copy-start(f32[4,8,128]{2,1,0:T(8,128)} %get-tuple-element.18) | copy-start | bytes 49156
  2.4 18.3 %copy-start.2 = (f32[8,8,128]{2,1,0:T(8,128)S(1)}, f32[8,8,128]{2,1,0:T(8,128)}, u32[]{:S(2)}) copy-start(f32[8,8,128]{2,1,0:T(8,128)} %get-tuple-element.19.s_ref) | copy-start | bytes 98308
  2.4 18.3 %all-to-all-start = ((f32[16,32,128]{2,1,0:T(8,128)}), f32[16,32,128]{2,1,0:T(8,128)S(1)}, u32[]{:S(2)}, u32[]{:S(2)}) async-start(f32[16,32,128]{2,1,0:T(8,128)} %get-tuple-element.16), calls=%async_computation | async-start | bytes 524288 | tf_op jit(solution)/shard_map/all_to_all | solution.py:648
  10.8 4.4 %collective-permute-start = (f32[4,8,128]{2,1,0:T(8,128)S(1)}, f32[4,8,128]{2,1,0:T(8,128)S(1)}, u32[]{:S(2)}, u32[]{:S(2)}) collective-permute-start(f32[4,8,128]{2,1,0:T(8,128)S(1)} %copy-done.9), channel_id=1, source_target_pairs={{0,2},{4,6},{8,10},{12,14},{16,18},{20,22},{24,26},{28,30},{2,0},{... | collective-permute-start | bytes 49160 | tf_op jit(solution)/shard_map/ppermute | solution.py:649
  12.8 2.4 %collective-permute-start.1 = (f32[4,8,128]{2,1,0:T(8,128)S(1)}, f32[4,8,128]{2,1,0:T(8,128)S(1)}, u32[]{:S(2)}, u32[]{:S(2)}) collective-permute-start(f32[4,8,128]{2,1,0:T(8,128)S(1)} %copy-done.8), channel_id=1, source_target_pairs={{2,4},{6,8},{10,12},{14,16},{18,20},{22,24},{26,28},{4,2},{8,6},{1... | collective-permute-start | bytes 49160 | tf_op jit(solution)/shard_map/ppermute | solution.py:649
  21.4 1.4 %collective-permute-start.2 = (f32[34,8,128]{2,1,0:T(8,128)S(1)}, f32[34,8,128]{2,1,0:T(8,128)S(1)}, u32[]{:S(2)}, u32[]{:S(2)}) collective-permute-start(f32[34,8,128]{2,1,0:T(8,128)S(1)} %get-tuple-element.20.refs_0_.window_ref), channel_id=1, source_target_pairs={{0,1},{1,0},{2,3},{3,2},{4,5},{5,4},{6,7},{7,6},{8,9},{9,8},{10,11... | collective-permute-start | bytes 417800 | tf_op jit(solution)/shard_map/ppermute | solution.py:667
  24.1 4.4 %copy-start.3 = (f32[8,128]{1,0:T(8,128)S(1)}, f32[8,128]{1,0:T(8,128)}, u32[]{:S(2)}) copy-start(f32[8,128]{1,0:T(8,128)} %radius_ref.5) | copy-start | bytes 12292
  24.1 4.4 %copy-start.5 = (s32[8]{0:T(128)S(1)}, s32[8]{0:T(128)}, u32[]{:S(2)}) copy-start(s32[8]{0:T(128)} %count_ref.5) | copy-start | bytes 100
  24.1 4.4 %copy-start.6 = (f32[3,8,128]{2,1,0:T(8,128)S(1)}, f32[3,8,128]{2,1,0:T(8,128)}, u32[]{:S(2)}) copy-start(f32[3,8,128]{2,1,0:T(8,128)} %pos_ref.1) | copy-start | bytes 36868
  24.1 4.4 %copy-start.7 = (s32[8,6]{1,0:T(8,128)S(1)}, s32[8,6]{1,0:T(8,128)}, u32[]{:S(2)}) copy-start(s32[8,6]{1,0:T(8,128)} %near_ref.1) | copy-start | bytes 580
  24.1 9.0 %copy-start = (f32[3,8,8,128]{3,2,1,0:T(8,128)S(1)}, f32[3,8,8,128]{3,2,1,0:T(8,128)}, u32[]{:S(2)}) copy-start(f32[3,8,8,128]{3,2,1,0:T(8,128)} %gas_ref.1) | copy-start | bytes 294916
  24.1 14.5 %all-to-all-start.1 = ((f32[16,32,128]{2,1,0:T(8,128)}), f32[16,32,128]{2,1,0:T(8,128)S(1)}, u32[]{:S(2)}, u32[]{:S(2)}) async-start(f32[16,32,128]{2,1,0:T(8,128)} %shard_map.123), calls=%async_computation.1 | async-start | bytes 524288 | tf_op jit(solution)/shard_map/all_to_all | solution.py:685
  43.5 11.3 %copy-start.1 = (f32[3,8,128]{2,1,0:T(8,128)S(1)}, f32[3,8,128]{2,1,0:T(8,128)}, u32[]{:S(2)}) copy-start(f32[3,8,128]{2,1,0:T(8,128)} %vel_ref.3) | copy-start | bytes 36868
  43.5 11.3 %copy-start.4 = (s32[8]{0:T(128)S(1)}, s32[8]{0:T(128)}, u32[]{:S(2)}) copy-start(s32[8]{0:T(128)} %offset_ref.3) | copy-start | bytes 100

commit v3 on v2

--- a/solution.py
+++ b/solution.py
@@ -290,8 +290,7 @@
             if k >= 2:
                 coef = jnp.where(masks[k - 2], coef, 0.0)
             coef_ref[k, i] = coef
-        if diag_ref is not None:
-            diag_ref[i] = diag * (0.5 / relax_weight)
+        diag_ref[i] = diag * (0.5 / relax_weight)
         first_ref[i] = (source_ref[i] - p * (1.0 / step_duration)) * inverse * 2.0
 
 
@@ -320,7 +319,7 @@
 
 
 def coarsen_kernel(wide, *refs):
-    *pieces, send_ref, void_ref, source_ref, coef_ref, diag_ref, first_ref, next_ref, fold_ref = refs
+    *pieces, send_ref, coef_ref, first_ref, next_ref, void_ref, source_ref, diag_ref, fold_ref = refs
     narrow = len(pieces)
     lanes = pieces[0].shape[1]
     n = lax.axis_index("narrow")
@@ -329,7 +328,7 @@
     fine_start(void_ref, source_ref, coef_ref, diag_ref, first_ref)
     layers, width_y, width = source_ref.shape
     depth = layers - 2 * REACH
-    fine_sweep(coef_ref, first_ref, first_ref, next_ref, REACH - 1, layers - REACH + 1)
+    fine_sweep(coef_ref, first_ref, first_ref, next_ref, 1, layers - 1)
     half = depth // 2
     rows = half * width_y
     for k in range(half):
@@ -474,18 +473,14 @@
             level.sweep()
 
 
-def solve_kernel(wide, recv_ref, rows_ref, drag_ref, base_ref, *refs):
-    pieces, refs = refs[: len(refs) - 36], refs[len(refs) - 36 :]
-    pressure_ref, gas_ref, send_ref = refs[:3]
-    level_refs = [refs[3 + 8 * i : 11 + 8 * i] for i in range(3)]
-    void_ref, source_ref, coef_ref, first_ref, one_ref, two_ref, coarse_ref, fold_ref, slope_ref = refs[27:36]
-    narrow = len(pieces)
-    lanes = pieces[0].shape[1]
+def solve_kernel(wide, recv_ref, coef_ref, first_ref, start_ref, *refs):
+    pressure_ref, slope_ref = refs[:2]
+    level_refs = [refs[2 + 8 * i : 10 + 8 * i] for i in range(3)]
+    one_ref, two_ref, coarse_ref, fold_ref, tilt_ref = refs[26:]
     n = lax.axis_index("narrow")
     w = lax.axis_index("wide")
-    spots = [n, 1 - n] if narrow == 2 else list(range(narrow))
-    fill_window(pieces, spots, lanes, void_ref, source_ref)
-    layers, width_y, width = source_ref.shape
+    lanes = pressure_ref.shape[1]
+    layers, width_y, width = first_ref.shape
     depth = layers - 2 * REACH
     half, coarse_y = depth // 2, width_y // 2
     levels = [Level(i + 1, level_refs[i]) for i in range(3)]
@@ -510,8 +505,6 @@
         level.start()
     coarse_cycle(levels, 0)
 
-    fine_start(void_ref, source_ref, coef_ref, None, first_ref)
-    fine_sweep(coef_ref, first_ref, first_ref, one_ref, 1, layers - 1)
     total = top.layers
     spans = layers // 2
     for k in range(spans):
@@ -529,7 +522,7 @@
     for i in range(1, layers - 1):
         k = i // 2
         correction = fold_ref[k * width_y : (k + 1) * width_y, :]
-        one_ref[i] = one_ref[i] + jnp.where(void_ref[i + 1] > 0.0, correction, 0.0)
+        one_ref[i] = start_ref[i] + correction
     fine_sweep(coef_ref, first_ref, one_ref, two_ref, 2, layers - 2)
     fine_sweep(coef_ref, first_ref, two_ref, one_ref, 3, layers - 3)
 
@@ -539,17 +532,21 @@
         i = REACH + z
         here = one_ref[i]
         before_y, after_y, before_x, after_x = sides(here, masks, 1, 1)
-        slope_ref[0, z] = 0.5 * (one_ref[i + 1] - one_ref[i - 1])
-        slope_ref[1, z] = 0.5 * (after_y - before_y)
-        slope_ref[2, z] = 0.5 * (after_x - before_x)
+        tilt_ref[0, z] = 0.5 * (one_ref[i + 1] - one_ref[i - 1])
+        tilt_ref[1, z] = 0.5 * (after_y - before_y)
+        tilt_ref[2, z] = 0.5 * (after_x - before_x)
         pressure_ref[z] = one_ref[i, own, :]
         for c in range(3):
-            gas_ref[c, z] = base_ref[c, z] - (step_duration / gas_density) * slope_ref[c, z, own, :]
-
+            slope_ref[c, z] = tilt_ref[c, z, own, :]
+
+
+def force_kernel(wide, rows_ref, drag_ref, slope_ref, send_ref):
+    w = lax.axis_index("wide")
+    _, depth, lanes, _ = slope_ref.shape
     zy, x = cell_rows(rows_ref[1])
 
     def table(c):
-        return lambda row: slope_ref[c, row // lanes, pl.ds(n * lanes + row % lanes, 1), :]
+        return lambda row: slope_ref[c, row // lanes, row % lanes : row % lanes + 1, :]
 
     slopes = gather_cells([table(0), table(1), table(2)], zy, x, depth * lanes)
     forces = [drag_ref[c] - rows_ref[0] * slopes[c] for c in range(3)]
@@ -559,10 +556,18 @@
         @pl.when(jnp.logical_and(target >= 0, target < wide))
         def _():
             for c in range(3):
-                send_ref[target, c * CAP : (c + 1) * CAP, :] = forces[c][g * CAP : (g + 1) * CAP]
-
-
-def contact_kernel(near_ref, count_ref, pos_ref, radius_ref, force_ref, across_ref):
+                for r in range(CAP):
+                    at = (c * CAP + r) * 128
+                    send_ref[target, :, at : at + 128] = forces[c][g * CAP + r : g * CAP + r + 1]
+
+
+def finish_kernel(base_ref, pressure_ref, slope_ref, pressure_out_ref, gas_ref):
+    pressure_out_ref[...] = pressure_ref[...]
+    gas_ref[...] = base_ref[...] - (step_duration / gas_density) * slope_ref[...]
+
+
+def contact_kernel(wide, near_ref, count_ref, offset_ref, pos_ref, radius_ref, vel_ref, still_ref, push_ref, seat_ref, across_ref):
+    w = lax.axis_index("wide")
     blocks, slots = radius_ref.shape
     neighbours = near_ref.shape[1]
     slot = iota((1, slots), 1)
@@ -572,6 +577,7 @@
             row = pos_ref[q, b : b + 1, :] if q < 3 else radius
             across_ref[q, b] = jnp.broadcast_to(row, (slots, slots)).T
 
+    offsets, rank = ranks(offset_ref, blocks)
     factor = stiffness / (slots * (neighbours + 1))
     for b in range(blocks):
         mine = [jnp.broadcast_to(pos_ref[c, b : b + 1, :], (8, slots)) for c in range(3)]
@@ -590,27 +596,27 @@
                     sums[c] = sums[c] + apart[c] * weight
             return tuple(sums)
 
-        sums = lax.fori_loop(0, neighbours + 1, one, tuple(jnp.zeros((8, slots), F32) for _ in range(3)))
-        for c in range(3):
-            force_ref[c, b : b + 1, :] = jnp.sum(sums[c], axis=0, keepdims=True) * factor
-
-
-def move_kernel(wide, offset_ref, count_ref, recv_ref, contact_ref, radius_ref, vel_ref, out_ref):
-    w = lax.axis_index("wide")
-    blocks, slots = radius_ref.shape
-    offsets, rank = ranks(offset_ref, blocks)
-    slot = iota((1, slots), 1)
-    for b in range(blocks):
-        home = jnp.clip(w + offsets[b], 0, wide - 1)
         live = jnp.where(slot < count_ref[b], 1.0, 0.0)
         radius = radius_ref[b : b + 1, :]
         inverse = 1.0 / (particle_density * (radius * radius * radius))
+        sums = lax.fori_loop(0, neighbours + 1, one, tuple(jnp.zeros((8, slots), F32) for _ in range(3)))
         for c in range(3):
-            fluid = recv_ref[home, pl.ds(c * CAP + rank[b], 1), :]
-            push = (contact_ref[c, b : b + 1, :] + fluid) * inverse
+            force = jnp.sum(sums[c], axis=0, keepdims=True) * factor
+            push = force * inverse
             if c == 0:
                 push = push + gravity
-            out_ref[c, b : b + 1, :] = live * (vel_ref[c, b : b + 1, :] + step_duration * push)
+            still_ref[c, b : b + 1, :] = live * (vel_ref[c, b : b + 1, :] + step_duration * push)
+        push_ref[b : b + 1, :] = live * (step_duration * inverse)
+        seat_ref[0, b] = jnp.clip(w + offsets[b], 0, wide - 1)
+        seat_ref[1, b] = rank[b]
+
+
+def move_kernel(seat_ref, recv_ref, still_ref, push_ref, out_ref):
+    for b in range(push_ref.shape[0]):
+        for c in range(3):
+            start = pl.multiple_of((c * CAP + seat_ref[1, b]) * 128, 128)
+            fluid = recv_ref[seat_ref[0, b], :, pl.ds(start, 128)]
+            out_ref[c, b : b + 1, :] = still_ref[c, b : b + 1, :] + push_ref[b : b + 1, :] * fluid
 
 
 def pairs_of(count, turn):
@@ -648,14 +654,14 @@
     recv = lax.all_to_all(send, "wide", 0, 0)
     edges = [lax.ppermute(part, "wide", pairs_of(wide, turn)) for turn, part in enumerate((edge, other_edge))]
 
-    contact = call(
-        contact_kernel,
-        f32s(3, blocks, slots),
-        [SMEM, SMEM, VMEM, VMEM],
-        VMEM,
+    still, push, seat = call(
+        functools.partial(contact_kernel, wide),
+        (f32s(3, blocks, slots), f32s(blocks, slots), jax.ShapeDtypeStruct((2, blocks), jnp.int32)),
+        [SMEM, SMEM, SMEM, VMEM, VMEM, VMEM],
+        (VMEM, VMEM, SMEM),
         [pltpu.VMEM((4, blocks, slots, slots), F32)],
         flops=56 * 128 * 128 * 20,
-    )(neighbours, block_live_count, particle_position, radius)
+    )(neighbours, block_live_count, block_offset, particle_position, radius, particle_velocity)
 
     window, rows = call(
         functools.partial(void_kernel, wide),
@@ -669,18 +675,18 @@
         every = lax.all_gather(window, "narrow")
         pieces = [every[i] for i in range(narrow)]
 
-    fine = [
-        pltpu.VMEM((voids, width_y, width), F32),
-        pltpu.VMEM((layers, width_y, width), F32),
-        pltpu.VMEM((6, layers, width_y, width), F32),
-    ]
-    plane = pltpu.VMEM((layers, width_y, width), F32)
-    coarse = call(
+    plane = (layers, width_y, width)
+    coarse, coefs, first, iterate = call(
         functools.partial(coarsen_kernel, wide),
-        f32s(wide, half * coarse_y, width),
+        (f32s(wide, half * coarse_y, width), f32s(6, *plane), f32s(*plane), f32s(*plane)),
         [VMEM] * len(pieces),
-        VMEM,
-        fine + [plane, plane, plane, pltpu.VMEM((2, half * width_y, width), F32)],
+        (VMEM,) * 4,
+        [
+            pltpu.VMEM((voids, width_y, width), F32),
+            pltpu.VMEM(plane, F32),
+            pltpu.VMEM(plane, F32),
+            pltpu.VMEM((2, half * width_y, width), F32),
+        ],
     )(*pieces)
     gathered = lax.all_to_all(coarse, "wide", 0, 0)
 
@@ -698,29 +704,42 @@
         body = pltpu.VMEM((count, coarse_y, width), F32)
         edged = pltpu.VMEM((count + 2, coarse_y, width), F32)
         level_scratch += [edged, body, pltpu.VMEM((6, count, coarse_y, width), F32), body, body, body, edged, edged]
-    gathered, contact = lax.optimization_barrier((gathered, contact))
-    pressure, gas_next, returning = call(
+    gathered, still, push, seat = lax.optimization_barrier((gathered, still, push, seat))
+    pressure, slope = call(
         functools.partial(solve_kernel, wide),
-        (f32s(depth, lanes, width), f32s(3, depth, lanes, width), f32s(wide, slot_rows, slots)),
-        [VMEM] * (4 + len(pieces)),
-        (VMEM, VMEM, VMEM),
+        (f32s(depth, lanes, width), f32s(3, depth, lanes, width)),
+        [VMEM] * 4,
+        (VMEM,) * 2,
         level_scratch
-        + fine
-        + [plane, plane, plane]
+        + [pltpu.VMEM(plane, F32), pltpu.VMEM(plane, F32)]
         + [
             pltpu.VMEM((layers // 2 * coarse_y, width), F32),
             pltpu.VMEM((layers // 2 * width_y, width), F32),
             pltpu.VMEM((3, depth, width_y, width), F32),
         ],
-    )(gathered, rows, drag, base, *pieces)
+    )(gathered, coefs, first, iterate)
+    returning = call(
+        functools.partial(force_kernel, wide),
+        f32s(wide, 1, 3 * CAP * slots),
+        [VMEM] * 3,
+        VMEM,
+    )(rows, drag, slope)
     returned = lax.all_to_all(returning, "wide", 0, 0)
+    pressure, gas_next = call(
+        finish_kernel,
+        (f32s(depth, lanes, width), f32s(3, depth, lanes, width)),
+        [VMEM] * 3,
+        (VMEM,) * 2,
+        flops=5_000_000,
+    )(base, pressure, slope)
+    returned, pressure, gas_next = lax.optimization_barrier((returned, pressure, gas_next))
 
     updated = call(
-        functools.partial(move_kernel, wide),
+        move_kernel,
         f32s(3, blocks, slots),
-        [SMEM, SMEM] + [VMEM] * 4,
+        [SMEM] + [VMEM] * 3,
         VMEM,
-    )(block_offset, block_live_count, returned, contact, radius, particle_velocity)
+    )(seat, returned, still, push)
     return (pressure, gas_next, updated)
 
 

time: 56.5 us -> 54.6 us (0.966)
  blocking collectives: 11.3 us -> 0 us
  waiting for transfers between devices: 12.9 us -> 19.1 us
  starting transfers between devices: 15.5 us -> 19.1 us
    all_to_all x1 -> x0, blocking collectives: 11.3 us -> none  [local(): returned = lax.all_to_all(returning, 'wide', 0, 0)]
    all_to_all x0 -> x1, waiting for transfers between devices: none -> 6.9 us  [local(): returned = lax.all_to_all(returning, 'wide', 0, 0)]
    all_to_all x0 -> x1, starting transfers between devices: none -> 3.55 us  [local(): returned = lax.all_to_all(returning, 'wide', 0, 0)]
    all_to_all x1, waiting for transfers between devices: 4.33 us -> 3.66 us  [local(): gathered = lax.all_to_all(coarse, 'wide', 0, 0)]
    pallas_call x7 -> x9, Pallas kernels: 15.5 us -> 15.1 us  [run(): pl.pallas_call(kernel, out_shape=out_shape, in_specs=in_specs, out_specs=...]
  transfers between devices with their start and end apart: 5 -> 6, of which waited for: 4 -> 5; matrix products, arithmetic and copies ran while one was open for 0% -> 0% of each run, Pallas kernels for 10% -> 13%
where the time goes in v3:
time: 54.6 us; the launch traced here: 54.1 us
  starting transfers between devices  19.1 us (35%)
  waiting for transfers between devices  19.1 us (35%)
  Pallas kernels  15.1 us (28%)
  between operations  0.81 us (1%)
    pallas_call x9, Pallas kernels, run(): pl.pallas_call(kernel, out_shape=out_shape, in_specs=in_specs, out_specs=...  15.1 us
    all_to_all x1, starting transfers between devices, local(): recv = lax.all_to_all(send, 'wide', 0, 0)  8.45 us
    all_to_all x1, waiting for transfers between devices, local(): returned = lax.all_to_all(returning, 'wide', 0, 0)  6.9 us
    all_to_all x1, waiting for transfers between devices, local(): recv = lax.all_to_all(send, 'wide', 0, 0)  5.48 us
    all_to_all x1, starting transfers between devices, local(): gathered = lax.all_to_all(coarse, 'wide', 0, 0)  4.35 us
    all_to_all x1, waiting for transfers between devices, local(): gathered = lax.all_to_all(coarse, 'wide', 0, 0)  3.66 us
    all_to_all x1, starting transfers between devices, local(): returned = lax.all_to_all(returning, 'wide', 0, 0)  3.55 us
    ppermute x2, starting transfers between devices, local(): lax.ppermute(part, 'wide', pairs_of(wide, turn))  2.64 us
  transfers between devices with their start and end apart: 6, of which 5 were waited for; matrix products, arithmetic and copies ran while one was open for 0% of the time, Pallas kernels for 13%

profile of v3, /device:TPU:0, one launch (start us, length us, event | category | flops | bytes accessed | tf_op | source)
XLA Modules:
  0.0 54.1 jit_solution(806797915888907850)
XLA Ops:
  0.6 1.7 %shard_map.121 = (f32[16,32,128]{2,1,0:T(8,128)}, f32[8,8,128]{2,1,0:T(8,128)}, f32[4,8,128]{2,1,0:T(8,128)}, f32[4,8,128]{2,1,0:T(8,128)}) custom-call(s32[8]{0:T(128)} %offset_ref.3, s32[8]{0:T(128)} %count_ref.3, f32[8,128]{1,0:T(8,128)} %radius_ref.3, f32[3,8,128]{2,1,0:T(8,128)} %vel_ref.3, s32[8,128]{1,0:T(8,128)} %cell_ref.1, ...), custom_call_target="tpu_custom_call" | custom-call | bytes 262144 | tf_op jit(solution)/shard_map/pallas_call | solution.py:49
  2.3 0.0 copy-start.9
  2.3 0.0 copy-start.8
  2.4 0.0 copy-start.1
  2.4 8.5 %all-to-all-start = ((f32[16,32,128]{2,1,0:T(8,128)}), f32[16,32,128]{2,1,0:T(8,128)S(1)}, u32[]{:S(2)}, u32[]{:S(2)}) async-start(f32[16,32,128]{2,1,0:T(8,128)} %get-tuple-element.29), calls=%async_computation | async-start | bytes 524288 | tf_op jit(solution)/shard_map/all_to_all | solution.py:654
  10.8 0.0 copy-done.9
  10.8 2.0 %collective-permute-start = (f32[4,8,128]{2,1,0:T(8,128)S(1)}, f32[4,8,128]{2,1,0:T(8,128)S(1)}, u32[]{:S(2)}, u32[]{:S(2)}) collective-permute-start(f32[4,8,128]{2,1,0:T(8,128)S(1)} %copy-done.9), channel_id=1, source_target_pairs={{0,2},{4,6},{8,10},{12,14},{16,18},{20,22},{24,26},{28,30},{2,0},{... | collective-permute-start | bytes 49160 | tf_op jit(solution)/shard_map/ppermute | solution.py:655
  12.8 0.0 copy-done.8
  12.8 0.7 %collective-permute-start.1 = (f32[4,8,128]{2,1,0:T(8,128)S(1)}, f32[4,8,128]{2,1,0:T(8,128)S(1)}, u32[]{:S(2)}, u32[]{:S(2)}) collective-permute-start(f32[4,8,128]{2,1,0:T(8,128)S(1)} %copy-done.8), channel_id=1, source_target_pairs={{2,4},{6,8},{10,12},{14,16},{18,20},{22,24},{26,28},{4,2},{8,6},{1... | collective-permute-start | bytes 49160 | tf_op jit(solution)/shard_map/ppermute | solution.py:655
  13.5 1.7 %collective-permute-done.edge_ref = f32[4,8,128]{2,1,0:T(8,128)S(1)} collective-permute-done((f32[4,8,128]{2,1,0:T(8,128)S(1)}, f32[4,8,128]{2,1,0:T(8,128)S(1)}, u32[]{:S(2)}, u32[]{:S(2)}) %collective-permute-start) | collective-permute-done | bytes 16416 | tf_op jit(solution)/shard_map/ppermute | solution.py:655
  15.2 0.0 collective-permute-done.1.other_edge_ref
  15.2 5.5 %all-to-all-done.recv_ref = f32[16,32,128]{2,1,0:T(8,128)S(1)} async-done(((f32[16,32,128]{2,1,0:T(8,128)}), f32[16,32,128]{2,1,0:T(8,128)S(1)}, u32[]{:S(2)}, u32[]{:S(2)}) %all-to-all-start) | async-done | bytes 262176 | tf_op jit(solution)/shard_map/all_to_all | solution.py:654
  20.7 0.0 copy-done.1
  20.7 0.7 %shard_map.122 = (f32[34,8,128]{2,1,0:T(8,128)S(1)}, f32[5,16,128]{2,1,0:T(8,128)S(1)}) custom-call(f32[16,32,128]{2,1,0:T(8,128)S(1)} %all-to-all-done.recv_ref, f32[4,8,128]{2,1,0:T(8,128)S(1)} %collective-permute-done.edge_ref, f32[4,8,128]{2,1,0:T(8,128)S(1)} %collective-permute-done.1.other_edge_ref, f32[8,8,128]{2,1,0:T(8,128)S(1)} %copy-done.1), custom_call_target="tpu_custom_call" | custom-call | bytes 262144 | tf_op jit(solution)/shard_map/pallas_call | solution.py:49
  21.4 0.1 collective-permute-start.2
  21.4 1.3 %collective-permute-done.2.refs_1_ = f32[34,8,128]{2,1,0:T(8,128)S(1)} collective-permute-done((f32[34,8,128]{2,1,0:T(8,128)S(1)}, f32[34,8,128]{2,1,0:T(8,128)S(1)}, u32[]{:S(2)}, u32[]{:S(2)}) %collective-permute-start.2) | collective-permute-done | bytes 139296 | tf_op jit(solution)/shard_map/ppermute | solution.py:673
  22.8 1.3 %shard_map.124 = (f32[16,32,128]{2,1,0:T(8,128)}, f32[6,16,16,128]{3,2,1,0:T(8,128)S(1)}, f32[16,16,128]{2,1,0:T(8,128)S(1)}, f32[16,16,128]{2,1,0:T(8,128)S(1)}) custom-call(f32[34,8,128]{2,1,0:T(8,128)S(1)} %get-tuple-element.34.window_ref.refs_0_, f32[34,8,128]{2,1,0:T(8,128)S(1)} %collective-permute-done.2.refs_1_), custom_call_target="tpu_custom_call" | custom-call | bytes 262144 | tf_op jit(solution)/shard_map/pallas_call | solution.py:49
  24.1 0.0 copy-start.2
  24.1 0.0 copy-start.3
  24.1 0.0 copy-start.4
  24.1 0.0 copy-start.5
  24.1 0.0 copy-start.6
  24.1 0.0 copy-start.7
  24.1 0.0 copy-start
  24.1 4.4 %all-to-all-start.1 = ((f32[16,32,128]{2,1,0:T(8,128)}), f32[16,32,128]{2,1,0:T(8,128)S(1)}, u32[]{:S(2)}, u32[]{:S(2)}) async-start(f32[16,32,128]{2,1,0:T(8,128)} %get-tuple-element.36), calls=%async_computation.1 | async-start | bytes 524288 | tf_op jit(solution)/shard_map/all_to_all | solution.py:691
  28.5 0.0 copy-done.2
  28.5 0.0 copy-done.3
  28.5 0.0 copy-done.4
  28.5 0.0 copy-done.5
  28.5 0.0 copy-done.6
  28.5 0.0 copy-done.7
  28.6 5.2 %shard_map.125 = (f32[3,8,128]{2,1,0:T(8,128)S(1)}, f32[8,128]{1,0:T(8,128)S(1)}, s32[2,8]{1,0:T(2,128)S(1)}) custom-call(s32[8,6]{1,0:T(8,128)S(1)} %copy-done.7, s32[8]{0:T(128)S(1)} %copy-done.5, s32[8]{0:T(128)S(1)} %copy-done.4, f32[3,8,128]{2,1,0:T(8,128)S(1)} %copy-done.6, f32[8,128]{1,0:T(8,128)S(1)} %copy-done.3, f32[3,8,128]{2,1,0:T(8,128)S(1)} %copy-done.2), custom_call_target="tpu_custom_call" | custom-call | flops 18350080 | bytes 262144 | tf_op jit(solution)/shard_map/pallas_call | solution.py:49
  33.8 0.0 copy-done
  33.8 1.2 %shard_map.123 = (f32[3,16,128]{2,1,0:T(8,128)S(1)}, f32[3,8,8,128]{3,2,1,0:T(8,128)S(1)}) custom-call(f32[34,8,128]{2,1,0:T(8,128)S(1)} %get-tuple-element.34.window_ref.refs_0_, f32[5,16,128]{2,1,0:T(8,128)S(1)} %get-tuple-element.33.rows_ref, f32[3,8,8,128]{3,2,1,0:T(8,128)S(1)} %copy-done), custom_call_target="tpu_custom_call" | custom-call | flops 10000000 | bytes 262144 | tf_op jit(solution)/shard_map/pallas_call | solution.py:49
  35.0 3.7 %all-to-all-done.1.recv_ref = f32[16,32,128]{2,1,0:T(8,128)S(1)} async-done(((f32[16,32,128]{2,1,0:T(8,128)}), f32[16,32,128]{2,1,0:T(8,128)S(1)}, u32[]{:S(2)}, u32[]{:S(2)}) %all-to-all-start.1) | async-done | bytes 262176 | tf_op jit(solution)/shard_map/all_to_all | solution.py:691
  38.7 2.0 %shard_map.126 = (f32[8,8,128]{2,1,0:T(8,128)S(1)}, f32[3,8,8,128]{3,2,1,0:T(8,128)S(1)}) custom-call(f32[16,32,128]{2,1,0:T(8,128)S(1)} %all-to-all-done.1.recv_ref, f32[6,16,16,128]{3,2,1,0:T(8,128)S(1)} %get-tuple-element.41.coef_ref, f32[16,16,128]{2,1,0:T(8,128)S(1)} %get-tuple-element.42.first_ref, f32[16,16,128]{2,1,0:T(8,128)S(1)} %get-tuple-element.43.start_ref), custom_call_target="tpu_custom_call" | custom-call | bytes 262144 | tf_op jit(solution)/shard_map/pallas_call | solution.py:49
  40.6 1.1 %shard_map.127 = f32[16,1,1152]{2,1,0:T(1,128)} custom-call(f32[5,16,128]{2,1,0:T(8,128)S(1)} %get-tuple-element.33.rows_ref, f32[3,16,128]{2,1,0:T(8,128)S(1)} %get-tuple-element.35.drag_ref, f32[3,8,8,128]{3,2,1,0:T(8,128)S(1)} %get-tuple-element.44.slope_ref), custom_call_target="tpu_custom_call" | custom-call | bytes 262144 | tf_op jit(solution)/shard_map/pallas_call | solution.py:49
  41.8 3.5 %all-to-all-start.2 = ((f32[16,1,1152]{2,1,0:T(1,128)}), f32[16,1,1152]{2,1,0:T(1,128)S(1)}, u32[]{:S(2)}, u32[]{:S(2)}) async-start(f32[16,1,1152]{2,1,0:T(1,128)} %shard_map.127), calls=%async_computation.2 | async-start | bytes 147456 | tf_op jit(solution)/shard_map/all_to_all | solution.py:727
  45.3 0.7 %shard_map.128 = (f32[8,8,128]{2,1,0:T(8,128)}, f32[3,8,8,128]{3,2,1,0:T(8,128)}) custom-call(f32[3,8,8,128]{3,2,1,0:T(8,128)S(1)} %get-tuple-element.45.base_ref, f32[8,8,128]{2,1,0:T(8,128)S(1)} %get-tuple-element.46.pressure_ref, f32[3,8,8,128]{3,2,1,0:T(8,128)S(1)} %get-tuple-element.44.slope_ref), custom_call_target="tpu_custom_call" | custom-call | flops 5000000 | bytes 262144 | tf_op jit(solution)/shard_map/pallas_call | solution.py:49
  46.0 6.9 %all-to-all-done.2.recv_ref = f32[16,1,1152]{2,1,0:T(1,128)S(1)} async-done(((f32[16,1,1152]{2,1,0:T(1,128)}), f32[16,1,1152]{2,1,0:T(1,128)S(1)}, u32[]{:S(2)}, u32[]{:S(2)}) %all-to-all-start.2) | async-done | bytes 73760 | tf_op jit(solution)/shard_map/all_to_all | solution.py:727
  52.9 1.2 %shard_map.129 = f32[3,8,128]{2,1,0:T(8,128)} custom-call(s32[2,8]{1,0:T(2,128)S(1)} %get-tuple-element.51.seat_ref, f32[16,1,1152]{2,1,0:T(1,128)S(1)} %all-to-all-done.2.recv_ref, f32[3,8,128]{2,1,0:T(8,128)S(1)} %get-tuple-element.53.still_ref, f32[8,128]{1,0:T(8,128)S(1)} %get-tuple-element.54.push_ref), custom_call_target="tpu_custom_call" | custom-call | bytes 262144 | tf_op jit(solution)/shard_map/pallas_call | solution.py:49
Async XLA Ops:
  2.3 8.5 %copy-start.9 = (f32[4,8,128]{2,1,0:T(8,128)S(1)}, f32[4,8,128]{2,1,0:T(8,128)}, u32[]{:S(2)}) copy-start(f32[4,8,128]{2,1,0:T(8,128)} %get-tuple-element.30) | copy-start | bytes 49156
  2.3 10.5 %copy-start.8 = (f32[4,8,128]{2,1,0:T(8,128)S(1)}, f32[4,8,128]{2,1,0:T(8,128)}, u32[]{:S(2)}) copy-start(f32[4,8,128]{2,1,0:T(8,128)} %get-tuple-element.31) | copy-start | bytes 49156
  2.4 18.3 %copy-start.1 = (f32[8,8,128]{2,1,0:T(8,128)S(1)}, f32[8,8,128]{2,1,0:T(8,128)}, u32[]{:S(2)}) copy-start(f32[8,8,128]{2,1,0:T(8,128)} %get-tuple-element.32.s_ref) | copy-start | bytes 98308
  2.4 18.3 %all-to-all-start = ((f32[16,32,128]{2,1,0:T(8,128)}), f32[16,32,128]{2,1,0:T(8,128)S(1)}, u32[]{:S(2)}, u32[]{:S(2)}) async-start(f32[16,32,128]{2,1,0:T(8,128)} %get-tuple-element.29), calls=%async_computation | async-start | bytes 524288 | tf_op jit(solution)/shard_map/all_to_all | solution.py:654
  10.8 4.4 %collective-permute-start = (f32[4,8,128]{2,1,0:T(8,128)S(1)}, f32[4,8,128]{2,1,0:T(8,128)S(1)}, u32[]{:S(2)}, u32[]{:S(2)}) collective-permute-start(f32[4,8,128]{2,1,0:T(8,128)S(1)} %copy-done.9), channel_id=1, source_target_pairs={{0,2},{4,6},{8,10},{12,14},{16,18},{20,22},{24,26},{28,30},{2,0},{... | collective-permute-start | bytes 49160 | tf_op jit(solution)/shard_map/ppermute | solution.py:655
  12.8 2.4 %collective-permute-start.1 = (f32[4,8,128]{2,1,0:T(8,128)S(1)}, f32[4,8,128]{2,1,0:T(8,128)S(1)}, u32[]{:S(2)}, u32[]{:S(2)}) collective-permute-start(f32[4,8,128]{2,1,0:T(8,128)S(1)} %copy-done.8), channel_id=1, source_target_pairs={{2,4},{6,8},{10,12},{14,16},{18,20},{22,24},{26,28},{4,2},{8,6},{1... | collective-permute-start | bytes 49160 | tf_op jit(solution)/shard_map/ppermute | solution.py:655
  21.4 1.4 %collective-permute-start.2 = (f32[34,8,128]{2,1,0:T(8,128)S(1)}, f32[34,8,128]{2,1,0:T(8,128)S(1)}, u32[]{:S(2)}, u32[]{:S(2)}) collective-permute-start(f32[34,8,128]{2,1,0:T(8,128)S(1)} %get-tuple-element.34.window_ref.refs_0_), channel_id=1, source_target_pairs={{0,1},{1,0},{2,3},{3,2},{4,5},{5,4},{6,7},{7,6},{8,9},{9,8},{10,11... | collective-permute-start | bytes 417800 | tf_op jit(solution)/shard_map/ppermute | solution.py:673
  24.1 4.4 %copy-start.2 = (f32[3,8,128]{2,1,0:T(8,128)S(1)}, f32[3,8,128]{2,1,0:T(8,128)}, u32[]{:S(2)}) copy-start(f32[3,8,128]{2,1,0:T(8,128)} %vel_ref.3) | copy-start | bytes 36868
  24.1 4.4 %copy-start.3 = (f32[8,128]{1,0:T(8,128)S(1)}, f32[8,128]{1,0:T(8,128)}, u32[]{:S(2)}) copy-start(f32[8,128]{1,0:T(8,128)} %radius_ref.3) | copy-start | bytes 12292
  24.1 4.4 %copy-start.4 = (s32[8]{0:T(128)S(1)}, s32[8]{0:T(128)}, u32[]{:S(2)}) copy-start(s32[8]{0:T(128)} %offset_ref.3) | copy-start | bytes 100
  24.1 4.4 %copy-start.5 = (s32[8]{0:T(128)S(1)}, s32[8]{0:T(128)}, u32[]{:S(2)}) copy-start(s32[8]{0:T(128)} %count_ref.3) | copy-start | bytes 100
  24.1 4.4 %copy-start.6 = (f32[3,8,128]{2,1,0:T(8,128)S(1)}, f32[3,8,128]{2,1,0:T(8,128)}, u32[]{:S(2)}) copy-start(f32[3,8,128]{2,1,0:T(8,128)} %pos_ref.1) | copy-start | bytes 36868
  24.1 4.4 %copy-start.7 = (s32[8,6]{1,0:T(8,128)S(1)}, s32[8,6]{1,0:T(8,128)}, u32[]{:S(2)}) copy-start(s32[8,6]{1,0:T(8,128)} %near_ref.1) | copy-start | bytes 580
  24.1 9.7 %copy-start = (f32[3,8,8,128]{3,2,1,0:T(8,128)S(1)}, f32[3,8,8,128]{3,2,1,0:T(8,128)}, u32[]{:S(2)}) copy-start(f32[3,8,8,128]{3,2,1,0:T(8,128)} %gas_ref.1) | copy-start | bytes 294916
  24.1 14.5 %all-to-all-start.1 = ((f32[16,32,128]{2,1,0:T(8,128)}), f32[16,32,128]{2,1,0:T(8,128)S(1)}, u32[]{:S(2)}, u32[]{:S(2)}) async-start(f32[16,32,128]{2,1,0:T(8,128)} %get-tuple-element.36), calls=%async_computation.1 | async-start | bytes 524288 | tf_op jit(solution)/shard_map/all_to_all | solution.py:691
  41.8 11.1 %all-to-all-start.2 = ((f32[16,1,1152]{2,1,0:T(1,128)}), f32[16,1,1152]{2,1,0:T(1,128)S(1)}, u32[]{:S(2)}, u32[]{:S(2)}) async-start(f32[16,1,1152]{2,1,0:T(1,128)} %shard_map.127), calls=%async_computation.2 | async-start | bytes 147456 | tf_op jit(solution)/shard_map/all_to_all | solution.py:727

commit v4 on v3

--- a/solution.py
+++ b/solution.py
@@ -346,8 +346,14 @@
     porous = fold_ref[1, pl.ds(0, rows // 2, stride=2), :] + fold_ref[1, pl.ds(1, rows // 2, stride=2), :]
     coarse = jnp.dot(right, mean_matrix(width, 0), precision=HIGHEST, preferred_element_type=F32)
     coarse = coarse + jnp.dot(porous, mean_matrix(width, width // 2), precision=HIGHEST, preferred_element_type=F32)
-    for t in range(wide):
-        send_ref[t] = coarse
+    coarse_y, part_y = width_y // 2, lanes // 2
+    for k in range(half):
+        part = coarse[k * coarse_y : k * coarse_y + part_y]
+        for i in range(1, narrow):
+            start = k * coarse_y + i * part_y
+            part = jnp.where(n == i, coarse[start : start + part_y], part)
+        for t in range(wide):
+            send_ref[t, k * part_y : (k + 1) * part_y, :] = part
 
 
 def loop(count, body, size=1):
@@ -473,7 +479,8 @@
             level.sweep()
 
 
-def solve_kernel(wide, recv_ref, coef_ref, first_ref, start_ref, *refs):
+def solve_kernel(wide, narrow, *refs):
+    part_refs, (coef_ref, first_ref, start_ref), refs = refs[:narrow], refs[narrow : narrow + 3], refs[narrow + 3 :]
     pressure_ref, slope_ref = refs[:2]
     level_refs = [refs[2 + 8 * i : 10 + 8 * i] for i in range(3)]
     one_ref, two_ref, coarse_ref, fold_ref, tilt_ref = refs[26:]
@@ -487,10 +494,17 @@
     top = levels[0]
     middle = width // 2
 
+    part_y = coarse_y // narrow
+
+    def whole(t, z):
+        parts = [ref[t, z * part_y : (z + 1) * part_y, :] for ref in part_refs]
+        if narrow == 2:
+            parts = [jnp.where(n == 0, parts[0], parts[1]), jnp.where(n == 0, parts[1], parts[0])]
+        return jnp.concatenate(parts, axis=0)
+
     def unpack(t):
         for z in range(half):
-            low = recv_ref[t, pl.ds(z * coarse_y, coarse_y), :]
-            high = recv_ref[t + wide // 2, pl.ds(z * coarse_y, coarse_y), :]
+            low, high = whole(t, z), whole(t + wide // 2, z)
             top.right[t * half + z] = jnp.where(top.first_half, low, pltpu.roll(high, middle, 1))
             top.porous[t * half + z + 1] = jnp.where(top.first_half, pltpu.roll(low, middle, 1), high)
 
@@ -566,20 +580,22 @@
     gas_ref[...] = base_ref[...] - (step_duration / gas_density) * slope_ref[...]
 
 
-def contact_kernel(wide, near_ref, count_ref, offset_ref, pos_ref, radius_ref, vel_ref, still_ref, push_ref, seat_ref, across_ref):
+def contact_kernel(wide, chosen, near_ref, count_ref, offset_ref, pos_ref, radius_ref, vel_ref, seat_ref, still_ref, push_ref, across_ref):
     w = lax.axis_index("wide")
     blocks, slots = radius_ref.shape
     neighbours = near_ref.shape[1]
     slot = iota((1, slots), 1)
-    for b in range(blocks):
-        radius = jnp.where(slot < count_ref[b], radius_ref[b : b + 1, :], -100.0)
-        for q in range(4):
-            row = pos_ref[q, b : b + 1, :] if q < 3 else radius
-            across_ref[q, b] = jnp.broadcast_to(row, (slots, slots)).T
+    reach = [jnp.where(slot < count_ref[b], radius_ref[b : b + 1, :], -100.0) for b in range(blocks)]
+    upright = jnp.concatenate([pos_ref[0], pos_ref[1], pos_ref[2]] + reach, axis=0).T
+    for q in range(4):
+        for b in range(blocks):
+            at = q * blocks + b
+            across_ref[q, b] = jnp.broadcast_to(upright[:, at : at + 1], (slots, slots))
 
     offsets, rank = ranks(offset_ref, blocks)
     factor = stiffness / (slots * (neighbours + 1))
-    for b in range(blocks):
+    for b in chosen:
+        at = b - chosen[0]
         mine = [jnp.broadcast_to(pos_ref[c, b : b + 1, :], (8, slots)) for c in range(3)]
         mine_radius = jnp.broadcast_to(radius_ref[b : b + 1, :], (8, slots))
 
@@ -605,18 +621,29 @@
             push = force * inverse
             if c == 0:
                 push = push + gravity
-            still_ref[c, b : b + 1, :] = live * (vel_ref[c, b : b + 1, :] + step_duration * push)
-        push_ref[b : b + 1, :] = live * (step_duration * inverse)
-        seat_ref[0, b] = jnp.clip(w + offsets[b], 0, wide - 1)
-        seat_ref[1, b] = rank[b]
-
-
-def move_kernel(seat_ref, recv_ref, still_ref, push_ref, out_ref):
-    for b in range(push_ref.shape[0]):
-        for c in range(3):
-            start = pl.multiple_of((c * CAP + seat_ref[1, b]) * 128, 128)
-            fluid = recv_ref[seat_ref[0, b], :, pl.ds(start, 128)]
-            out_ref[c, b : b + 1, :] = still_ref[c, b : b + 1, :] + push_ref[b : b + 1, :] * fluid
+            still_ref[c, at : at + 1, :] = live * (vel_ref[c, b : b + 1, :] + step_duration * push)
+        push_ref[at : at + 1, :] = live * (step_duration * inverse)
+        seat_ref[0, at] = jnp.clip(w + offsets[b], 0, wide - 1)
+        seat_ref[1, at] = rank[b]
+
+
+def move_kernel(*refs):
+    *refs, recv_ref, out_ref = refs
+    b = 0
+    for seat_ref, still_ref, push_ref in zip(refs[0::3], refs[1::3], refs[2::3]):
+        for at in range(push_ref.shape[0]):
+            for c in range(3):
+                start = pl.multiple_of((c * CAP + seat_ref[1, at]) * 128, 128)
+                fluid = recv_ref[seat_ref[0, at], :, pl.ds(start, 128)]
+                out_ref[c, b : b + 1, :] = still_ref[c, at : at + 1, :] + push_ref[at : at + 1, :] * fluid
+            b += 1
+
+
+def share(block, narrow):
+    if narrow == 2:
+        return [block, lax.ppermute(block, "narrow", [(0, 1), (1, 0)])]
+    every = lax.all_gather(block, "narrow")
+    return [every[i] for i in range(narrow)]
 
 
 def pairs_of(count, turn):
@@ -654,31 +681,31 @@
     recv = lax.all_to_all(send, "wide", 0, 0)
     edges = [lax.ppermute(part, "wide", pairs_of(wide, turn)) for turn, part in enumerate((edge, other_edge))]
 
-    still, push, seat = call(
-        functools.partial(contact_kernel, wide),
-        (f32s(3, blocks, slots), f32s(blocks, slots), jax.ShapeDtypeStruct((2, blocks), jnp.int32)),
-        [SMEM, SMEM, SMEM, VMEM, VMEM, VMEM],
-        (VMEM, VMEM, SMEM),
-        [pltpu.VMEM((4, blocks, slots, slots), F32)],
-        flops=56 * 128 * 128 * 20,
-    )(neighbours, block_live_count, block_offset, particle_position, radius, particle_velocity)
-
+    def contact(chosen):
+        count = len(chosen)
+        return call(
+            functools.partial(contact_kernel, wide, chosen),
+            (jax.ShapeDtypeStruct((2, count), jnp.int32), f32s(3, count, slots), f32s(count, slots)),
+            [SMEM, SMEM, SMEM, VMEM, VMEM, VMEM],
+            (SMEM, VMEM, VMEM),
+            [pltpu.VMEM((4, blocks, slots, slots), F32)],
+            flops=28 * 128 * 128 * 20,
+        )(neighbours, block_live_count, block_offset, particle_position, radius, particle_velocity)
+
+    early = blocks * 3 // 8
+    recv, moved = lax.optimization_barrier((recv, contact(range(early))))
     window, rows = call(
         functools.partial(void_kernel, wide),
         (f32s(voids + layers, lanes, width), f32s(5, slot_rows, slots)),
         [VMEM] * 4,
         (VMEM, VMEM),
     )(recv, *edges, source)
-    if narrow == 2:
-        pieces = [window, lax.ppermute(window, "narrow", [(0, 1), (1, 0)])]
-    else:
-        every = lax.all_gather(window, "narrow")
-        pieces = [every[i] for i in range(narrow)]
+    pieces = share(window, narrow)
 
     plane = (layers, width_y, width)
     coarse, coefs, first, iterate = call(
         functools.partial(coarsen_kernel, wide),
-        (f32s(wide, half * coarse_y, width), f32s(6, *plane), f32s(*plane), f32s(*plane)),
+        (f32s(wide, half * lanes // 2, width), f32s(6, *plane), f32s(*plane), f32s(*plane)),
         [VMEM] * len(pieces),
         (VMEM,) * 4,
         [
@@ -698,17 +725,19 @@
         flops=10_000_000,
     )(window, rows, gas_velocity)
 
+    gathered, moved_too = lax.optimization_barrier((gathered, contact(range(early, blocks))))
+    parts = share(gathered, narrow)
+
     level_scratch = []
     for index in range(3):
         count = wide * half // 2 >> index
         body = pltpu.VMEM((count, coarse_y, width), F32)
         edged = pltpu.VMEM((count + 2, coarse_y, width), F32)
         level_scratch += [edged, body, pltpu.VMEM((6, count, coarse_y, width), F32), body, body, body, edged, edged]
-    gathered, still, push, seat = lax.optimization_barrier((gathered, still, push, seat))
     pressure, slope = call(
-        functools.partial(solve_kernel, wide),
+        functools.partial(solve_kernel, wide, narrow),
         (f32s(depth, lanes, width), f32s(3, depth, lanes, width)),
-        [VMEM] * 4,
+        [VMEM] * (narrow + 3),
         (VMEM,) * 2,
         level_scratch
         + [pltpu.VMEM(plane, F32), pltpu.VMEM(plane, F32)]
@@ -717,7 +746,7 @@
             pltpu.VMEM((layers // 2 * width_y, width), F32),
             pltpu.VMEM((3, depth, width_y, width), F32),
         ],
-    )(gathered, coefs, first, iterate)
+    )(*parts, coefs, first, iterate)
     returning = call(
         functools.partial(force_kernel, wide),
         f32s(wide, 1, 3 * CAP * slots),
@@ -737,9 +766,9 @@
     updated = call(
         move_kernel,
         f32s(3, blocks, slots),
-        [SMEM] + [VMEM] * 3,
+        [SMEM, VMEM, VMEM] * 2 + [VMEM],
         VMEM,
-    )(seat, returned, still, push)
+    )(*moved, *moved_too, returned)
     return (pressure, gas_next, updated)
 
 

time: 54.6 us -> 53.7 us (0.984)
  waiting for transfers between devices: 19.1 us -> 15.9 us
  Pallas kernels: 15.1 us -> 17.2 us
    pallas_call x9 -> x10, Pallas kernels: 15.1 us -> 17.2 us  [run(): pl.pallas_call(kernel, out_shape=out_shape, in_specs=in_specs, out_specs=...]
    ppermute x2, waiting for transfers between devices: 1.73 us -> 0.01 us  [local(): lax.ppermute(part, 'wide', pairs_of(wide, turn))]
    all_to_all x1, waiting for transfers between devices: 5.48 us -> 3.89 us  [local(): recv = lax.all_to_all(send, 'wide', 0, 0)]
    ppermute x1 -> x2, waiting for transfers between devices: 1.35 us -> 1.49 us  [share(): return [block, lax.ppermute(block, 'narrow', [(0, 1), (1, 0)])]]
  transfers between devices with their start and end apart: 6 -> 7, of which waited for: 5 -> 5; matrix products, arithmetic and copies ran while one was open for 0% -> 0% of each run, Pallas kernels for 13% -> 17%
where the time goes in v4:
time: 53.7 us; the launch traced here: 53.2 us
  starting transfers between devices  19.2 us (36%)
  Pallas kernels  17.2 us (32%)
  waiting for transfers between devices  15.9 us (30%)
  between operations  0.83 us (2%)
    pallas_call x10, Pallas kernels, run(): pl.pallas_call(kernel, out_shape=out_shape, in_specs=in_specs, out_specs=...  17.2 us
    all_to_all x1, starting transfers between devices, local(): recv = lax.all_to_all(send, 'wide', 0, 0)  8.45 us
    all_to_all x1, waiting for transfers between devices, local(): returned = lax.all_to_all(returning, 'wide', 0, 0)  6.88 us
    all_to_all x1, starting transfers between devices, local(): gathered = lax.all_to_all(coarse, 'wide', 0, 0)  4.53 us
    all_to_all x1, waiting for transfers between devices, local(): recv = lax.all_to_all(send, 'wide', 0, 0)  3.89 us
    all_to_all x1, waiting for transfers between devices, local(): gathered = lax.all_to_all(coarse, 'wide', 0, 0)  3.67 us
    all_to_all x1, starting transfers between devices, local(): returned = lax.all_to_all(returning, 'wide', 0, 0)  3.5 us
    ppermute x2, starting transfers between devices, local(): lax.ppermute(part, 'wide', pairs_of(wide, turn))  2.64 us
  transfers between devices with their start and end apart: 7, of which 5 were waited for; matrix products, arithmetic and copies ran while one was open for 0% of the time, Pallas kernels for 17%

profile of v4, /device:TPU:0, one launch (start us, length us, event | category | flops | bytes accessed | tf_op | source)
XLA Modules:
  0.0 53.2 jit_solution(11527513655026262308)
XLA Ops:
  0.6 1.7 %shard_map.121 = (f32[16,32,128]{2,1,0:T(8,128)}, f32[8,8,128]{2,1,0:T(8,128)}, f32[4,8,128]{2,1,0:T(8,128)}, f32[4,8,128]{2,1,0:T(8,128)}) custom-call(s32[8]{0:T(128)} %offset_ref.5, s32[8]{0:T(128)} %count_ref.5, f32[8,128]{1,0:T(8,128)} %radius_ref.5, f32[3,8,128]{2,1,0:T(8,128)} %vel_ref.5, s32[8,128]{1,0:T(8,128)} %cell_ref.1, ...), custom_call_target="tpu_custom_call" | custom-call | bytes 262144 | tf_op jit(solution)/shard_map/pallas_call | solution.py:49
  2.3 0.0 copy-start.9
  2.3 0.0 copy-start.8
  2.3 0.0 copy-start.2
  2.4 0.0 copy-start.3
  2.4 0.0 copy-start.4
  2.4 0.0 copy-start.5
  2.4 0.0 copy-start.6
  2.4 0.0 copy-start.7
  2.4 8.5 %all-to-all-start = ((f32[16,32,128]{2,1,0:T(8,128)}), f32[16,32,128]{2,1,0:T(8,128)S(1)}, u32[]{:S(2)}, u32[]{:S(2)}) async-start(f32[16,32,128]{2,1,0:T(8,128)} %get-tuple-element.36), calls=%async_computation | async-start | bytes 524288 | tf_op jit(solution)/shard_map/all_to_all | solution.py:681
  10.9 0.0 copy-start.1
  10.9 0.0 copy-done.9
  10.9 2.0 %collective-permute-start = (f32[4,8,128]{2,1,0:T(8,128)S(1)}, f32[4,8,128]{2,1,0:T(8,128)S(1)}, u32[]{:S(2)}, u32[]{:S(2)}) collective-permute-start(f32[4,8,128]{2,1,0:T(8,128)S(1)} %copy-done.9), channel_id=1, source_target_pairs={{0,2},{4,6},{8,10},{12,14},{16,18},{20,22},{24,26},{28,30},{2,0},{... | collective-permute-start | bytes 49160 | tf_op jit(solution)/shard_map/ppermute | solution.py:682
  12.9 0.0 copy-done.8
  12.9 0.7 %collective-permute-start.1 = (f32[4,8,128]{2,1,0:T(8,128)S(1)}, f32[4,8,128]{2,1,0:T(8,128)S(1)}, u32[]{:S(2)}, u32[]{:S(2)}) collective-permute-start(f32[4,8,128]{2,1,0:T(8,128)S(1)} %copy-done.8), channel_id=1, source_target_pairs={{2,4},{6,8},{10,12},{14,16},{18,20},{22,24},{26,28},{4,2},{8,6},{1... | collective-permute-start | bytes 49160 | tf_op jit(solution)/shard_map/ppermute | solution.py:682
  13.6 0.0 copy-done.2
  13.6 0.0 copy-done.3
  13.6 0.0 copy-done.4
  13.6 0.0 copy-done.5
  13.6 0.0 copy-done.6
  13.6 0.0 copy-done.7
  13.6 3.2 %shard_map.122 = (s32[2,3]{1,0:T(2,128)S(1)}, f32[3,3,128]{2,1,0:T(4,128)S(1)}, f32[3,128]{1,0:T(4,128)S(1)}) custom-call(s32[8,6]{1,0:T(8,128)S(1)} %copy-done.7, s32[8]{0:T(128)S(1)} %copy-done.5, s32[8]{0:T(128)S(1)} %copy-done.4, f32[3,8,128]{2,1,0:T(8,128)S(1)} %copy-done.6, f32[8,128]{1,0:T(8,128)S(1)} %copy-done.3, f32[3,8,128]{2,1,0:T(8,128)S(1)} %copy-done.2), custom_call_target="tpu_custom_call" | custom-call | flops 9175040 | bytes 262144 | tf_op jit(solution)/shard_map/pallas_call | solution.py:49
  16.9 3.9 %all-to-all-done.recv_ref = f32[16,32,128]{2,1,0:T(8,128)S(1)} async-done(((f32[16,32,128]{2,1,0:T(8,128)}), f32[16,32,128]{2,1,0:T(8,128)S(1)}, u32[]{:S(2)}, u32[]{:S(2)}) %all-to-all-start) | async-done | bytes 262176 | tf_op jit(solution)/shard_map/all_to_all | solution.py:681
  20.8 0.0 collective-permute-done.edge_ref
  20.8 0.0 collective-permute-done.1.other_edge_ref
  20.8 0.0 copy-done.1
  20.8 0.7 %shard_map.123 = (f32[34,8,128]{2,1,0:T(8,128)S(1)}, f32[5,16,128]{2,1,0:T(8,128)S(1)}) custom-call(f32[16,32,128]{2,1,0:T(8,128)S(1)} %all-to-all-done.recv_ref, f32[4,8,128]{2,1,0:T(8,128)S(1)} %collective-permute-done.edge_ref, f32[4,8,128]{2,1,0:T(8,128)S(1)} %collective-permute-done.1.other_edge_ref, f32[8,8,128]{2,1,0:T(8,128)S(1)} %copy-done.1), custom_call_target="tpu_custom_call" | custom-call | bytes 262144 | tf_op jit(solution)/shard_map/pallas_call | solution.py:49
  21.4 0.1 collective-permute-start.2
  21.5 1.3 %collective-permute-done.2.refs_1_ = f32[34,8,128]{2,1,0:T(8,128)S(1)} collective-permute-done((f32[34,8,128]{2,1,0:T(8,128)S(1)}, f32[34,8,128]{2,1,0:T(8,128)S(1)}, u32[]{:S(2)}, u32[]{:S(2)}) %collective-permute-start.2) | collective-permute-done | bytes 139296 | tf_op jit(solution)/shard_map/ppermute | solution.py:644
  22.9 1.2 %shard_map.125 = (f32[16,16,128]{2,1,0:T(8,128)}, f32[6,16,16,128]{3,2,1,0:T(8,128)S(1)}, f32[16,16,128]{2,1,0:T(8,128)S(1)}, f32[16,16,128]{2,1,0:T(8,128)S(1)}) custom-call(f32[34,8,128]{2,1,0:T(8,128)S(1)} %get-tuple-element.45.window_ref.refs_0_, f32[34,8,128]{2,1,0:T(8,128)S(1)} %collective-permute-done.2.refs_1_), custom_call_target="tpu_custom_call" | custom-call | bytes 262144 | tf_op jit(solution)/shard_map/pallas_call | solution.py:49
  24.1 0.0 copy-start
  24.1 4.5 %all-to-all-start.1 = ((f32[16,16,128]{2,1,0:T(8,128)}), f32[16,16,128]{2,1,0:T(8,128)S(1)}, u32[]{:S(2)}, u32[]{:S(2)}) async-start(f32[16,16,128]{2,1,0:T(8,128)} %get-tuple-element.47), calls=%async_computation.1 | async-start | bytes 262144 | tf_op jit(solution)/shard_map/all_to_all | solution.py:718
  28.6 4.1 %shard_map.126 = (s32[2,5]{1,0:T(2,128)S(1)}, f32[3,5,128]{2,1,0:T(8,128)S(1)}, f32[5,128]{1,0:T(8,128)S(1)}) custom-call(s32[8,6]{1,0:T(8,128)S(1)} %copy-done.7, s32[8]{0:T(128)S(1)} %copy-done.5, s32[8]{0:T(128)S(1)} %copy-done.4, f32[3,8,128]{2,1,0:T(8,128)S(1)} %copy-done.6, f32[8,128]{1,0:T(8,128)S(1)} %copy-done.3, f32[3,8,128]{2,1,0:T(8,128)S(1)} %copy-done.2), custom_call_target="tpu_custom_call" | custom-call | flops 9175040 | bytes 262144 | tf_op jit(solution)/shard_map/pallas_call | solution.py:49
  32.8 3.7 %all-to-all-done.1.refs_0_ = f32[16,16,128]{2,1,0:T(8,128)S(1)} async-done(((f32[16,16,128]{2,1,0:T(8,128)}), f32[16,16,128]{2,1,0:T(8,128)S(1)}, u32[]{:S(2)}, u32[]{:S(2)}) %all-to-all-start.1) | async-done | bytes 131104 | tf_op jit(solution)/shard_map/all_to_all | solution.py:718
  36.4 0.0 collective-permute-start.3
  36.4 0.0 copy-done
  36.4 1.2 %shard_map.124 = (f32[3,16,128]{2,1,0:T(8,128)S(1)}, f32[3,8,8,128]{3,2,1,0:T(8,128)S(1)}) custom-call(f32[34,8,128]{2,1,0:T(8,128)S(1)} %get-tuple-element.45.window_ref.refs_0_, f32[5,16,128]{2,1,0:T(8,128)S(1)} %get-tuple-element.44.rows_ref, f32[3,8,8,128]{3,2,1,0:T(8,128)S(1)} %copy-done), custom_call_target="tpu_custom_call" | custom-call | flops 10000000 | bytes 262144 | tf_op jit(solution)/shard_map/pallas_call | solution.py:49
  37.6 0.1 collective-permute-done.3.refs_1_
  37.8 2.0 %shard_map.127 = (f32[8,8,128]{2,1,0:T(8,128)S(1)}, f32[3,8,8,128]{3,2,1,0:T(8,128)S(1)}) custom-call(f32[16,16,128]{2,1,0:T(8,128)S(1)} %all-to-all-done.1.refs_0_, f32[16,16,128]{2,1,0:T(8,128)S(1)} %collective-permute-done.3.refs_1_, f32[6,16,16,128]{3,2,1,0:T(8,128)S(1)} %get-tuple-element.52.refs_2_, f32[16,16,128]{2,1,0:T(8,128)S(1)} %get-tuple-element.53.refs_3_, ...), custom_call_target="tpu_custom_call" | custom-call | bytes 262144 | tf_op jit(solution)/shard_map/pallas_call | solution.py:49
  39.8 1.1 %shard_map.128 = f32[16,1,1152]{2,1,0:T(1,128)} custom-call(f32[5,16,128]{2,1,0:T(8,128)S(1)} %get-tuple-element.44.rows_ref, f32[3,16,128]{2,1,0:T(8,128)S(1)} %get-tuple-element.46.drag_ref, f32[3,8,8,128]{3,2,1,0:T(8,128)S(1)} %get-tuple-element.55.slope_ref), custom_call_target="tpu_custom_call" | custom-call | bytes 262144 | tf_op jit(solution)/shard_map/pallas_call | solution.py:49
  40.9 3.5 %all-to-all-start.2 = ((f32[16,1,1152]{2,1,0:T(1,128)}), f32[16,1,1152]{2,1,0:T(1,128)S(1)}, u32[]{:S(2)}, u32[]{:S(2)}) async-start(f32[16,1,1152]{2,1,0:T(1,128)} %shard_map.128), calls=%async_computation.2 | async-start | bytes 147456 | tf_op jit(solution)/shard_map/all_to_all | solution.py:756
  44.4 0.7 %shard_map.129 = (f32[8,8,128]{2,1,0:T(8,128)}, f32[3,8,8,128]{3,2,1,0:T(8,128)}) custom-call(f32[3,8,8,128]{3,2,1,0:T(8,128)S(1)} %get-tuple-element.56.base_ref, f32[8,8,128]{2,1,0:T(8,128)S(1)} %get-tuple-element.57.pressure_ref, f32[3,8,8,128]{3,2,1,0:T(8,128)S(1)} %get-tuple-element.55.slope_ref), custom_call_target="tpu_custom_call" | custom-call | flops 5000000 | bytes 262144 | tf_op jit(solution)/shard_map/pallas_call | solution.py:49
  45.1 6.9 %all-to-all-done.2.refs_6_ = f32[16,1,1152]{2,1,0:T(1,128)S(1)} async-done(((f32[16,1,1152]{2,1,0:T(1,128)}), f32[16,1,1152]{2,1,0:T(1,128)S(1)}, u32[]{:S(2)}, u32[]{:S(2)}) %all-to-all-start.2) | async-done | bytes 73760 | tf_op jit(solution)/shard_map/all_to_all | solution.py:756
  52.0 1.2 %shard_map.130 = f32[3,8,128]{2,1,0:T(8,128)} custom-call(s32[2,3]{1,0:T(2,128)S(1)} %get-tuple-element.62.refs_0_, f32[3,3,128]{2,1,0:T(4,128)S(1)} %get-tuple-element.63.refs_1_, f32[3,128]{1,0:T(4,128)S(1)} %get-tuple-element.64.refs_2_, s32[2,5]{1,0:T(2,128)S(1)} %get-tuple-element.65.refs_3_, f32[3,5,128]{2,1,0:T(8,128)S(1)} %get-tuple-element.66.refs_4_, ...), custom_call_target="tpu_custom_call" | custom-call | bytes 262144 | tf_op jit(solution)/shard_map/pallas_call | solution.py:49
Async XLA Ops:
  2.3 8.6 %copy-start.9 = (f32[4,8,128]{2,1,0:T(8,128)S(1)}, f32[4,8,128]{2,1,0:T(8,128)}, u32[]{:S(2)}) copy-start(f32[4,8,128]{2,1,0:T(8,128)} %get-tuple-element.41) | copy-start | bytes 49156
  2.3 10.6 %copy-start.8 = (f32[4,8,128]{2,1,0:T(8,128)S(1)}, f32[4,8,128]{2,1,0:T(8,128)}, u32[]{:S(2)}) copy-start(f32[4,8,128]{2,1,0:T(8,128)} %get-tuple-element.42) | copy-start | bytes 49156
  2.3 11.2 %copy-start.2 = (f32[3,8,128]{2,1,0:T(8,128)S(1)}, f32[3,8,128]{2,1,0:T(8,128)}, u32[]{:S(2)}) copy-start(f32[3,8,128]{2,1,0:T(8,128)} %vel_ref.5) | copy-start | bytes 36868
  2.4 11.2 %copy-start.3 = (f32[8,128]{1,0:T(8,128)S(1)}, f32[8,128]{1,0:T(8,128)}, u32[]{:S(2)}) copy-start(f32[8,128]{1,0:T(8,128)} %radius_ref.5) | copy-start | bytes 12292
  2.4 11.2 %copy-start.4 = (s32[8]{0:T(128)S(1)}, s32[8]{0:T(128)}, u32[]{:S(2)}) copy-start(s32[8]{0:T(128)} %offset_ref.5) | copy-start | bytes 100
  2.4 11.2 %copy-start.5 = (s32[8]{0:T(128)S(1)}, s32[8]{0:T(128)}, u32[]{:S(2)}) copy-start(s32[8]{0:T(128)} %count_ref.5) | copy-start | bytes 100
  2.4 11.2 %copy-start.6 = (f32[3,8,128]{2,1,0:T(8,128)S(1)}, f32[3,8,128]{2,1,0:T(8,128)}, u32[]{:S(2)}) copy-start(f32[3,8,128]{2,1,0:T(8,128)} %pos_ref.3) | copy-start | bytes 36868
  2.4 11.2 %copy-start.7 = (s32[8,6]{1,0:T(8,128)S(1)}, s32[8,6]{1,0:T(8,128)}, u32[]{:S(2)}) copy-start(s32[8,6]{1,0:T(8,128)} %near_ref.3) | copy-start | bytes 580
  2.4 18.3 %all-to-all-start = ((f32[16,32,128]{2,1,0:T(8,128)}), f32[16,32,128]{2,1,0:T(8,128)S(1)}, u32[]{:S(2)}, u32[]{:S(2)}) async-start(f32[16,32,128]{2,1,0:T(8,128)} %get-tuple-element.36), calls=%async_computation | async-start | bytes 524288 | tf_op jit(solution)/shard_map/all_to_all | solution.py:681
  10.9 9.9 %copy-start.1 = (f32[8,8,128]{2,1,0:T(8,128)S(1)}, f32[8,8,128]{2,1,0:T(8,128)}, u32[]{:S(2)}) copy-start(f32[8,8,128]{2,1,0:T(8,128)} %get-tuple-element.43.s_ref) | copy-start | bytes 98308
  10.9 9.8 %collective-permute-start = (f32[4,8,128]{2,1,0:T(8,128)S(1)}, f32[4,8,128]{2,1,0:T(8,128)S(1)}, u32[]{:S(2)}, u32[]{:S(2)}) collective-permute-start(f32[4,8,128]{2,1,0:T(8,128)S(1)} %copy-done.9), channel_id=1, source_target_pairs={{0,2},{4,6},{8,10},{12,14},{16,18},{20,22},{24,26},{28,30},{2,0},{... | collective-permute-start | bytes 49160 | tf_op jit(solution)/shard_map/ppermute | solution.py:682
  12.9 7.9 %collective-permute-start.1 = (f32[4,8,128]{2,1,0:T(8,128)S(1)}, f32[4,8,128]{2,1,0:T(8,128)S(1)}, u32[]{:S(2)}, u32[]{:S(2)}) collective-permute-start(f32[4,8,128]{2,1,0:T(8,128)S(1)} %copy-done.8), channel_id=1, source_target_pairs={{2,4},{6,8},{10,12},{14,16},{18,20},{22,24},{26,28},{4,2},{8,6},{1... | collective-permute-start | bytes 49160 | tf_op jit(solution)/shard_map/ppermute | solution.py:682
  21.4 1.4 %collective-permute-start.2 = (f32[34,8,128]{2,1,0:T(8,128)S(1)}, f32[34,8,128]{2,1,0:T(8,128)S(1)}, u32[]{:S(2)}, u32[]{:S(2)}) collective-permute-start(f32[34,8,128]{2,1,0:T(8,128)S(1)} %get-tuple-element.45.window_ref.refs_0_), channel_id=1, source_target_pairs={{0,1},{1,0},{2,3},{3,2},{4,5},{5,4},{6,7},{7,6},{8,9},{9,8},{10,11... | collective-permute-start | bytes 417800 | tf_op jit(solution)/shard_map/ppermute | solution.py:644
  24.1 12.3 %copy-start = (f32[3,8,8,128]{3,2,1,0:T(8,128)S(1)}, f32[3,8,8,128]{3,2,1,0:T(8,128)}, u32[]{:S(2)}) copy-start(f32[3,8,8,128]{3,2,1,0:T(8,128)} %gas_ref.1) | copy-start | bytes 294916
  24.1 12.3 %all-to-all-start.1 = ((f32[16,16,128]{2,1,0:T(8,128)}), f32[16,16,128]{2,1,0:T(8,128)S(1)}, u32[]{:S(2)}, u32[]{:S(2)}) async-start(f32[16,16,128]{2,1,0:T(8,128)} %get-tuple-element.47), calls=%async_computation.1 | async-start | bytes 262144 | tf_op jit(solution)/shard_map/all_to_all | solution.py:718
  36.4 1.3 %collective-permute-start.3 = (f32[16,16,128]{2,1,0:T(8,128)S(1)}, f32[16,16,128]{2,1,0:T(8,128)S(1)}, u32[]{:S(2)}, u32[]{:S(2)}) collective-permute-start(f32[16,16,128]{2,1,0:T(8,128)S(1)} %all-to-all-done.1.refs_0_), channel_id=1, source_target_pairs={{0,1},{1,0},{2,3},{3,2},{4,5},{5,4},{6,7},{7,6},{8,9},{9,8},{10,11... | collective-permute-start | bytes 393224 | tf_op jit(solution)/shard_map/ppermute | solution.py:644
  40.9 11.1 %all-to-all-start.2 = ((f32[16,1,1152]{2,1,0:T(1,128)}), f32[16,1,1152]{2,1,0:T(1,128)S(1)}, u32[]{:S(2)}, u32[]{:S(2)}) async-start(f32[16,1,1152]{2,1,0:T(1,128)} %shard_map.128), calls=%async_computation.2 | async-start | bytes 147456 | tf_op jit(solution)/shard_map/all_to_all | solution.py:756

commit v5 on v4

--- a/solution.py
+++ b/solution.py
@@ -79,35 +79,42 @@
     offsets = [offset_ref[i] for i in range(count)]
     found = []
     for i in range(count):
-        rank = jnp.int32(0)
+        rank = 0
         for j in range(i):
             rank = rank + jnp.where(offsets[j] == offsets[i], 1, 0)
         found.append(rank)
     return offsets, found
 
 
-def pack_kernel(wide, offset_ref, count_ref, radius_ref, vel_ref, cell_ref, source_ref, before_ref, send_ref, s_ref, edge_ref, other_edge_ref):
+def pack_kernel(wide, offset_ref, count_ref, radius_ref, vel_ref, cell_ref, source_ref, before_ref, send_ref, s_ref, edge_ref, other_edge_ref, slot_ref):
     w = lax.axis_index("wide")
     blocks, slots = radius_ref.shape
     depth, lanes, _ = source_ref.shape
-    send_ref[...] = jnp.zeros(send_ref.shape, F32)
+    slot_ref[...] = jnp.zeros(slot_ref.shape, F32)
+    for d in range(-SPREAD - 1, SPREAD + 2):
+        target = jnp.clip(w + d, 0, wide - 1)
+        send_ref[target] = jnp.zeros(send_ref.shape[1:], F32)
     offsets, rank = ranks(offset_ref, blocks)
     slot = iota((1, slots), 1)
     for b in range(blocks):
         radius = radius_ref[b : b + 1, :]
+        place = offsets[b] + SPREAD
         vol = jnp.where(slot < count_ref[b], radius * radius * radius, 0.0)
-        cell = cell_ref[b : b + 1, :].astype(F32)
+        slot_ref[place, pl.ds(rank[b], 1), :] = vol
+        slot_ref[place, pl.ds(CAP + rank[b], 1), :] = cell_ref[b : b + 1, :].astype(F32)
+        for c in range(3):
+            slot_ref[place, pl.ds((2 + c) * CAP + rank[b], 1), :] = vel_ref[c, b : b + 1, :]
+    for d in range(-SPREAD, SPREAD + 1):
         for e in (-1, 0, 1):
-            target = w + offsets[b] - e
+            target = w + d - e
 
             @pl.when(jnp.logical_and(target >= 0, target < wide))
             def _():
-                row = (e + 1) * CAP + rank[b]
-                send_ref[target, pl.ds(VOL_ROW + row, 1), :] = vol
-                send_ref[target, pl.ds(CELL_ROW + row, 1), :] = cell
+                row = (e + 1) * CAP
+                send_ref[target, VOL_ROW + row : VOL_ROW + row + CAP, :] = slot_ref[d + SPREAD, :CAP, :]
+                send_ref[target, CELL_ROW + row : CELL_ROW + row + CAP, :] = slot_ref[d + SPREAD, CAP : 2 * CAP, :]
                 if e == 0:
-                    for c in range(3):
-                        send_ref[target, pl.ds(VEL_ROW + c * CAP + rank[b], 1), :] = vel_ref[c, b : b + 1, :]
+                    send_ref[target, VEL_ROW : VEL_ROW + 3 * CAP, :] = slot_ref[d + SPREAD, 2 * CAP : 5 * CAP, :]
 
     for z in range(depth):
         s_ref[z] = source_ref[z] + before_ref[z] * (1.0 / step_duration)
@@ -676,6 +683,7 @@
         (f32s(wide, SEND_ROWS, width), f32s(depth, lanes, width), f32s(REACH, lanes, width), f32s(REACH, lanes, width)),
         [SMEM, SMEM] + [VMEM] * 5,
         (VMEM,) * 4,
+        [pltpu.VMEM((GROUPS, -(-5 * CAP // 8) * 8, slots), F32)],
         spare=VMEM_MOST,
     )(block_offset, block_live_count, radius, particle_velocity, cell_index, pressure_source, void_before)
     recv = lax.all_to_all(send, "wide", 0, 0)

time: 53.7 us -> 53.7 us (level)
  no operation moved by 1% of the time
where the time goes in v5:
time: 53.7 us; the launch traced here: 53.2 us
  starting transfers between devices  19.2 us (36%)
  Pallas kernels  17.2 us (32%)
  waiting for transfers between devices  15.9 us (30%)
  between operations  0.83 us (2%)
    pallas_call x10, Pallas kernels, run(): pl.pallas_call(kernel, out_shape=out_shape, in_specs=in_specs, out_specs=...  17.2 us
    all_to_all x1, starting transfers between devices, local(): recv = lax.all_to_all(send, 'wide', 0, 0)  8.46 us
    all_to_all x1, waiting for transfers between devices, local(): returned = lax.all_to_all(returning, 'wide', 0, 0)  6.88 us
    all_to_all x1, starting transfers between devices, local(): gathered = lax.all_to_all(coarse, 'wide', 0, 0)  4.52 us
    all_to_all x1, waiting for transfers between devices, local(): recv = lax.all_to_all(send, 'wide', 0, 0)  3.89 us
    all_to_all x1, waiting for transfers between devices, local(): gathered = lax.all_to_all(coarse, 'wide', 0, 0)  3.67 us
    all_to_all x1, starting transfers between devices, local(): returned = lax.all_to_all(returning, 'wide', 0, 0)  3.5 us
    ppermute x2, starting transfers between devices, local(): lax.ppermute(part, 'wide', pairs_of(wide, turn))  2.64 us
  transfers between devices with their start and end apart: 7, of which 5 were waited for; matrix products, arithmetic and copies ran while one was open for 0% of the time, Pallas kernels for 17%

profile of v5, /device:TPU:0, one launch (start us, length us, event | category | flops | bytes accessed | tf_op | source)
XLA Modules:
  0.0 53.2 jit_solution(16478066493308259032)
XLA Ops:
  0.6 1.7 %shard_map.121 = (f32[16,32,128]{2,1,0:T(8,128)}, f32[8,8,128]{2,1,0:T(8,128)}, f32[4,8,128]{2,1,0:T(8,128)}, f32[4,8,128]{2,1,0:T(8,128)}) custom-call(s32[8]{0:T(128)} %offset_ref.5, s32[8]{0:T(128)} %count_ref.5, f32[8,128]{1,0:T(8,128)} %radius_ref.5, f32[3,8,128]{2,1,0:T(8,128)} %vel_ref.5, s32[8,128]{1,0:T(8,128)} %cell_ref.1, ...), custom_call_target="tpu_custom_call" | custom-call | bytes 262144 | tf_op jit(solution)/shard_map/pallas_call | solution.py:49
  2.3 0.0 copy-start.9
  2.3 0.0 copy-start.8
  2.3 0.0 copy-start.2
  2.4 0.0 copy-start.3
  2.4 0.0 copy-start.4
  2.4 0.0 copy-start.5
  2.4 0.0 copy-start.6
  2.4 0.0 copy-start.7
  2.4 8.5 %all-to-all-start = ((f32[16,32,128]{2,1,0:T(8,128)}), f32[16,32,128]{2,1,0:T(8,128)S(1)}, u32[]{:S(2)}, u32[]{:S(2)}) async-start(f32[16,32,128]{2,1,0:T(8,128)} %get-tuple-element.36), calls=%async_computation | async-start | bytes 524288 | tf_op jit(solution)/shard_map/all_to_all | solution.py:689
  10.9 0.0 copy-start.1
  10.9 0.0 copy-done.9
  10.9 2.0 %collective-permute-start = (f32[4,8,128]{2,1,0:T(8,128)S(1)}, f32[4,8,128]{2,1,0:T(8,128)S(1)}, u32[]{:S(2)}, u32[]{:S(2)}) collective-permute-start(f32[4,8,128]{2,1,0:T(8,128)S(1)} %copy-done.9), channel_id=1, source_target_pairs={{0,2},{4,6},{8,10},{12,14},{16,18},{20,22},{24,26},{28,30},{2,0},{... | collective-permute-start | bytes 49160 | tf_op jit(solution)/shard_map/ppermute | solution.py:690
  12.9 0.0 copy-done.8
  12.9 0.7 %collective-permute-start.1 = (f32[4,8,128]{2,1,0:T(8,128)S(1)}, f32[4,8,128]{2,1,0:T(8,128)S(1)}, u32[]{:S(2)}, u32[]{:S(2)}) collective-permute-start(f32[4,8,128]{2,1,0:T(8,128)S(1)} %copy-done.8), channel_id=1, source_target_pairs={{2,4},{6,8},{10,12},{14,16},{18,20},{22,24},{26,28},{4,2},{8,6},{1... | collective-permute-start | bytes 49160 | tf_op jit(solution)/shard_map/ppermute | solution.py:690
  13.6 0.0 copy-done.2
  13.6 0.0 copy-done.3
  13.6 0.0 copy-done.4
  13.6 0.0 copy-done.5
  13.6 0.0 copy-done.6
  13.6 0.0 copy-done.7
  13.6 3.2 %shard_map.122 = (s32[2,3]{1,0:T(2,128)S(1)}, f32[3,3,128]{2,1,0:T(4,128)S(1)}, f32[3,128]{1,0:T(4,128)S(1)}) custom-call(s32[8,6]{1,0:T(8,128)S(1)} %copy-done.7, s32[8]{0:T(128)S(1)} %copy-done.5, s32[8]{0:T(128)S(1)} %copy-done.4, f32[3,8,128]{2,1,0:T(8,128)S(1)} %copy-done.6, f32[8,128]{1,0:T(8,128)S(1)} %copy-done.3, f32[3,8,128]{2,1,0:T(8,128)S(1)} %copy-done.2), custom_call_target="tpu_custom_call" | custom-call | flops 9175040 | bytes 262144 | tf_op jit(solution)/shard_map/pallas_call | solution.py:49
  16.9 3.9 %all-to-all-done.recv_ref = f32[16,32,128]{2,1,0:T(8,128)S(1)} async-done(((f32[16,32,128]{2,1,0:T(8,128)}), f32[16,32,128]{2,1,0:T(8,128)S(1)}, u32[]{:S(2)}, u32[]{:S(2)}) %all-to-all-start) | async-done | bytes 262176 | tf_op jit(solution)/shard_map/all_to_all | solution.py:689
  20.8 0.0 collective-permute-done.edge_ref
  20.8 0.0 collective-permute-done.1.other_edge_ref
  20.8 0.0 copy-done.1
  20.8 0.7 %shard_map.123 = (f32[34,8,128]{2,1,0:T(8,128)S(1)}, f32[5,16,128]{2,1,0:T(8,128)S(1)}) custom-call(f32[16,32,128]{2,1,0:T(8,128)S(1)} %all-to-all-done.recv_ref, f32[4,8,128]{2,1,0:T(8,128)S(1)} %collective-permute-done.edge_ref, f32[4,8,128]{2,1,0:T(8,128)S(1)} %collective-permute-done.1.other_edge_ref, f32[8,8,128]{2,1,0:T(8,128)S(1)} %copy-done.1), custom_call_target="tpu_custom_call" | custom-call | bytes 262144 | tf_op jit(solution)/shard_map/pallas_call | solution.py:49
  21.4 0.1 collective-permute-start.2
  21.5 1.3 %collective-permute-done.2.refs_1_ = f32[34,8,128]{2,1,0:T(8,128)S(1)} collective-permute-done((f32[34,8,128]{2,1,0:T(8,128)S(1)}, f32[34,8,128]{2,1,0:T(8,128)S(1)}, u32[]{:S(2)}, u32[]{:S(2)}) %collective-permute-start.2) | collective-permute-done | bytes 139296 | tf_op jit(solution)/shard_map/ppermute | solution.py:651
  22.9 1.2 %shard_map.125 = (f32[16,16,128]{2,1,0:T(8,128)}, f32[6,16,16,128]{3,2,1,0:T(8,128)S(1)}, f32[16,16,128]{2,1,0:T(8,128)S(1)}, f32[16,16,128]{2,1,0:T(8,128)S(1)}) custom-call(f32[34,8,128]{2,1,0:T(8,128)S(1)} %get-tuple-element.45.window_ref.refs_0_, f32[34,8,128]{2,1,0:T(8,128)S(1)} %collective-permute-done.2.refs_1_), custom_call_target="tpu_custom_call" | custom-call | bytes 262144 | tf_op jit(solution)/shard_map/pallas_call | solution.py:49
  24.1 0.0 copy-start
  24.1 4.5 %all-to-all-start.1 = ((f32[16,16,128]{2,1,0:T(8,128)}), f32[16,16,128]{2,1,0:T(8,128)S(1)}, u32[]{:S(2)}, u32[]{:S(2)}) async-start(f32[16,16,128]{2,1,0:T(8,128)} %get-tuple-element.47), calls=%async_computation.1 | async-start | bytes 262144 | tf_op jit(solution)/shard_map/all_to_all | solution.py:726
  28.6 4.1 %shard_map.126 = (s32[2,5]{1,0:T(2,128)S(1)}, f32[3,5,128]{2,1,0:T(8,128)S(1)}, f32[5,128]{1,0:T(8,128)S(1)}) custom-call(s32[8,6]{1,0:T(8,128)S(1)} %copy-done.7, s32[8]{0:T(128)S(1)} %copy-done.5, s32[8]{0:T(128)S(1)} %copy-done.4, f32[3,8,128]{2,1,0:T(8,128)S(1)} %copy-done.6, f32[8,128]{1,0:T(8,128)S(1)} %copy-done.3, f32[3,8,128]{2,1,0:T(8,128)S(1)} %copy-done.2), custom_call_target="tpu_custom_call" | custom-call | flops 9175040 | bytes 262144 | tf_op jit(solution)/shard_map/pallas_call | solution.py:49
  32.8 3.7 %all-to-all-done.1.refs_0_ = f32[16,16,128]{2,1,0:T(8,128)S(1)} async-done(((f32[16,16,128]{2,1,0:T(8,128)}), f32[16,16,128]{2,1,0:T(8,128)S(1)}, u32[]{:S(2)}, u32[]{:S(2)}) %all-to-all-start.1) | async-done | bytes 131104 | tf_op jit(solution)/shard_map/all_to_all | solution.py:726
  36.4 0.0 collective-permute-start.3
  36.4 0.0 copy-done
  36.4 1.2 %shard_map.124 = (f32[3,16,128]{2,1,0:T(8,128)S(1)}, f32[3,8,8,128]{3,2,1,0:T(8,128)S(1)}) custom-call(f32[34,8,128]{2,1,0:T(8,128)S(1)} %get-tuple-element.45.window_ref.refs_0_, f32[5,16,128]{2,1,0:T(8,128)S(1)} %get-tuple-element.44.rows_ref, f32[3,8,8,128]{3,2,1,0:T(8,128)S(1)} %copy-done), custom_call_target="tpu_custom_call" | custom-call | flops 10000000 | bytes 262144 | tf_op jit(solution)/shard_map/pallas_call | solution.py:49
  37.6 0.1 collective-permute-done.3.refs_1_
  37.8 2.0 %shard_map.127 = (f32[8,8,128]{2,1,0:T(8,128)S(1)}, f32[3,8,8,128]{3,2,1,0:T(8,128)S(1)}) custom-call(f32[16,16,128]{2,1,0:T(8,128)S(1)} %all-to-all-done.1.refs_0_, f32[16,16,128]{2,1,0:T(8,128)S(1)} %collective-permute-done.3.refs_1_, f32[6,16,16,128]{3,2,1,0:T(8,128)S(1)} %get-tuple-element.52.refs_2_, f32[16,16,128]{2,1,0:T(8,128)S(1)} %get-tuple-element.53.refs_3_, ...), custom_call_target="tpu_custom_call" | custom-call | bytes 262144 | tf_op jit(solution)/shard_map/pallas_call | solution.py:49
  39.8 1.1 %shard_map.128 = f32[16,1,1152]{2,1,0:T(1,128)} custom-call(f32[5,16,128]{2,1,0:T(8,128)S(1)} %get-tuple-element.44.rows_ref, f32[3,16,128]{2,1,0:T(8,128)S(1)} %get-tuple-element.46.drag_ref, f32[3,8,8,128]{3,2,1,0:T(8,128)S(1)} %get-tuple-element.55.slope_ref), custom_call_target="tpu_custom_call" | custom-call | bytes 262144 | tf_op jit(solution)/shard_map/pallas_call | solution.py:49
  40.9 3.5 %all-to-all-start.2 = ((f32[16,1,1152]{2,1,0:T(1,128)}), f32[16,1,1152]{2,1,0:T(1,128)S(1)}, u32[]{:S(2)}, u32[]{:S(2)}) async-start(f32[16,1,1152]{2,1,0:T(1,128)} %shard_map.128), calls=%async_computation.2 | async-start | bytes 147456 | tf_op jit(solution)/shard_map/all_to_all | solution.py:764
  44.4 0.7 %shard_map.129 = (f32[8,8,128]{2,1,0:T(8,128)}, f32[3,8,8,128]{3,2,1,0:T(8,128)}) custom-call(f32[3,8,8,128]{3,2,1,0:T(8,128)S(1)} %get-tuple-element.56.base_ref, f32[8,8,128]{2,1,0:T(8,128)S(1)} %get-tuple-element.57.pressure_ref, f32[3,8,8,128]{3,2,1,0:T(8,128)S(1)} %get-tuple-element.55.slope_ref), custom_call_target="tpu_custom_call" | custom-call | flops 5000000 | bytes 262144 | tf_op jit(solution)/shard_map/pallas_call | solution.py:49
  45.1 6.9 %all-to-all-done.2.refs_6_ = f32[16,1,1152]{2,1,0:T(1,128)S(1)} async-done(((f32[16,1,1152]{2,1,0:T(1,128)}), f32[16,1,1152]{2,1,0:T(1,128)S(1)}, u32[]{:S(2)}, u32[]{:S(2)}) %all-to-all-start.2) | async-done | bytes 73760 | tf_op jit(solution)/shard_map/all_to_all | solution.py:764
  52.0 1.2 %shard_map.130 = f32[3,8,128]{2,1,0:T(8,128)} custom-call(s32[2,3]{1,0:T(2,128)S(1)} %get-tuple-element.62.refs_0_, f32[3,3,128]{2,1,0:T(4,128)S(1)} %get-tuple-element.63.refs_1_, f32[3,128]{1,0:T(4,128)S(1)} %get-tuple-element.64.refs_2_, s32[2,5]{1,0:T(2,128)S(1)} %get-tuple-element.65.refs_3_, f32[3,5,128]{2,1,0:T(8,128)S(1)} %get-tuple-element.66.refs_4_, ...), custom_call_target="tpu_custom_call" | custom-call | bytes 262144 | tf_op jit(solution)/shard_map/pallas_call | solution.py:49
Async XLA Ops:
  2.3 8.6 %copy-start.9 = (f32[4,8,128]{2,1,0:T(8,128)S(1)}, f32[4,8,128]{2,1,0:T(8,128)}, u32[]{:S(2)}) copy-start(f32[4,8,128]{2,1,0:T(8,128)} %get-tuple-element.41) | copy-start | bytes 49156
  2.3 10.6 %copy-start.8 = (f32[4,8,128]{2,1,0:T(8,128)S(1)}, f32[4,8,128]{2,1,0:T(8,128)}, u32[]{:S(2)}) copy-start(f32[4,8,128]{2,1,0:T(8,128)} %get-tuple-element.42) | copy-start | bytes 49156
  2.3 11.2 %copy-start.2 = (f32[3,8,128]{2,1,0:T(8,128)S(1)}, f32[3,8,128]{2,1,0:T(8,128)}, u32[]{:S(2)}) copy-start(f32[3,8,128]{2,1,0:T(8,128)} %vel_ref.5) | copy-start | bytes 36868
  2.4 11.2 %copy-start.3 = (f32[8,128]{1,0:T(8,128)S(1)}, f32[8,128]{1,0:T(8,128)}, u32[]{:S(2)}) copy-start(f32[8,128]{1,0:T(8,128)} %radius_ref.5) | copy-start | bytes 12292
  2.4 11.2 %copy-start.4 = (s32[8]{0:T(128)S(1)}, s32[8]{0:T(128)}, u32[]{:S(2)}) copy-start(s32[8]{0:T(128)} %offset_ref.5) | copy-start | bytes 100
  2.4 11.2 %copy-start.5 = (s32[8]{0:T(128)S(1)}, s32[8]{0:T(128)}, u32[]{:S(2)}) copy-start(s32[8]{0:T(128)} %count_ref.5) | copy-start | bytes 100
  2.4 11.2 %copy-start.6 = (f32[3,8,128]{2,1,0:T(8,128)S(1)}, f32[3,8,128]{2,1,0:T(8,128)}, u32[]{:S(2)}) copy-start(f32[3,8,128]{2,1,0:T(8,128)} %pos_ref.3) | copy-start | bytes 36868
  2.4 11.2 %copy-start.7 = (s32[8,6]{1,0:T(8,128)S(1)}, s32[8,6]{1,0:T(8,128)}, u32[]{:S(2)}) copy-start(s32[8,6]{1,0:T(8,128)} %near_ref.3) | copy-start | bytes 580
  2.4 18.3 %all-to-all-start = ((f32[16,32,128]{2,1,0:T(8,128)}), f32[16,32,128]{2,1,0:T(8,128)S(1)}, u32[]{:S(2)}, u32[]{:S(2)}) async-start(f32[16,32,128]{2,1,0:T(8,128)} %get-tuple-element.36), calls=%async_computation | async-start | bytes 524288 | tf_op jit(solution)/shard_map/all_to_all | solution.py:689
  10.9 9.9 %copy-start.1 = (f32[8,8,128]{2,1,0:T(8,128)S(1)}, f32[8,8,128]{2,1,0:T(8,128)}, u32[]{:S(2)}) copy-start(f32[8,8,128]{2,1,0:T(8,128)} %get-tuple-element.43.s_ref) | copy-start | bytes 98308
  10.9 9.8 %collective-permute-start = (f32[4,8,128]{2,1,0:T(8,128)S(1)}, f32[4,8,128]{2,1,0:T(8,128)S(1)}, u32[]{:S(2)}, u32[]{:S(2)}) collective-permute-start(f32[4,8,128]{2,1,0:T(8,128)S(1)} %copy-done.9), channel_id=1, source_target_pairs={{0,2},{4,6},{8,10},{12,14},{16,18},{20,22},{24,26},{28,30},{2,0},{... | collective-permute-start | bytes 49160 | tf_op jit(solution)/shard_map/ppermute | solution.py:690
  12.9 7.9 %collective-permute-start.1 = (f32[4,8,128]{2,1,0:T(8,128)S(1)}, f32[4,8,128]{2,1,0:T(8,128)S(1)}, u32[]{:S(2)}, u32[]{:S(2)}) collective-permute-start(f32[4,8,128]{2,1,0:T(8,128)S(1)} %copy-done.8), channel_id=1, source_target_pairs={{2,4},{6,8},{10,12},{14,16},{18,20},{22,24},{26,28},{4,2},{8,6},{1... | collective-permute-start | bytes 49160 | tf_op jit(solution)/shard_map/ppermute | solution.py:690
  21.4 1.4 %collective-permute-start.2 = (f32[34,8,128]{2,1,0:T(8,128)S(1)}, f32[34,8,128]{2,1,0:T(8,128)S(1)}, u32[]{:S(2)}, u32[]{:S(2)}) collective-permute-start(f32[34,8,128]{2,1,0:T(8,128)S(1)} %get-tuple-element.45.window_ref.refs_0_), channel_id=1, source_target_pairs={{0,1},{1,0},{2,3},{3,2},{4,5},{5,4},{6,7},{7,6},{8,9},{9,8},{10,11... | collective-permute-start | bytes 417800 | tf_op jit(solution)/shard_map/ppermute | solution.py:651
  24.1 12.3 %copy-start = (f32[3,8,8,128]{3,2,1,0:T(8,128)S(1)}, f32[3,8,8,128]{3,2,1,0:T(8,128)}, u32[]{:S(2)}) copy-start(f32[3,8,8,128]{3,2,1,0:T(8,128)} %gas_ref.1) | copy-start | bytes 294916
  24.1 12.3 %all-to-all-start.1 = ((f32[16,16,128]{2,1,0:T(8,128)}), f32[16,16,128]{2,1,0:T(8,128)S(1)}, u32[]{:S(2)}, u32[]{:S(2)}) async-start(f32[16,16,128]{2,1,0:T(8,128)} %get-tuple-element.47), calls=%async_computation.1 | async-start | bytes 262144 | tf_op jit(solution)/shard_map/all_to_all | solution.py:726
  36.4 1.3 %collective-permute-start.3 = (f32[16,16,128]{2,1,0:T(8,128)S(1)}, f32[16,16,128]{2,1,0:T(8,128)S(1)}, u32[]{:S(2)}, u32[]{:S(2)}) collective-permute-start(f32[16,16,128]{2,1,0:T(8,128)S(1)} %all-to-all-done.1.refs_0_), channel_id=1, source_target_pairs={{0,1},{1,0},{2,3},{3,2},{4,5},{5,4},{6,7},{7,6},{8,9},{9,8},{10,11... | collective-permute-start | bytes 393224 | tf_op jit(solution)/shard_map/ppermute | solution.py:651
  40.9 11.1 %all-to-all-start.2 = ((f32[16,1,1152]{2,1,0:T(1,128)}), f32[16,1,1152]{2,1,0:T(1,128)S(1)}, u32[]{:S(2)}, u32[]{:S(2)}) async-start(f32[16,1,1152]{2,1,0:T(1,128)} %shard_map.128), calls=%async_computation.2 | async-start | bytes 147456 | tf_op jit(solution)/shard_map/all_to_all | solution.py:764

commit v6 on v5

--- a/solution.py
+++ b/solution.py
@@ -700,7 +700,7 @@
             flops=28 * 128 * 128 * 20,
         )(neighbours, block_live_count, block_offset, particle_position, radius, particle_velocity)
 
-    early = blocks * 3 // 8
+    early, late = blocks // 4, blocks * 5 // 8
     recv, moved = lax.optimization_barrier((recv, contact(range(early))))
     window, rows = call(
         functools.partial(void_kernel, wide),
@@ -733,7 +733,7 @@
         flops=10_000_000,
     )(window, rows, gas_velocity)
 
-    gathered, moved_too = lax.optimization_barrier((gathered, contact(range(early, blocks))))
+    gathered, moved_too = lax.optimization_barrier((gathered, contact(range(early, late))))
     parts = share(gathered, narrow)
 
     level_scratch = []
@@ -769,14 +769,16 @@
         (VMEM,) * 2,
         flops=5_000_000,
     )(base, pressure, slope)
-    returned, pressure, gas_next = lax.optimization_barrier((returned, pressure, gas_next))
+    returned, pressure, gas_next, moved_last = lax.optimization_barrier(
+        (returned, pressure, gas_next, contact(range(late, blocks)))
+    )
 
     updated = call(
         move_kernel,
         f32s(3, blocks, slots),
-        [SMEM, VMEM, VMEM] * 2 + [VMEM],
+        [SMEM, VMEM, VMEM] * 3 + [VMEM],
         VMEM,
-    )(*moved, *moved_too, returned)
+    )(*moved, *moved_too, *moved_last, returned)
     return (pressure, gas_next, updated)
 
 

time: 53.7 us -> 53.5 us (level)
  Pallas kernels: 17.2 us -> 19.2 us
  waiting for transfers between devices: 15.9 us -> 14 us
    all_to_all x1, waiting for transfers between devices: 6.88 us -> 3.61 us  [local(): returned = lax.all_to_all(returning, 'wide', 0, 0)]
    pallas_call x10 -> x11, Pallas kernels: 17.2 us -> 19.2 us  [run(): pl.pallas_call(kernel, out_shape=out_shape, in_specs=in_specs, out_specs=...]
    all_to_all x1, waiting for transfers between devices: 3.67 us -> 4.53 us  [local(): gathered = lax.all_to_all(coarse, 'wide', 0, 0)]
  transfers between devices with their start and end apart: 7 -> 7, of which waited for: 5 -> 5; matrix products, arithmetic and copies ran while one was open for 0% -> 0% of each run, Pallas kernels for 17% -> 21%
where the time goes in v6:
time: 53.5 us; the launch traced here: 53 us
  Pallas kernels  19.2 us (36%)
  starting transfers between devices  19 us (36%)
  waiting for transfers between devices  14 us (26%)
  between operations  0.84 us (2%)
    pallas_call x11, Pallas kernels, run(): pl.pallas_call(kernel, out_shape=out_shape, in_specs=in_specs, out_specs=...  19.2 us
    all_to_all x1, starting transfers between devices, local(): recv = lax.all_to_all(send, 'wide', 0, 0)  8.46 us
    all_to_all x1, waiting for transfers between devices, local(): gathered = lax.all_to_all(coarse, 'wide', 0, 0)  4.53 us
    all_to_all x1, starting transfers between devices, local(): gathered = lax.all_to_all(coarse, 'wide', 0, 0)  4.33 us
    all_to_all x1, waiting for transfers between devices, local(): recv = lax.all_to_all(send, 'wide', 0, 0)  4.32 us
    all_to_all x1, waiting for transfers between devices, local(): returned = lax.all_to_all(returning, 'wide', 0, 0)  3.61 us
    all_to_all x1, starting transfers between devices, local(): returned = lax.all_to_all(returning, 'wide', 0, 0)  3.5 us
    ppermute x2, starting transfers between devices, local(): lax.ppermute(part, 'wide', pairs_of(wide, turn))  2.64 us
  transfers between devices with their start and end apart: 7, of which 5 were waited for; matrix products, arithmetic and copies ran while one was open for 0% of the time, Pallas kernels for 21%

profile of v6, /device:TPU:0, one launch (start us, length us, event | category | flops | bytes accessed | tf_op | source)
XLA Modules:
  0.0 53.0 jit_solution(5493095189024717429)
XLA Ops:
  0.6 1.7 %shard_map.121 = (f32[16,32,128]{2,1,0:T(8,128)}, f32[8,8,128]{2,1,0:T(8,128)}, f32[4,8,128]{2,1,0:T(8,128)}, f32[4,8,128]{2,1,0:T(8,128)}) custom-call(s32[8]{0:T(128)} %offset_ref.7, s32[8]{0:T(128)} %count_ref.7, f32[8,128]{1,0:T(8,128)} %radius_ref.7, f32[3,8,128]{2,1,0:T(8,128)} %vel_ref.7, s32[8,128]{1,0:T(8,128)} %cell_ref.1, ...), custom_call_target="tpu_custom_call" | custom-call | bytes 262144 | tf_op jit(solution)/shard_map/pallas_call | solution.py:49
  2.4 0.0 copy-start.9
  2.4 0.0 copy-start.8
  2.4 0.0 copy-start.2
  2.4 0.0 copy-start.3
  2.4 0.0 copy-start.4
  2.4 0.0 copy-start.5
  2.4 0.0 copy-start.6
  2.4 0.0 copy-start.7
  2.4 8.5 %all-to-all-start = ((f32[16,32,128]{2,1,0:T(8,128)}), f32[16,32,128]{2,1,0:T(8,128)S(1)}, u32[]{:S(2)}, u32[]{:S(2)}) async-start(f32[16,32,128]{2,1,0:T(8,128)} %get-tuple-element.42), calls=%async_computation | async-start | bytes 524288 | tf_op jit(solution)/shard_map/all_to_all | solution.py:689
  10.9 0.0 copy-start.1
  10.9 0.0 copy-done.9
  10.9 2.0 %collective-permute-start = (f32[4,8,128]{2,1,0:T(8,128)S(1)}, f32[4,8,128]{2,1,0:T(8,128)S(1)}, u32[]{:S(2)}, u32[]{:S(2)}) collective-permute-start(f32[4,8,128]{2,1,0:T(8,128)S(1)} %copy-done.9), channel_id=1, source_target_pairs={{0,2},{4,6},{8,10},{12,14},{16,18},{20,22},{24,26},{28,30},{2,0},{... | collective-permute-start | bytes 49160 | tf_op jit(solution)/shard_map/ppermute | solution.py:690
  12.9 0.0 copy-done.8
  12.9 0.7 %collective-permute-start.1 = (f32[4,8,128]{2,1,0:T(8,128)S(1)}, f32[4,8,128]{2,1,0:T(8,128)S(1)}, u32[]{:S(2)}, u32[]{:S(2)}) collective-permute-start(f32[4,8,128]{2,1,0:T(8,128)S(1)} %copy-done.8), channel_id=1, source_target_pairs={{2,4},{6,8},{10,12},{14,16},{18,20},{22,24},{26,28},{4,2},{8,6},{1... | collective-permute-start | bytes 49160 | tf_op jit(solution)/shard_map/ppermute | solution.py:690
  13.6 0.0 copy-done.2
  13.6 0.0 copy-done.3
  13.6 0.0 copy-done.4
  13.6 0.0 copy-done.5
  13.6 0.0 copy-done.6
  13.6 0.0 copy-done.7
  13.6 2.8 %shard_map.122 = (s32[2,2]{1,0:T(2,128)S(1)}, f32[3,2,128]{2,1,0:T(2,128)S(1)}, f32[2,128]{1,0:T(2,128)S(1)}) custom-call(s32[8,6]{1,0:T(8,128)S(1)} %copy-done.7, s32[8]{0:T(128)S(1)} %copy-done.5, s32[8]{0:T(128)S(1)} %copy-done.4, f32[3,8,128]{2,1,0:T(8,128)S(1)} %copy-done.6, f32[8,128]{1,0:T(8,128)S(1)} %copy-done.3, f32[3,8,128]{2,1,0:T(8,128)S(1)} %copy-done.2), custom_call_target="tpu_custom_call" | custom-call | flops 9175040 | bytes 262144 | tf_op jit(solution)/shard_map/pallas_call | solution.py:49
  16.4 4.3 %all-to-all-done.recv_ref = f32[16,32,128]{2,1,0:T(8,128)S(1)} async-done(((f32[16,32,128]{2,1,0:T(8,128)}), f32[16,32,128]{2,1,0:T(8,128)S(1)}, u32[]{:S(2)}, u32[]{:S(2)}) %all-to-all-start) | async-done | bytes 262176 | tf_op jit(solution)/shard_map/all_to_all | solution.py:689
  20.8 0.0 collective-permute-done.edge_ref
  20.8 0.0 collective-permute-done.1.other_edge_ref
  20.8 0.0 copy-done.1
  20.8 0.7 %shard_map.123 = (f32[34,8,128]{2,1,0:T(8,128)S(1)}, f32[5,16,128]{2,1,0:T(8,128)S(1)}) custom-call(f32[16,32,128]{2,1,0:T(8,128)S(1)} %all-to-all-done.recv_ref, f32[4,8,128]{2,1,0:T(8,128)S(1)} %collective-permute-done.edge_ref, f32[4,8,128]{2,1,0:T(8,128)S(1)} %collective-permute-done.1.other_edge_ref, f32[8,8,128]{2,1,0:T(8,128)S(1)} %copy-done.1), custom_call_target="tpu_custom_call" | custom-call | bytes 262144 | tf_op jit(solution)/shard_map/pallas_call | solution.py:49
  21.5 0.1 collective-permute-start.2
  21.5 1.3 %collective-permute-done.2.refs_1_ = f32[34,8,128]{2,1,0:T(8,128)S(1)} collective-permute-done((f32[34,8,128]{2,1,0:T(8,128)S(1)}, f32[34,8,128]{2,1,0:T(8,128)S(1)}, u32[]{:S(2)}, u32[]{:S(2)}) %collective-permute-start.2) | collective-permute-done | bytes 139296 | tf_op jit(solution)/shard_map/ppermute | solution.py:651
  22.9 1.3 %shard_map.125 = (f32[16,16,128]{2,1,0:T(8,128)}, f32[6,16,16,128]{3,2,1,0:T(8,128)S(1)}, f32[16,16,128]{2,1,0:T(8,128)S(1)}, f32[16,16,128]{2,1,0:T(8,128)S(1)}) custom-call(f32[34,8,128]{2,1,0:T(8,128)S(1)} %get-tuple-element.51.window_ref.refs_0_, f32[34,8,128]{2,1,0:T(8,128)S(1)} %collective-permute-done.2.refs_1_), custom_call_target="tpu_custom_call" | custom-call | bytes 262144 | tf_op jit(solution)/shard_map/pallas_call | solution.py:49
  24.1 0.0 copy-start
  24.1 4.3 %all-to-all-start.1 = ((f32[16,16,128]{2,1,0:T(8,128)}), f32[16,16,128]{2,1,0:T(8,128)S(1)}, u32[]{:S(2)}, u32[]{:S(2)}) async-start(f32[16,16,128]{2,1,0:T(8,128)} %get-tuple-element.53), calls=%async_computation.1 | async-start | bytes 262144 | tf_op jit(solution)/shard_map/all_to_all | solution.py:726
  28.5 3.3 %shard_map.126 = (s32[2,3]{1,0:T(2,128)S(1)}, f32[3,3,128]{2,1,0:T(4,128)S(1)}, f32[3,128]{1,0:T(4,128)S(1)}) custom-call(s32[8,6]{1,0:T(8,128)S(1)} %copy-done.7, s32[8]{0:T(128)S(1)} %copy-done.5, s32[8]{0:T(128)S(1)} %copy-done.4, f32[3,8,128]{2,1,0:T(8,128)S(1)} %copy-done.6, f32[8,128]{1,0:T(8,128)S(1)} %copy-done.3, f32[3,8,128]{2,1,0:T(8,128)S(1)} %copy-done.2), custom_call_target="tpu_custom_call" | custom-call | flops 9175040 | bytes 262144 | tf_op jit(solution)/shard_map/pallas_call | solution.py:49
  31.7 4.5 %all-to-all-done.1.refs_0_ = f32[16,16,128]{2,1,0:T(8,128)S(1)} async-done(((f32[16,16,128]{2,1,0:T(8,128)}), f32[16,16,128]{2,1,0:T(8,128)S(1)}, u32[]{:S(2)}, u32[]{:S(2)}) %all-to-all-start.1) | async-done | bytes 131104 | tf_op jit(solution)/shard_map/all_to_all | solution.py:726
  36.3 0.0 collective-permute-start.3
  36.3 0.0 copy-done
  36.3 1.2 %shard_map.124 = (f32[3,16,128]{2,1,0:T(8,128)S(1)}, f32[3,8,8,128]{3,2,1,0:T(8,128)S(1)}) custom-call(f32[34,8,128]{2,1,0:T(8,128)S(1)} %get-tuple-element.51.window_ref.refs_0_, f32[5,16,128]{2,1,0:T(8,128)S(1)} %get-tuple-element.50.rows_ref, f32[3,8,8,128]{3,2,1,0:T(8,128)S(1)} %copy-done), custom_call_target="tpu_custom_call" | custom-call | flops 10000000 | bytes 262144 | tf_op jit(solution)/shard_map/pallas_call | solution.py:49
  37.5 0.1 collective-permute-done.3.refs_1_
  37.6 2.0 %shard_map.127 = (f32[8,8,128]{2,1,0:T(8,128)S(1)}, f32[3,8,8,128]{3,2,1,0:T(8,128)S(1)}) custom-call(f32[16,16,128]{2,1,0:T(8,128)S(1)} %all-to-all-done.1.refs_0_, f32[16,16,128]{2,1,0:T(8,128)S(1)} %collective-permute-done.3.refs_1_, f32[6,16,16,128]{3,2,1,0:T(8,128)S(1)} %get-tuple-element.58.refs_2_, f32[16,16,128]{2,1,0:T(8,128)S(1)} %get-tuple-element.59.refs_3_, ...), custom_call_target="tpu_custom_call" | custom-call | bytes 262144 | tf_op jit(solution)/shard_map/pallas_call | solution.py:49
  39.6 1.1 %shard_map.128 = f32[16,1,1152]{2,1,0:T(1,128)} custom-call(f32[5,16,128]{2,1,0:T(8,128)S(1)} %get-tuple-element.50.rows_ref, f32[3,16,128]{2,1,0:T(8,128)S(1)} %get-tuple-element.52.drag_ref, f32[3,8,8,128]{3,2,1,0:T(8,128)S(1)} %get-tuple-element.61.slope_ref), custom_call_target="tpu_custom_call" | custom-call | bytes 262144 | tf_op jit(solution)/shard_map/pallas_call | solution.py:49
  40.7 3.5 %all-to-all-start.2 = ((f32[16,1,1152]{2,1,0:T(1,128)}), f32[16,1,1152]{2,1,0:T(1,128)S(1)}, u32[]{:S(2)}, u32[]{:S(2)}) async-start(f32[16,1,1152]{2,1,0:T(1,128)} %shard_map.128), calls=%async_computation.2 | async-start | bytes 147456 | tf_op jit(solution)/shard_map/all_to_all | solution.py:764
  44.3 3.3 %shard_map.130 = (s32[2,3]{1,0:T(2,128)S(1)}, f32[3,3,128]{2,1,0:T(4,128)S(1)}, f32[3,128]{1,0:T(4,128)S(1)}) custom-call(s32[8,6]{1,0:T(8,128)S(1)} %copy-done.7, s32[8]{0:T(128)S(1)} %copy-done.5, s32[8]{0:T(128)S(1)} %copy-done.4, f32[3,8,128]{2,1,0:T(8,128)S(1)} %copy-done.6, f32[8,128]{1,0:T(8,128)S(1)} %copy-done.3, f32[3,8,128]{2,1,0:T(8,128)S(1)} %copy-done.2), custom_call_target="tpu_custom_call" | custom-call | flops 9175040 | bytes 262144 | tf_op jit(solution)/shard_map/pallas_call | solution.py:49
  47.5 0.7 %shard_map.129 = (f32[8,8,128]{2,1,0:T(8,128)}, f32[3,8,8,128]{3,2,1,0:T(8,128)}) custom-call(f32[3,8,8,128]{3,2,1,0:T(8,128)S(1)} %get-tuple-element.62.base_ref, f32[8,8,128]{2,1,0:T(8,128)S(1)} %get-tuple-element.63.pressure_ref, f32[3,8,8,128]{3,2,1,0:T(8,128)S(1)} %get-tuple-element.61.slope_ref), custom_call_target="tpu_custom_call" | custom-call | flops 5000000 | bytes 262144 | tf_op jit(solution)/shard_map/pallas_call | solution.py:49
  48.2 3.6 %all-to-all-done.2.refs_9_ = f32[16,1,1152]{2,1,0:T(1,128)S(1)} async-done(((f32[16,1,1152]{2,1,0:T(1,128)}), f32[16,1,1152]{2,1,0:T(1,128)S(1)}, u32[]{:S(2)}, u32[]{:S(2)}) %all-to-all-start.2) | async-done | bytes 73760 | tf_op jit(solution)/shard_map/all_to_all | solution.py:764
  51.8 1.2 %shard_map.131 = f32[3,8,128]{2,1,0:T(8,128)} custom-call(s32[2,2]{1,0:T(2,128)S(1)} %get-tuple-element.71.refs_0_, f32[3,2,128]{2,1,0:T(2,128)S(1)} %get-tuple-element.72.refs_1_, f32[2,128]{1,0:T(2,128)S(1)} %get-tuple-element.73.refs_2_, s32[2,3]{1,0:T(2,128)S(1)} %get-tuple-element.74.refs_3_, f32[3,3,128]{2,1,0:T(4,128)S(1)} %get-tuple-element.75.refs_4_, ...), custom_call_target="tpu_custom_call" | custom-call | bytes 262144 | tf_op jit(solution)/shard_map/pallas_call | solution.py:49
Async XLA Ops:
  2.4 8.6 %copy-start.9 = (f32[4,8,128]{2,1,0:T(8,128)S(1)}, f32[4,8,128]{2,1,0:T(8,128)}, u32[]{:S(2)}) copy-start(f32[4,8,128]{2,1,0:T(8,128)} %get-tuple-element.47) | copy-start | bytes 49156
  2.4 10.6 %copy-start.8 = (f32[4,8,128]{2,1,0:T(8,128)S(1)}, f32[4,8,128]{2,1,0:T(8,128)}, u32[]{:S(2)}) copy-start(f32[4,8,128]{2,1,0:T(8,128)} %get-tuple-element.48) | copy-start | bytes 49156
  2.4 11.2 %copy-start.2 = (f32[3,8,128]{2,1,0:T(8,128)S(1)}, f32[3,8,128]{2,1,0:T(8,128)}, u32[]{:S(2)}) copy-start(f32[3,8,128]{2,1,0:T(8,128)} %vel_ref.7) | copy-start | bytes 36868
  2.4 11.2 %copy-start.3 = (f32[8,128]{1,0:T(8,128)S(1)}, f32[8,128]{1,0:T(8,128)}, u32[]{:S(2)}) copy-start(f32[8,128]{1,0:T(8,128)} %radius_ref.7) | copy-start | bytes 12292
  2.4 11.2 %copy-start.4 = (s32[8]{0:T(128)S(1)}, s32[8]{0:T(128)}, u32[]{:S(2)}) copy-start(s32[8]{0:T(128)} %offset_ref.7) | copy-start | bytes 100
  2.4 11.2 %copy-start.5 = (s32[8]{0:T(128)S(1)}, s32[8]{0:T(128)}, u32[]{:S(2)}) copy-start(s32[8]{0:T(128)} %count_ref.7) | copy-start | bytes 100
  2.4 11.2 %copy-start.6 = (f32[3,8,128]{2,1,0:T(8,128)S(1)}, f32[3,8,128]{2,1,0:T(8,128)}, u32[]{:S(2)}) copy-start(f32[3,8,128]{2,1,0:T(8,128)} %pos_ref.5) | copy-start | bytes 36868
  2.4 11.2 %copy-start.7 = (s32[8,6]{1,0:T(8,128)S(1)}, s32[8,6]{1,0:T(8,128)}, u32[]{:S(2)}) copy-start(s32[8,6]{1,0:T(8,128)} %near_ref.5) | copy-start | bytes 580
  2.4 18.3 %all-to-all-start = ((f32[16,32,128]{2,1,0:T(8,128)}), f32[16,32,128]{2,1,0:T(8,128)S(1)}, u32[]{:S(2)}, u32[]{:S(2)}) async-start(f32[16,32,128]{2,1,0:T(8,128)} %get-tuple-element.42), calls=%async_computation | async-start | bytes 524288 | tf_op jit(solution)/shard_map/all_to_all | solution.py:689
  10.9 9.9 %copy-start.1 = (f32[8,8,128]{2,1,0:T(8,128)S(1)}, f32[8,8,128]{2,1,0:T(8,128)}, u32[]{:S(2)}) copy-start(f32[8,8,128]{2,1,0:T(8,128)} %get-tuple-element.49.s_ref) | copy-start | bytes 98308
  10.9 9.8 %collective-permute-start = (f32[4,8,128]{2,1,0:T(8,128)S(1)}, f32[4,8,128]{2,1,0:T(8,128)S(1)}, u32[]{:S(2)}, u32[]{:S(2)}) collective-permute-start(f32[4,8,128]{2,1,0:T(8,128)S(1)} %copy-done.9), channel_id=1, source_target_pairs={{0,2},{4,6},{8,10},{12,14},{16,18},{20,22},{24,26},{28,30},{2,0},{... | collective-permute-start | bytes 49160 | tf_op jit(solution)/shard_map/ppermute | solution.py:690
  12.9 7.9 %collective-permute-start.1 = (f32[4,8,128]{2,1,0:T(8,128)S(1)}, f32[4,8,128]{2,1,0:T(8,128)S(1)}, u32[]{:S(2)}, u32[]{:S(2)}) collective-permute-start(f32[4,8,128]{2,1,0:T(8,128)S(1)} %copy-done.8), channel_id=1, source_target_pairs={{2,4},{6,8},{10,12},{14,16},{18,20},{22,24},{26,28},{4,2},{8,6},{1... | collective-permute-start | bytes 49160 | tf_op jit(solution)/shard_map/ppermute | solution.py:690
  21.5 1.4 %collective-permute-start.2 = (f32[34,8,128]{2,1,0:T(8,128)S(1)}, f32[34,8,128]{2,1,0:T(8,128)S(1)}, u32[]{:S(2)}, u32[]{:S(2)}) collective-permute-start(f32[34,8,128]{2,1,0:T(8,128)S(1)} %get-tuple-element.51.window_ref.refs_0_), channel_id=1, source_target_pairs={{0,1},{1,0},{2,3},{3,2},{4,5},{5,4},{6,7},{7,6},{8,9},{9,8},{10,11... | collective-permute-start | bytes 417800 | tf_op jit(solution)/shard_map/ppermute | solution.py:651
  24.1 12.1 %copy-start = (f32[3,8,8,128]{3,2,1,0:T(8,128)S(1)}, f32[3,8,8,128]{3,2,1,0:T(8,128)}, u32[]{:S(2)}) copy-start(f32[3,8,8,128]{3,2,1,0:T(8,128)} %gas_ref.1) | copy-start | bytes 294916
  24.1 12.1 %all-to-all-start.1 = ((f32[16,16,128]{2,1,0:T(8,128)}), f32[16,16,128]{2,1,0:T(8,128)S(1)}, u32[]{:S(2)}, u32[]{:S(2)}) async-start(f32[16,16,128]{2,1,0:T(8,128)} %get-tuple-element.53), calls=%async_computation.1 | async-start | bytes 262144 | tf_op jit(solution)/shard_map/all_to_all | solution.py:726
  36.3 1.3 %collective-permute-start.3 = (f32[16,16,128]{2,1,0:T(8,128)S(1)}, f32[16,16,128]{2,1,0:T(8,128)S(1)}, u32[]{:S(2)}, u32[]{:S(2)}) collective-permute-start(f32[16,16,128]{2,1,0:T(8,128)S(1)} %all-to-all-done.1.refs_0_), channel_id=1, source_target_pairs={{0,1},{1,0},{2,3},{3,2},{4,5},{5,4},{6,7},{7,6},{8,9},{9,8},{10,11... | collective-permute-start | bytes 393224 | tf_op jit(solution)/shard_map/ppermute | solution.py:651
  40.7 11.1 %all-to-all-start.2 = ((f32[16,1,1152]{2,1,0:T(1,128)}), f32[16,1,1152]{2,1,0:T(1,128)S(1)}, u32[]{:S(2)}, u32[]{:S(2)}) async-start(f32[16,1,1152]{2,1,0:T(1,128)} %shard_map.128), calls=%async_computation.2 | async-start | bytes 147456 | tf_op jit(solution)/shard_map/all_to_all | solution.py:764
